TPU v7x, 128 devices: a whole 4x4x4 slice. The times are simulated.
128 devices in a mesh: ctx: 16 (over y_hi, z, core), kv: 8 (over x, y_lo).
Axes of the slice: x: 4, y: 4 (y_hi: 2, y_lo: 2; y = y_hi * 2 + y_lo), z: 4, core: 2. Of those that a mesh axis runs over, the one named last changes fastest.
Arguments:
- queries: bfloat16 [2, 512, 128, 128], P(None, 'ctx', 'kv'), may hold values from -6 to 6
- new_keys: bfloat16 [2, 512, 8, 128], P(None, 'ctx', 'kv'), may hold values from -6 to 6
- new_values: bfloat16 [2, 512, 8, 128], P(None, 'ctx', 'kv'), may hold values from -6 to 6
- cache_keys: bfloat16 [2, 32768, 8, 128], P(None, 'ctx', 'kv'), may hold values from -6 to 6
- cache_values: bfloat16 [2, 32768, 8, 128], P(None, 'ctx', 'kv'), may hold values from -6 to 6
- cached_len: int32 [2], replicated, may hold values from 4096 to 32768, as said below
- span_order: int32 [2, 32], replicated, may hold values from 0 to 31, as said below
Outputs:
- attention: bfloat16 [2, 512, 128, 128], P(None, ('ctx', 'kv'))
- log_norm: float32 [2, 512, 128], P(None, ('ctx', 'kv'))
Inputs may be any that keep to these rules, and one draw needn't show every extreme that they name: `cached_len`: one request holds all 32768 slots. `span_order`: each row is a permutation in which block slots 2 q and 2 q + 1 hold blocks c and 31 - c for some c.
All inputs are finite; a program needn't handle non-finite values.
Results may differ from a plain program's by a relative error of at most 0.0058.
Values may be sent and summed in bfloat16 or wider, within the bound.
No kernel may reach another device: no remote copies, remote signals or barrier semaphores. Data moves between devices by JAX's collectives and lax.ppermute only.
A program may use at most 64 MiB of HBM per device.

v0:
```python
import jax
import jax.numpy as jnp
from jax import lax
from jax.sharding import PartitionSpec as P

masked_score = -1e30


def passed_along(value, axis, steps):
    count = lax.axis_size(axis)
    pairs = [(source, (source + steps) % count) for source in range(count)]
    return lax.ppermute(value, axis, pairs)


def combine_parts(partials, log_parts):
    highest = jnp.max(log_parts, 0)
    log_total = highest + jnp.log(jnp.sum(jnp.exp(log_parts - highest), 0))
    shares = jnp.exp(log_parts - log_total)
    return (jnp.sum(shares[..., None] * partials.astype(jnp.float32), 0), log_total)


def on_device(queries, new_keys, new_values, cache_keys, cache_values, cached_len, span_order):
    cycle_size = lax.axis_size("ctx")
    my_index = lax.axis_index("ctx")
    requests, new_rows, local_heads, head_dim = queries.shape
    cache_rows = cache_keys.shape[1]
    kv_local = cache_keys.shape[2]
    group_size = local_heads // kv_local
    span_rows = new_rows // 2
    key_rows = jnp.concatenate([cache_keys, new_keys], 1)
    value_rows = jnp.concatenate([cache_values, new_values], 1)
    cache_valid = (my_index * cache_rows + jnp.arange(cache_rows, dtype=jnp.int32))[
        None, :
    ] < cached_len[:, None]

    def slot_positions(source):
        chosen = lax.dynamic_slice_in_dim(span_order, 2 * source, 2, 1)
        spread = (
            chosen[:, :, None] * span_rows + jnp.arange(span_rows, dtype=jnp.int32)[None, None, :]
        )
        return spread.reshape(requests, new_rows)

    key_positions = slot_positions(my_index)

    def shard_partial(visiting, source):
        query_positions = slot_positions(source)
        visible = jnp.concatenate(
            [
                jnp.broadcast_to(cache_valid[:, None, :], (requests, new_rows, cache_rows)),
                key_positions[:, None, :] <= query_positions[:, :, None],
            ],
            2,
        )
        grouped = visiting.reshape(requests, new_rows, kv_local, group_size, head_dim)
        scores = jnp.einsum(
            "rtkgd,rskd->rkgts", grouped, key_rows, preferred_element_type=jnp.float32
        ) * head_dim ** (-0.5)
        scores = jnp.where(visible[:, None, None], scores, masked_score)
        highest = jnp.max(scores, -1, keepdims=True)
        exponent = jnp.exp(scores - highest)
        totals = jnp.sum(exponent, -1, keepdims=True)
        log_total = (highest + jnp.log(totals))[..., 0]
        weights = (exponent / totals).astype(jnp.bfloat16)
        outputs = jnp.einsum(
            "rkgts,rskd->rtkgd", weights, value_rows, preferred_element_type=jnp.float32
        )
        outputs = outputs.reshape(requests, new_rows, local_heads, head_dim).astype(jnp.bfloat16)
        log_total = jnp.transpose(log_total, (0, 3, 1, 2)).reshape(requests, new_rows, local_heads)
        return (outputs, log_total)

    def store_partial(buffers, visiting, source):
        outputs, log_total = shard_partial(visiting, source)
        return (
            lax.dynamic_update_index_in_dim(buffers[0], outputs, source, 0),
            lax.dynamic_update_index_in_dim(buffers[1], log_total, source, 0),
        )

    buffers = (
        jnp.zeros((cycle_size, requests, new_rows, local_heads, head_dim), jnp.bfloat16),
        jnp.zeros((cycle_size, requests, new_rows, local_heads), jnp.float32),
    )
    buffers = store_partial(buffers, queries, my_index)

    def cycle_step(step_index, loop_state):
        visiting, stored = loop_state
        visiting = passed_along(visiting, "ctx", 1)
        source = jnp.mod(my_index - step_index, cycle_size)
        return (visiting, store_partial(stored, visiting, source))

    _, buffers = lax.fori_loop(1, cycle_size, cycle_step, (queries, buffers))
    partials, log_parts = (
        lax.all_to_all(
            lax.all_to_all(
                buffers[0].astype(jnp.float32), "ctx", split_axis=0, concat_axis=0, tiled=True
            ),
            "kv",
            split_axis=2,
            concat_axis=3,
            tiled=True,
        ).astype(jnp.bfloat16),
        lax.all_to_all(
            lax.all_to_all(buffers[1], "ctx", split_axis=0, concat_axis=0, tiled=True),
            "kv",
            split_axis=2,
            concat_axis=3,
            tiled=True,
        ),
    )
    outputs, log_norm = combine_parts(partials, log_parts)
    return (outputs.astype(jnp.bfloat16), log_norm)


def solution(mesh):
    placed = (
        P(None, "ctx", "kv", None),
        P(None, "ctx", "kv", None),
        P(None, "ctx", "kv", None),
        P(None, "ctx", "kv", None),
        P(None, "ctx", "kv", None),
        P(),
        P(),
    )
    return jax.shard_map(
        on_device,
        mesh=mesh,
        in_specs=placed,
        out_specs=(P(None, ("ctx", "kv"), None, None), P(None, ("ctx", "kv"), None)),
        check_vma=False,
    )
```

profile of v0, /device:TPU:0, one launch (start us, length us, event | category | flops | bytes accessed | tf_op | source)
XLA Modules:
  0.0 410.3 jit_solution(1768998340070853773)
XLA Ops:
  1.7 1.7 copy.56
  4.3 3.0 fusion.35
  7.3 3.4 copy-done.1
  14.5 5.2 %fusion.28 = bf16[16,2,32,16,128]{4,2,3,1,0:T(8,128)(2,1)S(1)} fusion(bf16[16,2,32,16,128]{4,2,3,1,0:T(8,128)(2,1)S(1)} %broadcast_in_dim.115, s32[]{:T(128)S(6)} %select_n.67, f32[2,16,32]{2,1,0:T(8,128)S(1)} %fusion.19, f32[2,1,16,32,2080]{4,3,2,0,1:T(8,128)} %copy-done.1, f32[2,16,32]{2,1,0:T(8,128)S(1)} %get-tuple-element.355, ...), kind=kOutput, calls=%fused_computation.31 | convolution fusion | flops 553910272 | bytes 9879556 | tf_op jit(solution)/shard_map/rkgts,rskd->rtkgd/dot_general | solution.py:64
  19.8 1.9 copy-done
  21.7 227.3 %while.20 = (s32[]{:T(128)}, bf16[2,32,16,128]{3,1,2,0:T(8,128)(2,1)S(1)}, bf16[16,2,32,16,128]{4,2,3,1,0:T(8,128)(2,1)}, f32[16,2,32,16]{2,3,1,0:T(8,128)S(1)},...) while((s32[]{:T(128)}, ...), condition=%wide.region_5.6_spmd.clone, body=%wide.region_2.5_spmd.clone.sunk | while | flops 1107827840 | bytes 30408160 | solution.py:90
  22.5 9.5 %collective-permute-done = bf16[2,32,16,128]{3,1,2,0:T(8,128)(2,1)S(1)} collective-permute-done((bf16[2,32,16,128]{3,1,2,0:T(8,128)(2,1)S(1)}, bf16[2,32,16,128]{3,1,2,0:T(8,128)(2,1)S(1)}, u32[]{:S(2)}, u32[]{:S(2)}) %collective-permute-start) | collective-permute-done | bytes 262176 | tf_op jit(solution)/shard_map/while/body/eval_jaxpr/ppermute | solution.py:12
  32.0 1.6 fusion.46
  35.0 2.6 fusion.48
  38.5 8.6 %collective-permute-done = bf16[2,32,16,128]{3,1,2,0:T(8,128)(2,1)S(1)} collective-permute-done((bf16[2,32,16,128]{3,1,2,0:T(8,128)(2,1)S(1)}, bf16[2,32,16,128]{3,1,2,0:T(8,128)(2,1)S(1)}, u32[]{:S(2)}, u32[]{:S(2)}) %collective-permute-start) | collective-permute-done | bytes 262176 | tf_op jit(solution)/shard_map/while/body/eval_jaxpr/ppermute | solution.py:12
  50.1 2.6 fusion.48
  53.5 8.6 %collective-permute-done = bf16[2,32,16,128]{3,1,2,0:T(8,128)(2,1)S(1)} collective-permute-done((bf16[2,32,16,128]{3,1,2,0:T(8,128)(2,1)S(1)}, bf16[2,32,16,128]{3,1,2,0:T(8,128)(2,1)S(1)}, u32[]{:S(2)}, u32[]{:S(2)}) %collective-permute-start) | collective-permute-done | bytes 262176 | tf_op jit(solution)/shard_map/while/body/eval_jaxpr/ppermute | solution.py:12
  65.2 2.6 fusion.48
  68.6 8.6 %collective-permute-done = bf16[2,32,16,128]{3,1,2,0:T(8,128)(2,1)S(1)} collective-permute-done((bf16[2,32,16,128]{3,1,2,0:T(8,128)(2,1)S(1)}, bf16[2,32,16,128]{3,1,2,0:T(8,128)(2,1)S(1)}, u32[]{:S(2)}, u32[]{:S(2)}) %collective-permute-start) | collective-permute-done | bytes 262176 | tf_op jit(solution)/shard_map/while/body/eval_jaxpr/ppermute | solution.py:12
  80.3 2.6 fusion.48
  83.7 8.6 %collective-permute-done = bf16[2,32,16,128]{3,1,2,0:T(8,128)(2,1)S(1)} collective-permute-done((bf16[2,32,16,128]{3,1,2,0:T(8,128)(2,1)S(1)}, bf16[2,32,16,128]{3,1,2,0:T(8,128)(2,1)S(1)}, u32[]{:S(2)}, u32[]{:S(2)}) %collective-permute-start) | collective-permute-done | bytes 262176 | tf_op jit(solution)/shard_map/while/body/eval_jaxpr/ppermute | solution.py:12
  95.4 2.6 fusion.48
  98.8 8.6 %collective-permute-done = bf16[2,32,16,128]{3,1,2,0:T(8,128)(2,1)S(1)} collective-permute-done((bf16[2,32,16,128]{3,1,2,0:T(8,128)(2,1)S(1)}, bf16[2,32,16,128]{3,1,2,0:T(8,128)(2,1)S(1)}, u32[]{:S(2)}, u32[]{:S(2)}) %collective-permute-start) | collective-permute-done | bytes 262176 | tf_op jit(solution)/shard_map/while/body/eval_jaxpr/ppermute | solution.py:12
  110.5 2.6 fusion.48
  113.9 8.6 %collective-permute-done = bf16[2,32,16,128]{3,1,2,0:T(8,128)(2,1)S(1)} collective-permute-done((bf16[2,32,16,128]{3,1,2,0:T(8,128)(2,1)S(1)}, bf16[2,32,16,128]{3,1,2,0:T(8,128)(2,1)S(1)}, u32[]{:S(2)}, u32[]{:S(2)}) %collective-permute-start) | collective-permute-done | bytes 262176 | tf_op jit(solution)/shard_map/while/body/eval_jaxpr/ppermute | solution.py:12
  125.6 2.6 fusion.48
  129.0 8.6 %collective-permute-done = bf16[2,32,16,128]{3,1,2,0:T(8,128)(2,1)S(1)} collective-permute-done((bf16[2,32,16,128]{3,1,2,0:T(8,128)(2,1)S(1)}, bf16[2,32,16,128]{3,1,2,0:T(8,128)(2,1)S(1)}, u32[]{:S(2)}, u32[]{:S(2)}) %collective-permute-start) | collective-permute-done | bytes 262176 | tf_op jit(solution)/shard_map/while/body/eval_jaxpr/ppermute | solution.py:12
  140.7 2.6 fusion.48
  144.1 8.6 %collective-permute-done = bf16[2,32,16,128]{3,1,2,0:T(8,128)(2,1)S(1)} collective-permute-done((bf16[2,32,16,128]{3,1,2,0:T(8,128)(2,1)S(1)}, bf16[2,32,16,128]{3,1,2,0:T(8,128)(2,1)S(1)}, u32[]{:S(2)}, u32[]{:S(2)}) %collective-permute-start) | collective-permute-done | bytes 262176 | tf_op jit(solution)/shard_map/while/body/eval_jaxpr/ppermute | solution.py:12
  155.7 2.6 fusion.48
  159.2 8.6 %collective-permute-done = bf16[2,32,16,128]{3,1,2,0:T(8,128)(2,1)S(1)} collective-permute-done((bf16[2,32,16,128]{3,1,2,0:T(8,128)(2,1)S(1)}, bf16[2,32,16,128]{3,1,2,0:T(8,128)(2,1)S(1)}, u32[]{:S(2)}, u32[]{:S(2)}) %collective-permute-start) | collective-permute-done | bytes 262176 | tf_op jit(solution)/shard_map/while/body/eval_jaxpr/ppermute | solution.py:12
  170.8 2.6 fusion.48
  174.3 8.6 %collective-permute-done = bf16[2,32,16,128]{3,1,2,0:T(8,128)(2,1)S(1)} collective-permute-done((bf16[2,32,16,128]{3,1,2,0:T(8,128)(2,1)S(1)}, bf16[2,32,16,128]{3,1,2,0:T(8,128)(2,1)S(1)}, u32[]{:S(2)}, u32[]{:S(2)}) %collective-permute-start) | collective-permute-done | bytes 262176 | tf_op jit(solution)/shard_map/while/body/eval_jaxpr/ppermute | solution.py:12
  185.9 2.6 fusion.48
  189.4 8.6 %collective-permute-done = bf16[2,32,16,128]{3,1,2,0:T(8,128)(2,1)S(1)} collective-permute-done((bf16[2,32,16,128]{3,1,2,0:T(8,128)(2,1)S(1)}, bf16[2,32,16,128]{3,1,2,0:T(8,128)(2,1)S(1)}, u32[]{:S(2)}, u32[]{:S(2)}) %collective-permute-start) | collective-permute-done | bytes 262176 | tf_op jit(solution)/shard_map/while/body/eval_jaxpr/ppermute | solution.py:12
  201.0 2.6 fusion.48
  204.5 8.6 %collective-permute-done = bf16[2,32,16,128]{3,1,2,0:T(8,128)(2,1)S(1)} collective-permute-done((bf16[2,32,16,128]{3,1,2,0:T(8,128)(2,1)S(1)}, bf16[2,32,16,128]{3,1,2,0:T(8,128)(2,1)S(1)}, u32[]{:S(2)}, u32[]{:S(2)}) %collective-permute-start) | collective-permute-done | bytes 262176 | tf_op jit(solution)/shard_map/while/body/eval_jaxpr/ppermute | solution.py:12
  216.1 2.6 fusion.48
  219.6 8.6 %collective-permute-done = bf16[2,32,16,128]{3,1,2,0:T(8,128)(2,1)S(1)} collective-permute-done((bf16[2,32,16,128]{3,1,2,0:T(8,128)(2,1)S(1)}, bf16[2,32,16,128]{3,1,2,0:T(8,128)(2,1)S(1)}, u32[]{:S(2)}, u32[]{:S(2)}) %collective-permute-start) | collective-permute-done | bytes 262176 | tf_op jit(solution)/shard_map/while/body/eval_jaxpr/ppermute | solution.py:12
  231.2 2.6 fusion.48
  234.7 8.6 %collective-permute-done = bf16[2,32,16,128]{3,1,2,0:T(8,128)(2,1)S(1)} collective-permute-done((bf16[2,32,16,128]{3,1,2,0:T(8,128)(2,1)S(1)}, bf16[2,32,16,128]{3,1,2,0:T(8,128)(2,1)S(1)}, u32[]{:S(2)}, u32[]{:S(2)}) %collective-permute-start) | collective-permute-done | bytes 262176 | tf_op jit(solution)/shard_map/while/body/eval_jaxpr/ppermute | solution.py:12
  246.3 2.6 fusion.48
  249.8 3.8 all-to-all-start
  253.6 5.9 %copy.73 = bf16[16,2,32,16,128]{4,3,1,2,0:T(8,128)(2,1)} copy(bf16[16,2,32,16,128]{4,2,3,1,0:T(8,128)(2,1)} %get-tuple-element.247) | data formatting | bytes 8388608 | tf_op jit(solution)/shard_map/while | solution.py:90
  259.5 1.7 all-to-all-done
  261.3 5.5 %all-to-all-start.2 = ((bf16[16,2,32,16,128]{4,3,1,2,0:T(8,128)(2,1)}), bf16[16,2,32,16,128]{4,3,1,2,0:T(8,128)(2,1)}, u32[]{:S(2)}, u32[]{:S(2)}) async-start(bf16[16,2,32,16,128]{4,3,1,2,0:T(8,128)(2,1)} %copy.73), calls=%async_computation.2 | async-start | bytes 8388608 | tf_op jit(solution)/shard_map/all_to_all | solution.py:93
  269.6 52.7 %all-to-all-done.2 = bf16[16,2,32,16,128]{4,3,1,2,0:T(8,128)(2,1)} async-done(((bf16[16,2,32,16,128]{4,3,1,2,0:T(8,128)(2,1)}), bf16[16,2,32,16,128]{4,3,1,2,0:T(8,128)(2,1)}, u32[]{:S(2)}, u32[]{:S(2)}) %all-to-all-start.2) | async-done | bytes 4194336 | tf_op jit(solution)/shard_map/all_to_all | solution.py:93
  322.3 4.3 %all-to-all-start.1 = ((f32[8,1,2048]{2,1,0:T(1,128)}), f32[8,1,2048]{2,1,0:T(1,128)S(1)}, u32[]{:S(2)}, u32[]{:S(2)}) async-start(f32[8,1,2048]{2,1,0:T(1,128)} %reshape.312), calls=%async_computation.1 | async-start | bytes 131072 | tf_op jit(solution)/shard_map/all_to_all | solution.py:101
  326.6 5.4 %copy.61 = bf16[16,2,32,16,128]{4,3,1,0,2:T(8,128)(2,1)} copy(bf16[16,2,32,16,128]{4,3,1,2,0:T(8,128)(2,1)} %all-to-all-done.2) | data formatting | bytes 8388608 | tf_op jit(solution)/shard_map/all_to_all | solution.py:93
  332.9 4.9 %all-to-all-start.3 = ((bf16[16,2,32,16,128]{4,3,1,0,2:T(8,128)(2,1)}), bf16[16,2,32,16,128]{4,3,1,0,2:T(8,128)(2,1)}, u32[]{:S(2)}, u32[]{:S(2)}) async-start(bf16[16,2,32,16,128]{4,3,1,0,2:T(8,128)(2,1)} %copy.61), calls=%async_computation.3 | async-start | bytes 8388608 | tf_op jit(solution)/shard_map/all_to_all | solution.py:92
  341.5 55.4 %all-to-all-done.3 = bf16[16,2,32,16,128]{4,3,1,0,2:T(8,128)(2,1)} async-done(((bf16[16,2,32,16,128]{4,3,1,0,2:T(8,128)(2,1)}), bf16[16,2,32,16,128]{4,3,1,0,2:T(8,128)(2,1)}, u32[]{:S(2)}, u32[]{:S(2)}) %all-to-all-start.3) | async-done | bytes 4194336 | tf_op jit(solution)/shard_map/all_to_all | solution.py:92
  396.9 3.3 bitcast_convert_fusion
  400.2 9.3 %fusion.18 = bf16[2,4,8,16,128]{4,1,2,3,0:T(4,128)(2,1)S(1)} fusion(f32[16,2,8,4,16,128]{5,4,1,0,3,2:T(8,128)S(1)} %bitcast_convert_fusion, f32[16,2,4,8,16]{2,3,4,1,0:T(8,128)S(1)} %copy.59), kind=kLoop, calls=%fused_computation.24 | loop fusion | flops 4063232 | bytes 8716288 | tf_op jit(solution)/shard_map/reduce_sum | solution.py:19
  (304 shorter events, 69.2 us)
Async XLA Ops:
  7.3 3.4 copy-start.1
  10.7 1.3 copy-start.2
  10.7 1.3 copy-start.7
  10.7 1.3 copy-start.8
  12.0 2.5 copy-start.3
  14.5 7.2 %copy-start.4 = (bf16[2,32,16,128]{3,1,2,0:T(8,128)(2,1)S(1)}, bf16[2,32,16,128]{3,1,2,0:T(8,128)(2,1)}, u32[]{:S(2)}) copy-start(bf16[2,32,16,128]{3,1,2,0:T(8,128)(2,1)} %copy.56) | copy-start | bytes 786436
  14.5 7.2 %copy-start.5 = (s32[2,32]{1,0:T(2,128)S(1)}, s32[2,32]{1,0:T(2,128)}, u32[]{:S(2)}) copy-start(s32[2,32]{1,0:T(2,128)} %param.15) | copy-start | bytes 772
  14.5 7.1 %copy-start.6 = (s32[2]{0:T(128)S(1)}, s32[2]{0:T(128)}, u32[]{:S(2)}) copy-start(s32[2]{0:T(128)} %param.14) | copy-start | bytes 28
  19.7 1.9 copy-start
  21.7 10.3 %collective-permute-start = (bf16[2,32,16,128]{3,1,2,0:T(8,128)(2,1)S(1)}, bf16[2,32,16,128]{3,1,2,0:T(8,128)(2,1)S(1)}, u32[]{:S(2)}, u32[]{:S(2)}) collective-permute-start(bf16[2,32,16,128]{3,1,2,0:T(8,128)(2,1)S(1)} %get-tuple-element.448), channel_id=1, source_target_pairs={{0,8},{8,16},{16,24},{24,32},{32,40},{40,48},{48,56},{56,64},{64,7... | collective-permute-start | bytes 786440 | tf_op jit(solution)/shard_map/while/body/eval_jaxpr/ppermute | solution.py:12
  37.6 9.5 %collective-permute-start = (bf16[2,32,16,128]{3,1,2,0:T(8,128)(2,1)S(1)}, bf16[2,32,16,128]{3,1,2,0:T(8,128)(2,1)S(1)}, u32[]{:S(2)}, u32[]{:S(2)}) collective-permute-start(bf16[2,32,16,128]{3,1,2,0:T(8,128)(2,1)S(1)} %get-tuple-element.448), channel_id=1, source_target_pairs={{0,8},{8,16},{16,24},{24,32},{32,40},{40,48},{48,56},{56,64},{64,7... | collective-permute-start | bytes 786440 | tf_op jit(solution)/shard_map/while/body/eval_jaxpr/ppermute | solution.py:12
  52.7 9.5 %collective-permute-start = (bf16[2,32,16,128]{3,1,2,0:T(8,128)(2,1)S(1)}, bf16[2,32,16,128]{3,1,2,0:T(8,128)(2,1)S(1)}, u32[]{:S(2)}, u32[]{:S(2)}) collective-permute-start(bf16[2,32,16,128]{3,1,2,0:T(8,128)(2,1)S(1)} %get-tuple-element.448), channel_id=1, source_target_pairs={{0,8},{8,16},{16,24},{24,32},{32,40},{40,48},{48,56},{56,64},{64,7... | collective-permute-start | bytes 786440 | tf_op jit(solution)/shard_map/while/body/eval_jaxpr/ppermute | solution.py:12
  67.8 9.5 %collective-permute-start = (bf16[2,32,16,128]{3,1,2,0:T(8,128)(2,1)S(1)}, bf16[2,32,16,128]{3,1,2,0:T(8,128)(2,1)S(1)}, u32[]{:S(2)}, u32[]{:S(2)}) collective-permute-start(bf16[2,32,16,128]{3,1,2,0:T(8,128)(2,1)S(1)} %get-tuple-element.448), channel_id=1, source_target_pairs={{0,8},{8,16},{16,24},{24,32},{32,40},{40,48},{48,56},{56,64},{64,7... | collective-permute-start | bytes 786440 | tf_op jit(solution)/shard_map/while/body/eval_jaxpr/ppermute | solution.py:12
  82.9 9.5 %collective-permute-start = (bf16[2,32,16,128]{3,1,2,0:T(8,128)(2,1)S(1)}, bf16[2,32,16,128]{3,1,2,0:T(8,128)(2,1)S(1)}, u32[]{:S(2)}, u32[]{:S(2)}) collective-permute-start(bf16[2,32,16,128]{3,1,2,0:T(8,128)(2,1)S(1)} %get-tuple-element.448), channel_id=1, source_target_pairs={{0,8},{8,16},{16,24},{24,32},{32,40},{40,48},{48,56},{56,64},{64,7... | collective-permute-start | bytes 786440 | tf_op jit(solution)/shard_map/while/body/eval_jaxpr/ppermute | solution.py:12
  98.0 9.5 %collective-permute-start = (bf16[2,32,16,128]{3,1,2,0:T(8,128)(2,1)S(1)}, bf16[2,32,16,128]{3,1,2,0:T(8,128)(2,1)S(1)}, u32[]{:S(2)}, u32[]{:S(2)}) collective-permute-start(bf16[2,32,16,128]{3,1,2,0:T(8,128)(2,1)S(1)} %get-tuple-element.448), channel_id=1, source_target_pairs={{0,8},{8,16},{16,24},{24,32},{32,40},{40,48},{48,56},{56,64},{64,7... | collective-permute-start | bytes 786440 | tf_op jit(solution)/shard_map/while/body/eval_jaxpr/ppermute | solution.py:12
  113.1 9.5 %collective-permute-start = (bf16[2,32,16,128]{3,1,2,0:T(8,128)(2,1)S(1)}, bf16[2,32,16,128]{3,1,2,0:T(8,128)(2,1)S(1)}, u32[]{:S(2)}, u32[]{:S(2)}) collective-permute-start(bf16[2,32,16,128]{3,1,2,0:T(8,128)(2,1)S(1)} %get-tuple-element.448), channel_id=1, source_target_pairs={{0,8},{8,16},{16,24},{24,32},{32,40},{40,48},{48,56},{56,64},{64,7... | collective-permute-start | bytes 786440 | tf_op jit(solution)/shard_map/while/body/eval_jaxpr/ppermute | solution.py:12
  128.2 9.5 %collective-permute-start = (bf16[2,32,16,128]{3,1,2,0:T(8,128)(2,1)S(1)}, bf16[2,32,16,128]{3,1,2,0:T(8,128)(2,1)S(1)}, u32[]{:S(2)}, u32[]{:S(2)}) collective-permute-start(bf16[2,32,16,128]{3,1,2,0:T(8,128)(2,1)S(1)} %get-tuple-element.448), channel_id=1, source_target_pairs={{0,8},{8,16},{16,24},{24,32},{32,40},{40,48},{48,56},{56,64},{64,7... | collective-permute-start | bytes 786440 | tf_op jit(solution)/shard_map/while/body/eval_jaxpr/ppermute | solution.py:12
  143.3 9.5 %collective-permute-start = (bf16[2,32,16,128]{3,1,2,0:T(8,128)(2,1)S(1)}, bf16[2,32,16,128]{3,1,2,0:T(8,128)(2,1)S(1)}, u32[]{:S(2)}, u32[]{:S(2)}) collective-permute-start(bf16[2,32,16,128]{3,1,2,0:T(8,128)(2,1)S(1)} %get-tuple-element.448), channel_id=1, source_target_pairs={{0,8},{8,16},{16,24},{24,32},{32,40},{40,48},{48,56},{56,64},{64,7... | collective-permute-start | bytes 786440 | tf_op jit(solution)/shard_map/while/body/eval_jaxpr/ppermute | solution.py:12
  158.4 9.5 %collective-permute-start = (bf16[2,32,16,128]{3,1,2,0:T(8,128)(2,1)S(1)}, bf16[2,32,16,128]{3,1,2,0:T(8,128)(2,1)S(1)}, u32[]{:S(2)}, u32[]{:S(2)}) collective-permute-start(bf16[2,32,16,128]{3,1,2,0:T(8,128)(2,1)S(1)} %get-tuple-element.448), channel_id=1, source_target_pairs={{0,8},{8,16},{16,24},{24,32},{32,40},{40,48},{48,56},{56,64},{64,7... | collective-permute-start | bytes 786440 | tf_op jit(solution)/shard_map/while/body/eval_jaxpr/ppermute | solution.py:12
  173.5 9.5 %collective-permute-start = (bf16[2,32,16,128]{3,1,2,0:T(8,128)(2,1)S(1)}, bf16[2,32,16,128]{3,1,2,0:T(8,128)(2,1)S(1)}, u32[]{:S(2)}, u32[]{:S(2)}) collective-permute-start(bf16[2,32,16,128]{3,1,2,0:T(8,128)(2,1)S(1)} %get-tuple-element.448), channel_id=1, source_target_pairs={{0,8},{8,16},{16,24},{24,32},{32,40},{40,48},{48,56},{56,64},{64,7... | collective-permute-start | bytes 786440 | tf_op jit(solution)/shard_map/while/body/eval_jaxpr/ppermute | solution.py:12
  188.6 9.5 %collective-permute-start = (bf16[2,32,16,128]{3,1,2,0:T(8,128)(2,1)S(1)}, bf16[2,32,16,128]{3,1,2,0:T(8,128)(2,1)S(1)}, u32[]{:S(2)}, u32[]{:S(2)}) collective-permute-start(bf16[2,32,16,128]{3,1,2,0:T(8,128)(2,1)S(1)} %get-tuple-element.448), channel_id=1, source_target_pairs={{0,8},{8,16},{16,24},{24,32},{32,40},{40,48},{48,56},{56,64},{64,7... | collective-permute-start | bytes 786440 | tf_op jit(solution)/shard_map/while/body/eval_jaxpr/ppermute | solution.py:12
  203.7 9.5 %collective-permute-start = (bf16[2,32,16,128]{3,1,2,0:T(8,128)(2,1)S(1)}, bf16[2,32,16,128]{3,1,2,0:T(8,128)(2,1)S(1)}, u32[]{:S(2)}, u32[]{:S(2)}) collective-permute-start(bf16[2,32,16,128]{3,1,2,0:T(8,128)(2,1)S(1)} %get-tuple-element.448), channel_id=1, source_target_pairs={{0,8},{8,16},{16,24},{24,32},{32,40},{40,48},{48,56},{56,64},{64,7... | collective-permute-start | bytes 786440 | tf_op jit(solution)/shard_map/while/body/eval_jaxpr/ppermute | solution.py:12
  218.8 9.5 %collective-permute-start = (bf16[2,32,16,128]{3,1,2,0:T(8,128)(2,1)S(1)}, bf16[2,32,16,128]{3,1,2,0:T(8,128)(2,1)S(1)}, u32[]{:S(2)}, u32[]{:S(2)}) collective-permute-start(bf16[2,32,16,128]{3,1,2,0:T(8,128)(2,1)S(1)} %get-tuple-element.448), channel_id=1, source_target_pairs={{0,8},{8,16},{16,24},{24,32},{32,40},{40,48},{48,56},{56,64},{64,7... | collective-permute-start | bytes 786440 | tf_op jit(solution)/shard_map/while/body/eval_jaxpr/ppermute | solution.py:12
  233.9 9.5 %collective-permute-start = (bf16[2,32,16,128]{3,1,2,0:T(8,128)(2,1)S(1)}, bf16[2,32,16,128]{3,1,2,0:T(8,128)(2,1)S(1)}, u32[]{:S(2)}, u32[]{:S(2)}) collective-permute-start(bf16[2,32,16,128]{3,1,2,0:T(8,128)(2,1)S(1)} %get-tuple-element.448), channel_id=1, source_target_pairs={{0,8},{8,16},{16,24},{24,32},{32,40},{40,48},{48,56},{56,64},{64,7... | collective-permute-start | bytes 786440 | tf_op jit(solution)/shard_map/while/body/eval_jaxpr/ppermute | solution.py:12
  249.8 11.5 %all-to-all-start = ((f32[16,1,1024]{2,1,0:T(1,128)}), f32[16,1,1024]{2,1,0:T(1,128)S(1)}, u32[]{:S(2)}, u32[]{:S(2)}) async-start(f32[16,1,1024]{2,1,0:T(1,128)} %reshape.310), calls=%async_computation | async-start | bytes 131072 | tf_op jit(solution)/shard_map/all_to_all | solution.py:102
  261.3 61.0 %all-to-all-start.2 = ((bf16[16,2,32,16,128]{4,3,1,2,0:T(8,128)(2,1)}), bf16[16,2,32,16,128]{4,3,1,2,0:T(8,128)(2,1)}, u32[]{:S(2)}, u32[]{:S(2)}) async-start(bf16[16,2,32,16,128]{4,3,1,2,0:T(8,128)(2,1)} %copy.73), calls=%async_computation.2 | async-start | bytes 8388608 | tf_op jit(solution)/shard_map/all_to_all | solution.py:93
  322.3 10.6 %all-to-all-start.1 = ((f32[8,1,2048]{2,1,0:T(1,128)}), f32[8,1,2048]{2,1,0:T(1,128)S(1)}, u32[]{:S(2)}, u32[]{:S(2)}) async-start(f32[8,1,2048]{2,1,0:T(1,128)} %reshape.312), calls=%async_computation.1 | async-start | bytes 131072 | tf_op jit(solution)/shard_map/all_to_all | solution.py:101
  332.9 64.0 %all-to-all-start.3 = ((bf16[16,2,32,16,128]{4,3,1,0,2:T(8,128)(2,1)}), bf16[16,2,32,16,128]{4,3,1,0,2:T(8,128)(2,1)}, u32[]{:S(2)}, u32[]{:S(2)}) async-start(bf16[16,2,32,16,128]{4,3,1,0,2:T(8,128)(2,1)} %copy.61), calls=%async_computation.3 | async-start | bytes 8388608 | tf_op jit(solution)/shard_map/all_to_all | solution.py:92
where the time goes:
time: 418 us; the launch traced here: 410 us
  waiting for transfers between devices  241 us (58%)
  matrix products  71.7 us (17%)
  other arithmetic  43.9 us (11%)
  local copies, waits for them, and re-layouts  31.5 us (8%)
  starting transfers between devices  19.7 us (5%)
    ppermute x15, waiting for transfers between devices, passed_along(): return lax.ppermute(value, axis, pairs)  130 us
    all_to_all x1, waiting for transfers between devices, on_device(): lax.all_to_all(lax.all_to_all(buffers[0].astype(jnp.float32), 'ctx', spli...  55.4 us
    all_to_all x1, waiting for transfers between devices, on_device(): lax.all_to_all(buffers[0].astype(jnp.float32), 'ctx', split_axis=0, conca...  52.7 us
    dot_general x16, matrix products, shard_partial(): jnp.einsum('rkgts,rskd->rtkgd', weights, value_rows, preferred_element_ty...  44.2 us
    dot_general x16, matrix products, shard_partial(): jnp.einsum('rtkgd,rskd->rkgts', grouped, key_rows, preferred_element_type...  27.5 us
    reduce_sum x16, other arithmetic, shard_partial(): totals = jnp.sum(exponent, -1, keepdims=True)  21.2 us
    reduce_sum x1, other arithmetic, combine_parts(): jnp.sum(shares[..., None] * partials.astype(jnp.float32), 0)  9.32 us
    unnamed x23, local copies, waits for them, and re-layouts  9.07 us
  transfers between devices with their start and end apart: 19, of which 19 were waited for; matrix products, arithmetic and copies ran while one was open for 7% of the time, Pallas kernels for 0%

commit v1 on v0

v1 whole, which is shorter than its diff:
```python
import functools

import jax
import jax.numpy as jnp
from jax import lax
from jax.experimental import pallas as pl
from jax.experimental.pallas import tpu as pltpu
from jax.sharding import Mesh
from jax.sharding import PartitionSpec as P

LOG2E = 1.4426950408889634
LN2 = 0.6931471805599453
MASKED = -1e30
SUM_LOW = 2.0**-60
SUM_HIGH = 2.0**100
VMEM = 56 << 20


def dot_nt(a, b):
    return lax.dot_general(a, b, (((1,), (1,)), ((), ())), preferred_element_type=jnp.float32)


def prepare_kernel(where_ref, len_ref, vo_ref, vp_ref, no_ref, np_ref, ko_ref, kp_ref, vt_ref, kn_ref):
    r = pl.program_id(0)
    rows = vo_ref.shape[1]
    extra = vt_ref.shape[1] - 128
    me = where_ref[0]
    for part, ref in enumerate((vo_ref, vp_ref)):
        owner = me if part == 0 else me + 1 - 2 * lax.rem(me, 2)
        valid = len_ref[r] - owner * rows
        row_id = lax.broadcasted_iota(jnp.int32, (rows, 128), 0)
        kept = jnp.where(row_id < valid, ref[0].astype(jnp.float32), 0.0).astype(jnp.bfloat16)
        vt_ref[0, :128, part * rows : (part + 1) * rows] = jnp.transpose(kept)
        col_id = lax.broadcasted_iota(jnp.int32, (extra, rows), 1)
        vt_ref[0, 128:, part * rows : (part + 1) * rows] = jnp.where(
            col_id < valid, 1.0, 0.0
        ).astype(jnp.bfloat16)
    new = no_ref.shape[1]
    fresh = jnp.concatenate(
        [no_ref[0], np_ref[0], jnp.zeros((128 - 2 * new, 128), jnp.bfloat16)], 0
    )
    vt_ref[0, :128, 2 * rows :] = jnp.transpose(fresh)
    vt_ref[0, 128:, 2 * rows :] = jnp.ones((extra, 128), jnp.bfloat16)
    kn_ref[0, :new, :] = ko_ref[0]
    kn_ref[0, new:, :] = kp_ref[0]


def prepare(where, cached_len, v_own, v_par, n_own, n_par, k_own, k_par):
    requests, rows, dim = v_own.shape
    new = n_own.shape[1]
    whole = lambda n: pl.BlockSpec((1, n, dim), lambda r, *_: (r, 0, 0))
    return pl.pallas_call(
        prepare_kernel,
        grid_spec=pltpu.PrefetchScalarGridSpec(
            num_scalar_prefetch=2,
            grid=(requests,),
            in_specs=[whole(rows), whole(rows), whole(new), whole(new), whole(new), whole(new)],
            out_specs=[
                pl.BlockSpec((1, 144, 2 * rows + 128), lambda r, *_: (r, 0, 0)),
                whole(2 * new),
            ],
        ),
        out_shape=[
            jax.ShapeDtypeStruct((requests, 144, 2 * rows + 128), jnp.bfloat16),
            jax.ShapeDtypeStruct((requests, 2 * new, dim), jnp.bfloat16),
        ],
        compiler_params=pltpu.CompilerParams(vmem_limit_bytes=VMEM),
        cost_estimate=pl.CostEstimate(flops=10**6, bytes_accessed=4 << 20, transcendentals=0),
    )(where, cached_len, v_own, v_par, n_own, n_par, k_own, k_par)


def attend_kernel(
    request, pairs, where_ref, len_ref, span_ref, *refs
):
    n_blocks = 2 * len(pairs)
    q_refs = refs[:n_blocks]
    ko_ref, kp_ref, kn_ref, vt_ref, out_ref = refs[n_blocks : n_blocks + 5]
    q_buf, acc_ref, top_ref, sems = refs[n_blocks + 5 :]
    step = pl.program_id(0)
    me = where_ref[0]
    core = lax.rem(me, 2)
    chip = me // 2
    rows = ko_ref.shape[1]
    n_new = kn_ref.shape[1]
    block = q_buf.shape[1]
    width = 2 * block

    def fetch(n):
        slot = 2 * (n // 2) + (n % 2 + lax.rem(chip, 2)) % 2
        return pltpu.make_async_copy(q_refs[n].at[request], q_buf.at[slot], sems.at[n // 2])

    @pl.when(step == 0)
    def _():
        for n in range(n_blocks):
            fetch(n).start()

    for n in range(n_blocks):

        @pl.when(step == n // 2)
        def _(n=n):
            fetch(n).wait()

    relative = jnp.int32(pairs[0])
    for n, pair in enumerate(pairs):
        relative = jnp.where(step == n, jnp.int32(pair), relative)
    low_chip = 2 * ((chip // 2) ^ relative)

    q = q_buf[pl.ds(2 * step, 2)].reshape(width, 128)
    scale = LOG2E * 128**-0.5

    def span(shard, half):
        return span_ref[request, 2 * shard + half]

    lane = lax.broadcasted_iota(jnp.int32, (1, width), 1)
    q_span = jnp.zeros((1, width), jnp.int32)
    for n in range(4):
        q_span = jnp.where(
            lane // (block // 2) == n, span(2 * (low_chip + n // 2) + core, n % 2), q_span
        )
    q_pos = q_span * 16 + lax.rem(lane // 16, 16)
    key = lax.broadcasted_iota(jnp.int32, (n_new, 1), 0)
    k_span = jnp.zeros((n_new, 1), jnp.int32)
    first_pos = jnp.int32(1 << 30)
    for n in range(4):
        owner = me if n < 2 else me + 1 - 2 * core
        k_span = jnp.where(key // 16 == n, span(owner, n % 2), k_span)
        first_pos = jnp.minimum(first_pos, span(owner, n % 2) * 16)
    shown = (k_span * 16 + lax.rem(key, 16)) <= q_pos

    def new_scores():
        return jnp.where(shown, dot_nt(kn_ref[0], q) * scale, MASKED)

    def values(p, start, size):
        return jnp.dot(
            vt_ref[0, :, pl.ds(start, size)],
            p.astype(jnp.bfloat16),
            preferred_element_type=jnp.float32,
        )

    acc = values(jnp.exp2(dot_nt(ko_ref[0], q) * scale), 0, rows)
    acc = acc + values(jnp.exp2(dot_nt(kp_ref[0], q) * scale), rows, rows)
    acc = acc + values(jnp.exp2(new_scores()), 2 * rows, n_new)
    acc_ref[...] = acc
    top_ref[...] = jnp.zeros_like(top_ref)

    held = [len_ref[request] - (me if n == 0 else me + 1 - 2 * core) * rows for n in range(2)]
    any_cache = jnp.maximum(held[0], held[1]) > 0
    has_key = (q_pos >= first_pos) | any_cache
    total = acc[128:129, :]
    fine = (total < SUM_HIGH) & ((total > SUM_LOW) | jnp.logical_not(has_key))
    redo = jnp.min(jnp.where(fine, 1, 0)) == 0

    @pl.when(redo)
    def _():
        part = 256

        def highest(ref, valid):
            def body(j, top):
                s = dot_nt(ref[0, pl.ds(j * part, part), :], q) * scale
                row = lax.broadcasted_iota(jnp.int32, (part, width), 0) + j * part
                return jnp.maximum(
                    top, jnp.max(jnp.where(row < valid, s, MASKED), 0, keepdims=True)
                )

            return lambda top: lax.fori_loop(0, rows // part, body, top)

        s_new = new_scores()
        top = jnp.max(s_new, 0, keepdims=True)
        top = highest(ko_ref, held[0])(top)
        top = highest(kp_ref, held[1])(top)
        top_ref[...] = jnp.broadcast_to(top, top_ref.shape)
        acc_ref[...] = values(
            jnp.where(shown, jnp.exp2(jnp.minimum(s_new - top, 0.0)), 0.0), 2 * rows, n_new
        )

        def add(ref, first):
            def body(j, carry):
                s = dot_nt(ref[0, pl.ds(j * part, part), :], q) * scale
                start = pl.multiple_of(first + j * part, part)
                acc_ref[...] += values(jnp.exp2(jnp.minimum(s - top, 0.0)), start, part)
                return carry

            lax.fori_loop(0, rows // part, body, 0)

        add(ko_ref, 0)
        add(kp_ref, rows)

    total = acc_ref[128:129, :]
    some = total > 0.0
    inverse = jnp.where(some, 1.0 / jnp.where(some, total, 1.0), 0.0)
    outputs = jnp.transpose(acc_ref[:128, :] * inverse).astype(jnp.bfloat16)
    log_total = jnp.where(
        some, (top_ref[0:1, :] + jnp.log2(jnp.where(some, total, 1.0))) * LN2, MASKED
    )
    high = log_total.astype(jnp.bfloat16).astype(jnp.float32)
    middle = (log_total - high).astype(jnp.bfloat16).astype(jnp.float32)
    low = log_total - high - middle
    logs = jnp.concatenate(
        [high, middle, low, jnp.zeros((5, width), jnp.float32)], 0
    ).astype(jnp.bfloat16)
    owners = out_ref.shape[1]
    share = block // owners
    out_ref[:, :, :share, :] = outputs.reshape(2, owners, share, 128)
    for n in range(2):
        for owner in range(owners):
            start = n * block + owner * share // 128 * 128
            out_ref[n, owner, share:, :] = logs[:, start : start + 128]


def attend(request, pairs, where, cached_len, span_order, blocks, k_own, k_par, k_new, vt):
    rows = k_own.shape[1]
    n_new = k_new.shape[1]
    block = blocks[0].shape[1]
    owners = 8
    share = block // owners
    steps = len(pairs)

    def out_place(step, where_ref, *_):
        relative = jnp.int32(pairs[0])
        for n, pair in enumerate(pairs):
            relative = jnp.where(step == n, jnp.int32(pair), relative)
        return ((where_ref[0] // 4) ^ relative, 0, 0, 0)

    flops = steps * 2 * block * 2 * rows * 128 * 4
    return pl.pallas_call(
        functools.partial(attend_kernel, request, pairs),
        grid_spec=pltpu.PrefetchScalarGridSpec(
            num_scalar_prefetch=3,
            grid=(steps,),
            in_specs=[pl.BlockSpec(memory_space=pl.ANY)] * (2 * steps)
            + [
                pl.BlockSpec((1, rows, 128), lambda s, *_: (request, 0, 0)),
                pl.BlockSpec((1, rows, 128), lambda s, *_: (request, 0, 0)),
                pl.BlockSpec((1, n_new, 128), lambda s, *_: (request, 0, 0)),
                pl.BlockSpec((1, 144, 2 * rows + 128), lambda s, *_: (request, 0, 0)),
            ],
            out_specs=pl.BlockSpec((2, owners, share + 8, 128), out_place),
            scratch_shapes=[
                pltpu.VMEM((2 * steps, block, 128), jnp.bfloat16),
                pltpu.VMEM((144, 2 * block), jnp.float32),
                pltpu.VMEM((8, 2 * block), jnp.float32),
                pltpu.SemaphoreType.DMA((steps,)),
            ],
        ),
        out_shape=jax.ShapeDtypeStruct((8, owners, share + 8, 128), jnp.bfloat16),
        compiler_params=pltpu.CompilerParams(vmem_limit_bytes=VMEM),
        cost_estimate=pl.CostEstimate(
            flops=flops, bytes_accessed=6 << 20, transcendentals=steps * 2 * block * 2 * rows
        ),
    )(where, cached_len, span_order, *blocks, k_own, k_par, k_new, vt)


def combine_kernel(where_ref, in_ref, *refs):
    out_ref, norm_ref = refs[-2:]
    sources, groups = in_ref.shape[:2]
    share = in_ref.shape[2] - 8
    odd = lax.rem(where_ref[1], 2) == 1
    logs = in_ref[:, :, share:, :].astype(jnp.float32)
    logs = logs[:, :, 0, :] + logs[:, :, 1, :] + logs[:, :, 2, :]
    logs = logs.reshape(sources * groups, 128)
    logs = jnp.where(odd, jnp.concatenate([logs[:, 64:], logs[:, :64]], 1), logs)
    logs = logs.reshape(sources, groups, 128)
    highest = jnp.max(logs, 0)
    weight = jnp.exp(logs - highest[None])
    total = jnp.sum(weight, 0)
    norm_ref[...] = highest + jnp.log(total)
    shares = (weight / total[None]).reshape(sources * groups, 128)
    columns = jnp.transpose(
        jnp.concatenate([shares, jnp.zeros((128 - sources * groups, 128), jnp.float32)], 0)
    )
    tokens = out_ref.shape[1]
    for group in range(groups):
        summed = jnp.zeros((share, 128), jnp.float32)
        for source in range(sources):
            n = source * groups + group
            summed = summed + columns[:share, n : n + 1] * in_ref[
                source, group, :share, :
            ].astype(jnp.float32)
        out_ref[0, :, group] = summed.reshape(tokens, share // tokens, 128).astype(jnp.bfloat16)


def combine(request, requests, where, parts, earlier):
    sources, groups, rows, dim = parts.shape
    share = rows - 8
    tokens = share // 16
    shape = (requests, tokens, groups, 16, dim)
    operands = [where, parts] + ([] if earlier is None else [earlier])
    return pl.pallas_call(
        combine_kernel,
        grid_spec=pltpu.PrefetchScalarGridSpec(
            num_scalar_prefetch=1,
            grid=(1,),
            in_specs=[pl.BlockSpec(parts.shape, lambda *_: (0, 0, 0, 0))]
            + ([] if earlier is None else [pl.BlockSpec(memory_space=pl.ANY)]),
            out_specs=[
                pl.BlockSpec((1,) + shape[1:], lambda *_: (request, 0, 0, 0, 0)),
                pl.BlockSpec((groups, 128), lambda *_: (0, 0)),
            ],
        ),
        out_shape=[
            jax.ShapeDtypeStruct(shape, jnp.bfloat16),
            jax.ShapeDtypeStruct((groups, 128), jnp.float32),
        ],
        input_output_aliases={} if earlier is None else {2: 0},
        compiler_params=pltpu.CompilerParams(vmem_limit_bytes=VMEM),
        cost_estimate=pl.CostEstimate(flops=10**7, bytes_accessed=2 << 20, transcendentals=0),
    )(*operands)


def on_device(queries, new_keys, new_values, cache_keys, cache_values, cached_len, span_order):
    requests, tokens, heads, dim = queries.shape
    yz = lax.axis_index("yz")
    core = lax.axis_index("core")
    kv = lax.axis_index("kv")
    where = jnp.stack([yz * 2 + core, kv]).astype(jnp.int32)
    chips = lax.axis_size("yz")

    def other_core(x):
        return lax.ppermute(x, "core", [(0, 1), (1, 0)])

    k_own = cache_keys.reshape(requests, -1, dim)
    v_own = cache_values.reshape(requests, -1, dim)
    kn_own = new_keys.reshape(requests, -1, dim)
    vn_own = new_values.reshape(requests, -1, dim)
    q_own = queries.reshape(requests, tokens * heads, dim)
    k_par, v_par, kn_par, vn_par = (other_core(x) for x in (k_own, v_own, kn_own, vn_own))
    blocks = [q_own] + [
        lax.ppermute(q_own, "yz", [(c, c ^ s) for c in range(chips)]) for s in range(1, chips)
    ]
    vt, k_new = prepare(where, cached_len, v_own, v_par, vn_own, vn_par, kn_own, kn_par)

    received = []
    for r in range(requests):
        parts = attend(
            r, (0, 1, 2, 3), where, cached_len, span_order, blocks, k_own, k_par, k_new, vt
        )
        sent = parts.reshape((64,) + parts.shape[2:])
        got = lax.all_to_all(sent, ("yz", "kv"), 0, 0, tiled=True)
        received.append(got.reshape(parts.shape))
    attention = None
    norms = []
    for r in range(requests):
        attention, norm = combine(r, requests, where, received[r], attention)
        norms.append(norm[:, : tokens // 8 * heads].reshape(8, tokens // 8, heads))
    norm = jnp.stack(norms).transpose(0, 2, 1, 3).reshape(requests, tokens // 8, 8 * heads)
    return attention.reshape(requests, tokens // 8, 8 * heads, dim), norm


def solution(mesh):
    split = Mesh(mesh.devices.reshape(8, 2, 8), ("yz", "core", "kv"))
    placed = P(None, ("yz", "core"), "kv", None)
    return jax.shard_map(
        on_device,
        mesh=split,
        in_specs=(placed,) * 5 + (P(), P()),
        out_specs=(
            P(None, ("yz", "core", "kv"), None, None),
            P(None, ("yz", "core", "kv"), None),
        ),
        check_vma=False,
    )
```

time: 418 us -> 228 us (0.55); the launches traced: 410 us -> 227 us
  waiting for transfers between devices: 241 us -> 30.2 us
  Pallas kernels: 0 us -> 161 us
  matrix products: 71.7 us -> 0 us
  other arithmetic: 43.9 us -> 0.62 us
  local copies, waits for them, and re-layouts: 31.5 us -> 4.56 us
  starting transfers between devices: 19.7 us -> 30.3 us
    pallas_call x0 -> x5, Pallas kernels: none -> 161 us  [the longest x2 150 us: attend(): pl.pallas_call(functools.partial(attend_kernel, request, pairs), grid_spe...]
    ppermute x15 -> x11, waiting for transfers between devices: 130 us -> 16.9 us  [the longest x7 16.9 us: on_device(): lax.ppermute(q_own, 'yz', [(c, c ^ s) for c in range(chips)])]
    all_to_all x4 -> x2, waiting for transfers between devices: 111 us -> 13.3 us  [on_device(): got = lax.all_to_all(sent, ('yz', 'kv'), 0, 0, tiled=True)]
    dot_general x32 -> x0, matrix products: 71.7 us -> none  [the longest x16 44.2 us: shard_partial(): jnp.einsum('rkgts,rskd->rtkgd', weights, value_rows, preferred_element_ty...]
    reduce_sum x18 -> x0, other arithmetic: 30.7 us -> none  [the longest x16 21.2 us: shard_partial(): totals = jnp.sum(exponent, -1, keepdims=True)]
    ppermute x15 -> x11, starting transfers between devices: 1.12 us -> 17.7 us  [the longest x7 16.6 us: on_device(): lax.ppermute(q_own, 'yz', [(c, c ^ s) for c in range(chips)])]
    all_to_all x4 -> x0, local copies, waits for them, and re-layouts: 6.45 us -> none  [the longest x1 5.42 us: on_device(): lax.all_to_all(buffers[0].astype(jnp.float32), 'ctx', split_axis=0, conca...]
    while x16 -> x0, local copies, waits for them, and re-layouts: 6.19 us -> none  [the longest x1 5.92 us: on_device(): _, buffers = lax.fori_loop(1, cycle_size, cycle_step, (queries, buffers))]
  transfers between devices with their start and end apart: 19 -> 13, of which waited for: 19 -> 6; matrix products, arithmetic and copies ran while one was open for 7% -> 0% of each run, Pallas kernels for 0% -> 36%
where the time goes in v1:
time: 228 us; the launch traced here: 227 us
  Pallas kernels  161 us (71%)
  starting transfers between devices  30.3 us (13%)
  waiting for transfers between devices  30.2 us (13%)
  local copies, waits for them, and re-layouts  4.56 us (2%)
    pallas_call x2, Pallas kernels, attend(): pl.pallas_call(functools.partial(attend_kernel, request, pairs), grid_spe...  150 us
    ppermute x7, waiting for transfers between devices, on_device(): lax.ppermute(q_own, 'yz', [(c, c ^ s) for c in range(chips)])  16.9 us
    ppermute x7, starting transfers between devices, on_device(): lax.ppermute(q_own, 'yz', [(c, c ^ s) for c in range(chips)])  16.6 us
    all_to_all x2, waiting for transfers between devices, on_device(): got = lax.all_to_all(sent, ('yz', 'kv'), 0, 0, tiled=True)  13.3 us
    all_to_all x2, starting transfers between devices, on_device(): got = lax.all_to_all(sent, ('yz', 'kv'), 0, 0, tiled=True)  12.6 us
    pallas_call x2, Pallas kernels, combine(): pl.pallas_call(combine_kernel, grid_spec=pltpu.PrefetchScalarGridSpec(num...  7.16 us
  transfers between devices with their start and end apart: 13, of which 6 were waited for; matrix products, arithmetic and copies ran while one was open for 0% of the time, Pallas kernels for 36%

profile of v1, /device:TPU:0, one launch (start us, length us, event | category | flops | bytes accessed | tf_op | source)
XLA Modules:
  0.0 227.0 jit_solution(2121538964004371009)
XLA Ops:
  0.6 0.1 collective-permute-start.8
  0.7 0.5 collective-permute-start.7
  1.2 0.1 collective-permute-start.10
  1.3 0.4 collective-permute-start.9
  1.7 6.8 %collective-permute-start.6 = (bf16[2,512,128]{2,1,0:T(8,128)(2,1)}, bf16[2,512,128]{2,1,0:T(8,128)(2,1)S(1)}, u32[]{:S(2)}, u32[]{:S(2)}) collective-permute-start(bf16[2,512,128]{2,1,0:T(8,128)(2,1)} %bitcast.34), channel_id=1, source_target_pairs={{0,112},{16,96},{32,80},{48,64},{64,48},{80,32},{96,16},{112,0},{1... | collective-permute-start | bytes 786440 | tf_op jit(solution)/shard_map/ppermute | solution.py:328
  8.5 0.0 collective-permute-done.10.kp_ref
  8.5 3.2 %collective-permute-start.5 = (bf16[2,512,128]{2,1,0:T(8,128)(2,1)}, bf16[2,512,128]{2,1,0:T(8,128)(2,1)S(1)}, u32[]{:S(2)}, u32[]{:S(2)}) collective-permute-start(bf16[2,512,128]{2,1,0:T(8,128)(2,1)} %bitcast.35), channel_id=1, source_target_pairs={{0,96},{16,112},{32,64},{48,80},{64,32},{80,48},{96,0},{112,16},{1... | collective-permute-start | bytes 786440 | tf_op jit(solution)/shard_map/ppermute | solution.py:328
  11.7 0.0 collective-permute-done.9.np_ref
  11.7 0.8 collective-permute-start.4
  12.5 3.6 %collective-permute-done.6.refs_7_ = bf16[2,512,128]{2,1,0:T(8,128)(2,1)S(1)} collective-permute-done((bf16[2,512,128]{2,1,0:T(8,128)(2,1)}, bf16[2,512,128]{2,1,0:T(8,128)(2,1)S(1)}, u32[]{:S(2)}, u32[]{:S(2)}) %collective-permute-start.6) | collective-permute-done | bytes 262176 | tf_op jit(solution)/shard_map/ppermute | solution.py:328
  16.1 1.8 collective-permute-start.3
  17.9 4.2 %collective-permute-done.5.refs_6_ = bf16[2,512,128]{2,1,0:T(8,128)(2,1)S(1)} collective-permute-done((bf16[2,512,128]{2,1,0:T(8,128)(2,1)}, bf16[2,512,128]{2,1,0:T(8,128)(2,1)S(1)}, u32[]{:S(2)}, u32[]{:S(2)}) %collective-permute-start.5) | collective-permute-done | bytes 262176 | tf_op jit(solution)/shard_map/ppermute | solution.py:328
  22.1 2.3 %collective-permute-start.2 = (bf16[2,512,128]{2,1,0:T(8,128)(2,1)}, bf16[2,512,128]{2,1,0:T(8,128)(2,1)S(1)}, u32[]{:S(2)}, u32[]{:S(2)}) collective-permute-start(bf16[2,512,128]{2,1,0:T(8,128)(2,1)} %bitcast.38), channel_id=1, source_target_pairs={{0,48},{16,32},{32,16},{48,0},{64,112},{80,96},{96,80},{112,64},{1... | collective-permute-start | bytes 786440 | tf_op jit(solution)/shard_map/ppermute | solution.py:328
  24.4 2.9 %collective-permute-done.4.refs_5_ = bf16[2,512,128]{2,1,0:T(8,128)(2,1)S(1)} collective-permute-done((bf16[2,512,128]{2,1,0:T(8,128)(2,1)}, bf16[2,512,128]{2,1,0:T(8,128)(2,1)S(1)}, u32[]{:S(2)}, u32[]{:S(2)}) %collective-permute-start.4) | collective-permute-done | bytes 262176 | tf_op jit(solution)/shard_map/ppermute | solution.py:328
  27.3 1.2 collective-permute-start.1
  28.5 0.0 collective-permute-done.8.vp_ref
  28.5 0.6 collective-permute-start
  29.1 0.6 pad_add_fusion.where_ref
  29.7 0.0 copy-done.3
  29.7 0.0 copy-done.4
  29.7 0.0 copy-done.2
  29.7 3.8 %shard_map.86 = (bf16[2,144,4224]{2,1,0:T(8,128)(2,1)}, bf16[2,64,128]{2,1,0:T(8,128)(2,1)}) custom-call(s32[2]{0:T(128)} %pad_add_fusion.where_ref, s32[2]{0:T(128)} %len_ref.5, bf16[2,2048,128]{2,1,0:T(8,128)(2,1)} %bitcast.23, bf16[2,2048,128]{2,1,0:T(8,128)(2,1)} %copy-done.2, bf16[2,32,128]{2,1,0:T(8,128)(2,1)} %bitcast.26, ...), custom_call_target="tpu_custom_call" | custom-call | flops 1000000 | bytes 4194304 | tf_op jit(solution)/shard_map/pallas_call | solution.py:52
  33.5 0.0 collective-permute-done.3.refs_4_
  33.5 0.0 copy-start.10
  33.5 0.0 collective-permute-done.2.refs_3_
  33.5 0.0 copy-start.11
  33.5 4.8 %collective-permute-done.1.refs_2_ = bf16[2,512,128]{2,1,0:T(8,128)(2,1)} collective-permute-done((bf16[2,512,128]{2,1,0:T(8,128)(2,1)}, bf16[2,512,128]{2,1,0:T(8,128)(2,1)}, u32[]{:S(2)}, u32[]{:S(2)}) %collective-permute-start.1) | collective-permute-done | bytes 262176 | tf_op jit(solution)/shard_map/ppermute | solution.py:328
  38.3 1.4 collective-permute-done.refs_1_
  39.7 0.0 collective-permute-done.7.refs_9_
  39.7 0.0 copy-done.7
  39.7 0.0 copy-done.8
  39.7 0.0 copy-done.9
  39.7 0.0 copy-done.10
  39.8 1.0 copy-done.6
  40.7 74.8 %shard_map.88 = bf16[8,8,72,128]{3,2,1,0:T(8,128)(2,1)} custom-call(s32[2]{0:T(128)} %pad_add_fusion.where_ref, s32[2]{0:T(128)} %len_ref.5, s32[2,32]{1,0:T(2,128)} %span_ref.3, bf16[2,512,128]{2,1,0:T(8,128)(2,1)} %bitcast.41, bf16[2,512,128]{2,1,0:T(8,128)(2,1)} %collective-permute-done.refs_1_, bf16[2,512,128]{2,1,0:T(8,128)(2,1)} %collective-permute-done.1.refs_2_, ...), custom_call_target="tpu_custom_call" | custom-call | flops 8589934592 | bytes 6291456 | tf_op jit(solution)/shard_map/pallas_call | solution.py:225
  115.5 6.5 %all-to-all-start.1 = ((bf16[64,72,128]{2,1,0:T(8,128)(2,1)}), bf16[64,72,128]{2,1,0:T(8,128)(2,1)S(1)}, u32[]{:S(2)}, u32[]{:S(2)}) async-start(bf16[64,72,128]{2,1,0:T(8,128)(2,1)} %bitcast.21), calls=%async_computation.1 | async-start | bytes 2359296 | tf_op jit(solution)/shard_map/all_to_all | solution.py:338
  122.0 74.9 %shard_map.87 = bf16[8,8,72,128]{3,2,1,0:T(8,128)(2,1)} custom-call(s32[2]{0:T(128)} %pad_add_fusion.where_ref, s32[2]{0:T(128)} %len_ref.5, s32[2,32]{1,0:T(2,128)} %span_ref.3, bf16[2,512,128]{2,1,0:T(8,128)(2,1)} %bitcast.42, bf16[2,512,128]{2,1,0:T(8,128)(2,1)} %collective-permute-done.refs_1_, bf16[2,512,128]{2,1,0:T(8,128)(2,1)} %collective-permute-done.1.refs_2_, ...), custom_call_target="tpu_custom_call" | custom-call | flops 8589934592 | bytes 6291456 | tf_op jit(solution)/shard_map/pallas_call | solution.py:225
  196.9 0.0 all-to-all-done.1
  196.9 1.0 copy-done
  197.9 6.1 %all-to-all-start = ((bf16[64,72,128]{2,1,0:T(8,128)(2,1)}), bf16[64,72,128]{2,1,0:T(8,128)(2,1)S(1)}, u32[]{:S(2)}, u32[]{:S(2)}) async-start(bf16[64,72,128]{2,1,0:T(8,128)(2,1)} %bitcast.20), calls=%async_computation | async-start | bytes 2359296 | tf_op jit(solution)/shard_map/all_to_all | solution.py:338
  204.0 3.6 %shard_map.89 = (bf16[2,4,8,16,128]{4,3,2,1,0:T(8,128)(2,1)}, f32[8,128]{1,0:T(8,128)}) custom-call(s32[2]{0:T(128)} %pad_add_fusion.where_ref, bf16[8,8,72,128]{3,2,1,0:T(8,128)(2,1)} %bitcast.18), custom_call_target="tpu_custom_call" | custom-call | flops 10000000 | bytes 2097152 | tf_op jit(solution)/shard_map/pallas_call | solution.py:288
  207.6 13.3 %all-to-all-done = bf16[64,72,128]{2,1,0:T(8,128)(2,1)S(1)} async-done(((bf16[64,72,128]{2,1,0:T(8,128)(2,1)}), bf16[64,72,128]{2,1,0:T(8,128)(2,1)S(1)}, u32[]{:S(2)}, u32[]{:S(2)}) %all-to-all-start) | async-done | bytes 1179680 | tf_op jit(solution)/shard_map/all_to_all | solution.py:338
  220.9 1.0 copy-done.1
  221.9 3.6 %shard_map.90 = (bf16[2,4,8,16,128]{4,3,2,1,0:T(8,128)(2,1)}, f32[8,128]{1,0:T(8,128)}) custom-call(s32[2]{0:T(128)} %pad_add_fusion.where_ref, bf16[8,8,72,128]{3,2,1,0:T(8,128)(2,1)} %bitcast.19, bf16[2,4,8,16,128]{4,3,2,1,0:T(8,128)(2,1)} %get-tuple-element.10.refs_0_), custom_call_target="tpu_custom_call", output_to_operand_aliasing={{0}: (2, {})} | custom-call | flops 10000000 | bytes 2097152 | tf_op jit(solution)/shard_map/pallas_call | solution.py:288
  225.5 0.8 stack_reshape.7
  226.2 0.0 copy-done.5
  226.2 0.1 stack_reshape.6
  226.3 0.7 reshape.47
  (13 shorter events, 0.0 us)
Async XLA Ops:
  0.6 27.9 %collective-permute-start.8 = (bf16[2,2048,128]{2,1,0:T(8,128)(2,1)}, bf16[2,2048,128]{2,1,0:T(8,128)(2,1)S(1)}, u32[]{:S(2)}, u32[]{:S(2)}) collective-permute-start(bf16[2,2048,128]{2,1,0:T(8,128)(2,1)} %bitcast.22), channel_id=1, source_target_pairs={{0,8},{8,0},{1,9},{9,1},{2,10},{10,2},{3,11},{11,3},{4,12},{12,4},... | collective-permute-start | bytes 3145736 | tf_op jit(solution)/shard_map/ppermute | solution.py:319
  0.7 39.0 %collective-permute-start.7 = (bf16[2,2048,128]{2,1,0:T(8,128)(2,1)}, bf16[2,2048,128]{2,1,0:T(8,128)(2,1)S(1)}, u32[]{:S(2)}, u32[]{:S(2)}) collective-permute-start(bf16[2,2048,128]{2,1,0:T(8,128)(2,1)} %bitcast.31), channel_id=1, source_target_pairs={{0,8},{8,0},{1,9},{9,1},{2,10},{10,2},{3,11},{11,3},{4,12},{12,4},... | collective-permute-start | bytes 3145736 | tf_op jit(solution)/shard_map/ppermute | solution.py:319
  1.2 7.3 %collective-permute-start.10 = (bf16[2,32,128]{2,1,0:T(8,128)(2,1)}, bf16[2,32,128]{2,1,0:T(8,128)(2,1)S(1)}, u32[]{:S(2)}, u32[]{:S(2)}) collective-permute-start(bf16[2,32,128]{2,1,0:T(8,128)(2,1)} %bitcast.27), channel_id=1, source_target_pairs={{0,8},{8,0},{1,9},{9,1},{2,10},{10,2},{3,11},{11,3},{4,12},{12,4},... | collective-permute-start | bytes 49160 | tf_op jit(solution)/shard_map/ppermute | solution.py:319
  1.3 10.4 %collective-permute-start.9 = (bf16[2,32,128]{2,1,0:T(8,128)(2,1)}, bf16[2,32,128]{2,1,0:T(8,128)(2,1)S(1)}, u32[]{:S(2)}, u32[]{:S(2)}) collective-permute-start(bf16[2,32,128]{2,1,0:T(8,128)(2,1)} %bitcast.25), channel_id=1, source_target_pairs={{0,8},{8,0},{1,9},{9,1},{2,10},{10,2},{3,11},{11,3},{4,12},{12,4},... | collective-permute-start | bytes 49160 | tf_op jit(solution)/shard_map/ppermute | solution.py:319
  1.7 14.4 %collective-permute-start.6 = (bf16[2,512,128]{2,1,0:T(8,128)(2,1)}, bf16[2,512,128]{2,1,0:T(8,128)(2,1)S(1)}, u32[]{:S(2)}, u32[]{:S(2)}) collective-permute-start(bf16[2,512,128]{2,1,0:T(8,128)(2,1)} %bitcast.34), channel_id=1, source_target_pairs={{0,112},{16,96},{32,80},{48,64},{64,48},{80,32},{96,16},{112,0},{1... | collective-permute-start | bytes 786440 | tf_op jit(solution)/shard_map/ppermute | solution.py:328
  8.5 21.2 %copy-start.3 = (bf16[2,32,128]{2,1,0:T(8,128)(2,1)}, bf16[2,32,128]{2,1,0:T(8,128)(2,1)S(1)}, u32[]{:S(2)}) copy-start(bf16[2,32,128]{2,1,0:T(8,128)(2,1)S(1)} %collective-permute-done.10.kp_ref) | copy-start | bytes 49156
  8.5 13.6 %collective-permute-start.5 = (bf16[2,512,128]{2,1,0:T(8,128)(2,1)}, bf16[2,512,128]{2,1,0:T(8,128)(2,1)S(1)}, u32[]{:S(2)}, u32[]{:S(2)}) collective-permute-start(bf16[2,512,128]{2,1,0:T(8,128)(2,1)} %bitcast.35), channel_id=1, source_target_pairs={{0,96},{16,112},{32,64},{48,80},{64,32},{80,48},{96,0},{112,16},{1... | collective-permute-start | bytes 786440 | tf_op jit(solution)/shard_map/ppermute | solution.py:328
  11.7 18.0 %copy-start.4 = (bf16[2,32,128]{2,1,0:T(8,128)(2,1)}, bf16[2,32,128]{2,1,0:T(8,128)(2,1)S(1)}, u32[]{:S(2)}) copy-start(bf16[2,32,128]{2,1,0:T(8,128)(2,1)S(1)} %collective-permute-done.9.np_ref) | copy-start | bytes 49156
  11.7 15.6 %collective-permute-start.4 = (bf16[2,512,128]{2,1,0:T(8,128)(2,1)}, bf16[2,512,128]{2,1,0:T(8,128)(2,1)S(1)}, u32[]{:S(2)}, u32[]{:S(2)}) collective-permute-start(bf16[2,512,128]{2,1,0:T(8,128)(2,1)} %bitcast.36), channel_id=1, source_target_pairs={{0,80},{16,64},{32,112},{48,96},{64,16},{80,0},{96,48},{112,32},{1... | collective-permute-start | bytes 786440 | tf_op jit(solution)/shard_map/ppermute | solution.py:328
  16.1 23.6 %copy-start.7 = (bf16[2,512,128]{2,1,0:T(8,128)(2,1)}, bf16[2,512,128]{2,1,0:T(8,128)(2,1)S(1)}, u32[]{:S(2)}) copy-start(bf16[2,512,128]{2,1,0:T(8,128)(2,1)S(1)} %collective-permute-done.6.refs_7_) | copy-start | bytes 786436
  16.1 17.4 %collective-permute-start.3 = (bf16[2,512,128]{2,1,0:T(8,128)(2,1)}, bf16[2,512,128]{2,1,0:T(8,128)(2,1)S(1)}, u32[]{:S(2)}, u32[]{:S(2)}) collective-permute-start(bf16[2,512,128]{2,1,0:T(8,128)(2,1)} %bitcast.37), channel_id=1, source_target_pairs={{0,64},{16,80},{32,96},{48,112},{64,0},{80,16},{96,32},{112,48},{1... | collective-permute-start | bytes 786440 | tf_op jit(solution)/shard_map/ppermute | solution.py:328
  22.1 17.6 %copy-start.8 = (bf16[2,512,128]{2,1,0:T(8,128)(2,1)}, bf16[2,512,128]{2,1,0:T(8,128)(2,1)S(1)}, u32[]{:S(2)}) copy-start(bf16[2,512,128]{2,1,0:T(8,128)(2,1)S(1)} %collective-permute-done.5.refs_6_) | copy-start | bytes 786436
  22.1 11.4 %collective-permute-start.2 = (bf16[2,512,128]{2,1,0:T(8,128)(2,1)}, bf16[2,512,128]{2,1,0:T(8,128)(2,1)S(1)}, u32[]{:S(2)}, u32[]{:S(2)}) collective-permute-start(bf16[2,512,128]{2,1,0:T(8,128)(2,1)} %bitcast.38), channel_id=1, source_target_pairs={{0,48},{16,32},{32,16},{48,0},{64,112},{80,96},{96,80},{112,64},{1... | collective-permute-start | bytes 786440 | tf_op jit(solution)/shard_map/ppermute | solution.py:328
  27.3 12.5 %copy-start.9 = (bf16[2,512,128]{2,1,0:T(8,128)(2,1)}, bf16[2,512,128]{2,1,0:T(8,128)(2,1)S(1)}, u32[]{:S(2)}) copy-start(bf16[2,512,128]{2,1,0:T(8,128)(2,1)S(1)} %collective-permute-done.4.refs_5_) | copy-start | bytes 786436
  27.3 11.1 %collective-permute-start.1 = (bf16[2,512,128]{2,1,0:T(8,128)(2,1)}, bf16[2,512,128]{2,1,0:T(8,128)(2,1)}, u32[]{:S(2)}, u32[]{:S(2)}) collective-permute-start(bf16[2,512,128]{2,1,0:T(8,128)(2,1)} %bitcast.39), channel_id=1, source_target_pairs={{0,32},{16,48},{32,0},{48,16},{64,96},{80,112},{96,64},{112,80},{1... | collective-permute-start | bytes 786440 | tf_op jit(solution)/shard_map/ppermute | solution.py:328
  28.5 1.2 copy-start.2
  28.5 11.2 %collective-permute-start = (bf16[2,512,128]{2,1,0:T(8,128)(2,1)}, bf16[2,512,128]{2,1,0:T(8,128)(2,1)}, u32[]{:S(2)}, u32[]{:S(2)}) collective-permute-start(bf16[2,512,128]{2,1,0:T(8,128)(2,1)} %bitcast.40), channel_id=1, source_target_pairs={{0,16},{16,0},{32,48},{48,32},{64,80},{80,64},{96,112},{112,96},{1... | collective-permute-start | bytes 786440 | tf_op jit(solution)/shard_map/ppermute | solution.py:328
  33.5 6.3 %copy-start.10 = (bf16[2,512,128]{2,1,0:T(8,128)(2,1)}, bf16[2,512,128]{2,1,0:T(8,128)(2,1)S(1)}, u32[]{:S(2)}) copy-start(bf16[2,512,128]{2,1,0:T(8,128)(2,1)S(1)} %collective-permute-done.3.refs_4_) | copy-start | bytes 786436
  33.5 6.2 %copy-start.11 = (bf16[2,512,128]{2,1,0:T(8,128)(2,1)}, bf16[2,512,128]{2,1,0:T(8,128)(2,1)S(1)}, u32[]{:S(2)}) copy-start(bf16[2,512,128]{2,1,0:T(8,128)(2,1)S(1)} %collective-permute-done.2.refs_3_) | copy-start | bytes 786436
  39.7 1.0 copy-start.6
  115.5 81.4 %all-to-all-start.1 = ((bf16[64,72,128]{2,1,0:T(8,128)(2,1)}), bf16[64,72,128]{2,1,0:T(8,128)(2,1)S(1)}, u32[]{:S(2)}, u32[]{:S(2)}) async-start(bf16[64,72,128]{2,1,0:T(8,128)(2,1)} %bitcast.21), calls=%async_computation.1 | async-start | bytes 2359296 | tf_op jit(solution)/shard_map/all_to_all | solution.py:338
  196.9 1.0 copy-start
  197.9 22.9 %all-to-all-start = ((bf16[64,72,128]{2,1,0:T(8,128)(2,1)}), bf16[64,72,128]{2,1,0:T(8,128)(2,1)S(1)}, u32[]{:S(2)}, u32[]{:S(2)}) async-start(bf16[64,72,128]{2,1,0:T(8,128)(2,1)} %bitcast.20), calls=%async_computation | async-start | bytes 2359296 | tf_op jit(solution)/shard_map/all_to_all | solution.py:338
  207.6 18.6 %copy-start.5 = (f32[8,128]{1,0:T(8,128)S(1)}, f32[8,128]{1,0:T(8,128)}, u32[]{:S(2)}) copy-start(f32[8,128]{1,0:T(8,128)} %get-tuple-element.12) | copy-start | bytes 12292
  220.9 1.0 copy-start.1

commit v2 on v0

v2 whole, which is shorter than its diff:
```python
import functools

import jax
import jax.numpy as jnp
from jax import lax
from jax.experimental import pallas as pl
from jax.experimental.pallas import tpu as pltpu
from jax.sharding import Mesh
from jax.sharding import PartitionSpec as P

LOG2E = 1.4426950408889634
LN2 = 0.6931471805599453
MASKED = -1e30
SUM_LOW = 2.0**-60
SUM_HIGH = 2.0**100
VMEM = 56 << 20


def dot_nt(a, b):
    return lax.dot_general(a, b, (((1,), (1,)), ((), ())), preferred_element_type=jnp.float32)


def my_place():
    y, z, core = lax.axis_index("y"), lax.axis_index("z"), lax.axis_index("core")
    return (y * 4 + z) * 2 + core, core, y, z, lax.axis_index("kv")


def prepare_kernel(len_ref, vo_ref, vp_ref, vt_ref):
    r = pl.program_id(0)
    rows = vo_ref.shape[1]
    extra = vt_ref.shape[1] - 128
    me, core = my_place()[:2]
    for part, ref in enumerate((vo_ref, vp_ref)):
        owner = me if part == 0 else me + 1 - 2 * core
        valid = len_ref[r] - owner * rows
        row_id = lax.broadcasted_iota(jnp.int32, (rows, 128), 0)
        kept = jnp.where(row_id < valid, ref[0].astype(jnp.float32), 0.0).astype(jnp.bfloat16)
        vt_ref[0, :128, part * rows : (part + 1) * rows] = jnp.transpose(kept)
        col_id = lax.broadcasted_iota(jnp.int32, (extra, rows), 1)
        vt_ref[0, 128:, part * rows : (part + 1) * rows] = jnp.where(
            col_id < valid, 1.0, 0.0
        ).astype(jnp.bfloat16)


def prepare(cached_len, v_own, v_par):
    requests, rows, dim = v_own.shape
    whole = pl.BlockSpec((1, rows, dim), lambda r, *_: (r, 0, 0))
    return pl.pallas_call(
        prepare_kernel,
        grid_spec=pltpu.PrefetchScalarGridSpec(
            num_scalar_prefetch=1,
            grid=(requests,),
            in_specs=[whole, whole],
            out_specs=pl.BlockSpec((1, 144, 2 * rows), lambda r, *_: (r, 0, 0)),
        ),
        out_shape=jax.ShapeDtypeStruct((requests, 144, 2 * rows), jnp.bfloat16),
        compiler_params=pltpu.CompilerParams(vmem_limit_bytes=VMEM),
        cost_estimate=pl.CostEstimate(flops=10**6, bytes_accessed=4 << 20, transcendentals=0),
    )(cached_len, v_own, v_par)


def attend_kernel(tiles, n_q, n_aliased, len_ref, span_ref, *refs):
    inputs = refs[: n_q + 5]
    n_out = 1 + max(tile[0] for tile in tiles) - min(tile[0] for tile in tiles)
    first_out = n_q + 5 + n_aliased
    out_refs = refs[first_out : first_out + n_out]
    scratch = refs[first_out + n_out :]
    ko_ref, kp_ref, no_ref, np_ref, vt_ref, q_buf, acc_ref, top_ref, stage, sem, in_sem = scratch
    requests = sorted({tile[0] for tile in tiles})
    lowest = requests[0]
    rows = ko_ref.shape[1]

    loads = {}

    def load(name, source, target):
        loads[name] = pltpu.make_async_copy(source, target, in_sem.at[len(loads)])
        loads[name].start()

    def load_q(t):
        for half, (source, part) in enumerate(tiles[t][2]):
            array = inputs[source] if part is None else inputs[source].at[part]
            load(("q", t, half), array.at[tiles[t][0]], q_buf.at[t, half])

    def load_v(n):
        for r in requests:
            part = pl.ds(n * rows, rows)
            load(("v", n, r), inputs[n_q + 4].at[r, :, part], vt_ref.at[r - lowest, :, part])

    def load_k(name, index, ref):
        for r in requests:
            load((name, 0, r), inputs[n_q + index].at[r], ref.at[r - lowest])

    load_q(0)
    load_k("ko", 0, ko_ref)
    load_v(0)
    load_k("kp", 1, kp_ref)
    load_v(1)
    load_k("no", 2, no_ref)
    load_k("np", 3, np_ref)
    for t in range(1, len(tiles)):
        load_q(t)
    arrived = set()

    def need(*names):
        for name in names:
            if name not in arrived:
                arrived.add(name)
                loads[name].wait()

    me, core, my_y, my_z, _ = my_place()
    partner = me + 1 - 2 * core
    n_new = 2 * no_ref.shape[2]
    block = q_buf.shape[2]
    width = 2 * block
    scale = LOG2E * 128**-0.5

    def of_tile(t, field):
        if isinstance(t, int):
            return tiles[t][field]
        value = jnp.int32(tiles[0][field])
        for n in range(1, len(tiles)):
            value = jnp.where(t == n, jnp.int32(tiles[n][field]), value)
        return value

    def new_visible(t):
        request, hop = of_tile(t, 0), of_tile(t, 1)
        lane = lax.broadcasted_iota(jnp.int32, (1, width), 1)
        key = lax.broadcasted_iota(jnp.int32, (n_new, 1), 0)
        q_span = jnp.zeros((1, width), jnp.int32)
        k_span = jnp.zeros((n_new, 1), jnp.int32)
        first = jnp.int32(1 << 30)
        for n in range(4):
            source = 2 * ((my_y ^ (n // 2)) * 4 + (my_z ^ hop)) + core
            chosen = span_ref[request, 2 * source + n % 2]
            q_span = jnp.where(lane // (block // 2) == n, chosen, q_span)
            held = span_ref[request, 2 * (me if n < 2 else partner) + n % 2]
            k_span = jnp.where(key // 16 == n, held, k_span)
            first = jnp.minimum(first, held * 16)
        q_pos = q_span * 16 + lax.rem(lane // 16, 16)
        shown = (k_span * 16 + lax.rem(key, 16)) <= q_pos
        cached = len_ref[request] - jnp.minimum(me, partner) * rows > 0
        return shown, (q_pos >= first) | cached

    def values(request, p, start, size):
        return jnp.dot(
            vt_ref[request - lowest, :, pl.ds(start, size)],
            p.astype(jnp.bfloat16),
            preferred_element_type=jnp.float32,
        )

    def new_keys(at):
        return jnp.concatenate([no_ref[at, 0], np_ref[at, 0]], 0)

    def new_values(at, p):
        fresh = [no_ref[at, 1].astype(jnp.float32), np_ref[at, 1].astype(jnp.float32)]
        fresh = jnp.concatenate(fresh + [jnp.zeros((128 - n_new, 128), jnp.float32)], 0)
        turned = jnp.concatenate(
            [jnp.transpose(fresh), jnp.ones((vt_ref.shape[1] - 128, 128), jnp.float32)], 0
        ).astype(jnp.bfloat16)
        return jnp.dot(
            turned[:, :n_new], p.astype(jnp.bfloat16), preferred_element_type=jnp.float32
        )

    def send(t, request, hop):
        place = out_refs[request - lowest].at[my_z ^ hop]
        return pltpu.make_async_copy(stage.at[t], place, sem.at[t])

    def finish(t, acc, top):
        total = acc[128:129, :]
        some = total > 0.0
        safe = jnp.where(some, total, 1.0)
        inverse = jnp.where(some, 1.0 / safe, 0.0)
        outputs = jnp.transpose(acc[:128, :] * inverse).astype(jnp.bfloat16)
        log_total = jnp.where(some, (top + jnp.log2(safe)) * LN2, MASKED)
        high = log_total.astype(jnp.bfloat16).astype(jnp.float32)
        middle = (log_total - high).astype(jnp.bfloat16).astype(jnp.float32)
        low = log_total - high - middle
        logs = jnp.concatenate(
            [high, middle, low, jnp.zeros((5, width), jnp.float32)], 0
        ).astype(jnp.bfloat16)
        owners = stage.shape[2]
        share = block // owners
        for n in range(2):
            place = my_y ^ n
            stage[t, place, :, :share, :] = outputs[n * block : (n + 1) * block].reshape(
                owners, share, 128
            )
            for owner in range(owners):
                start = n * block + owner * share // 128 * 128
                stage[t, place, owner, share:, :] = logs[:, start : start + 128]

    worst = jnp.ones((1, width), jnp.int32)
    for t, (request, hop, source) in enumerate(tiles):
        at = request - lowest
        need(("q", t, 0), ("q", t, 1), ("ko", 0, request))
        q = q_buf[t].reshape(width, 128)
        p = jnp.exp2(dot_nt(ko_ref[at], q) * scale)
        need(("v", 0, request))
        acc = values(request, p, 0, rows)
        need(("kp", 0, request), ("v", 1, request))
        acc = acc + values(request, jnp.exp2(dot_nt(kp_ref[at], q) * scale), rows, rows)
        need(("no", 0, request), ("np", 0, request))
        shown, has_key = new_visible(t)
        s_new = jnp.where(shown, dot_nt(new_keys(at), q) * scale, MASKED)
        acc = acc + new_values(at, jnp.exp2(s_new))
        total = acc[128:129, :]
        fine = (total < SUM_HIGH) & ((total > SUM_LOW) | jnp.logical_not(has_key))
        worst = jnp.minimum(worst, jnp.where(fine, 1, 0))
        finish(t, acc, jnp.zeros((1, width), jnp.float32))
        send(t, request, hop).start()

    @pl.when(jnp.min(worst) == 0)
    def _():
        part = 256
        for t, (request, hop, _) in enumerate(tiles):
            send(t, request, hop).wait()

        def again(t, carry):
            request = of_tile(t, 0)
            q = q_buf[t].reshape(width, 128)
            shown, _ = new_visible(t)
            s_new = jnp.where(shown, dot_nt(new_keys(request - lowest), q) * scale, MASKED)

            def highest(ref, valid, top):
                def body(j, top):
                    s = dot_nt(ref[request - lowest, pl.ds(j * part, part), :], q) * scale
                    row = lax.broadcasted_iota(jnp.int32, (part, width), 0) + j * part
                    s = jnp.where(row < valid, s, MASKED)
                    return jnp.maximum(top, jnp.max(s, 0, keepdims=True))

                return lax.fori_loop(0, rows // part, body, top)

            top = jnp.max(s_new, 0, keepdims=True)
            top = highest(ko_ref, len_ref[request] - me * rows, top)
            top = highest(kp_ref, len_ref[request] - partner * rows, top)
            p_new = jnp.where(shown, jnp.exp2(jnp.minimum(s_new - top, 0.0)), 0.0)
            acc_ref[...] = new_values(request - lowest, p_new)

            def add(ref, first):
                def body(j, carry):
                    s = dot_nt(ref[request - lowest, pl.ds(j * part, part), :], q) * scale
                    start = pl.multiple_of(first + j * part, part)
                    acc_ref[...] += values(
                        request, jnp.exp2(jnp.minimum(s - top, 0.0)), start, part
                    )
                    return carry

                lax.fori_loop(0, rows // part, body, 0)

            add(ko_ref, 0)
            add(kp_ref, rows)
            top_ref[...] = jnp.broadcast_to(top, top_ref.shape)
            finish(t, acc_ref[...], top_ref[0:1, :])
            return carry

        lax.fori_loop(0, len(tiles), again, 0)
        for t, (request, hop, _) in enumerate(tiles):
            send(t, request, hop).start()

    for t, (request, hop, _) in enumerate(tiles):
        send(t, request, hop).wait()


def attend(tiles, cached_len, span_order, q_arrays, k_own, k_par, n_own, n_par, vt, partials):
    rows = k_own.shape[1]
    block = q_arrays[0].shape[-2]
    owners = 8
    share = block // owners
    width = 2 * block
    requests = sorted({tile[0] for tile in tiles})
    result = jax.ShapeDtypeStruct((4, 2, owners, share + 8, 128), jnp.bfloat16)
    keys = (k_own, k_par, n_own, n_par, vt)
    n_in = len(q_arrays) + len(keys)
    return pl.pallas_call(
        functools.partial(attend_kernel, tiles, len(q_arrays), len(partials)),
        in_specs=[pl.BlockSpec(memory_space=pltpu.SMEM)] * 2
        + [pl.BlockSpec(memory_space=pl.ANY)] * (n_in + len(partials)),
        out_specs=[pl.BlockSpec(memory_space=pl.ANY)] * len(requests),
        scratch_shapes=[pltpu.VMEM((len(requests),) + x.shape[1:], x.dtype) for x in keys]
        + [
            pltpu.VMEM((len(tiles), 2, block, 128), jnp.bfloat16),
            pltpu.VMEM((144, width), jnp.float32),
            pltpu.VMEM((8, width), jnp.float32),
            pltpu.VMEM((len(tiles), 2, owners, share + 8, 128), jnp.bfloat16),
            pltpu.SemaphoreType.DMA((len(tiles),)),
            pltpu.SemaphoreType.DMA((len(requests) * 6 + 2 * len(tiles),)),
        ],
        out_shape=[result] * len(requests),
        input_output_aliases={2 + n_in + n: n for n in range(len(partials))},
        compiler_params=pltpu.CompilerParams(vmem_limit_bytes=VMEM),
        cost_estimate=pl.CostEstimate(
            flops=len(tiles) * width * 2 * rows * 128 * 4,
            bytes_accessed=6 << 20,
            transcendentals=len(tiles) * width * 2 * rows,
        ),
    )(cached_len, span_order, *q_arrays, *keys, *partials)


def combine_kernel(request, in_ref, *refs):
    out_ref, norm_ref, held, sem = refs[-4:]
    sources, groups, rows, dim = held.shape
    share = rows - 8
    odd = lax.rem(lax.axis_index("kv"), 2) == 1
    copy = pltpu.make_async_copy(in_ref, held, sem)
    copy.start()
    lane = lax.broadcasted_iota(jnp.int32, (share, 128), 1)
    diagonal = lax.rem(lane, share) == lax.broadcasted_iota(jnp.int32, (share, 128), 0)
    shape = (sources, groups, 128)
    upper = lax.broadcasted_iota(jnp.int32, shape, 2) >= 64
    odd_source = lax.rem(lax.broadcasted_iota(jnp.int32, shape, 0), 2) == 1
    copy.wait()
    logs = held[:, :, share:, :].astype(jnp.float32)
    logs = logs[:, :, 0, :] + logs[:, :, 1, :] + logs[:, :, 2, :]
    turned = jnp.concatenate([logs[..., 64:], logs[..., :64]], 2)
    logs = jnp.where(upper == odd, logs, turned)
    highest = jnp.max(logs, 0)
    weight = jnp.exp(logs - highest[None])
    total = jnp.sum(weight, 0)
    norm = highest + jnp.log(total)
    shares = jnp.where(upper == odd_source, weight / total[None], 0.0)
    tokens = out_ref.shape[1]
    for group in range(groups):
        spread = jnp.concatenate(
            [
                jnp.where(
                    diagonal,
                    shares[n, group : group + 1] + shares[n + 1, group : group + 1],
                    0.0,
                )
                for n in range(0, sources, 2)
            ],
            1,
        )
        high = spread.astype(jnp.bfloat16)
        low = (spread - high.astype(jnp.float32)).astype(jnp.bfloat16)
        values = held[:, group, :share, :].reshape(sources * share, dim)
        summed = jnp.dot(high, values, preferred_element_type=jnp.float32) + jnp.dot(
            low, values, preferred_element_type=jnp.float32
        )
        out_ref[0, :, group] = summed.reshape(tokens, share // tokens, dim).astype(jnp.bfloat16)
    wide = share // tokens
    for token in range(tokens):
        norm_ref[0, token : token + 1, :] = jnp.concatenate(
            [norm[n : n + 1, token * wide : (token + 1) * wide] for n in range(groups)], 1
        )


def combine(request, requests, parts, earlier):
    sources, groups, rows, dim = parts.shape
    share = rows - 8
    tokens = share // 16
    shape = (requests, tokens, groups, 16, dim)
    return pl.pallas_call(
        functools.partial(combine_kernel, request),
        grid=(1,),
        in_specs=[pl.BlockSpec(memory_space=pl.ANY)] * (1 + len(earlier)),
        out_specs=[
            pl.BlockSpec((1,) + shape[1:], lambda *_: (request, 0, 0, 0, 0)),
            pl.BlockSpec((1, tokens, groups * 16), lambda *_: (request, 0, 0)),
        ],
        scratch_shapes=[
            pltpu.VMEM(parts.shape, parts.dtype),
            pltpu.SemaphoreType.DMA,
        ],
        out_shape=[
            jax.ShapeDtypeStruct(shape, jnp.bfloat16),
            jax.ShapeDtypeStruct((requests, tokens, groups * 16), jnp.float32),
        ],
        input_output_aliases={1 + n: n for n in range(len(earlier))},
        compiler_params=pltpu.CompilerParams(vmem_limit_bytes=63 << 20),
        cost_estimate=pl.CostEstimate(flops=10**7, bytes_accessed=2 << 20, transcendentals=0),
    )(parts, *earlier)


def on_device(queries, new_keys, new_values, cache_keys, cache_values, cached_len, span_order):
    requests, tokens, heads, dim = queries.shape

    def swapped(x, axis, flip=1):
        size = lax.axis_size(axis)
        return lax.ppermute(x, axis, [(n, n ^ flip) for n in range(size)])

    k_own = cache_keys.reshape(requests, -1, dim)
    v_own = cache_values.reshape(requests, -1, dim)
    n_own = jnp.stack(
        [new_keys.reshape(requests, -1, dim), new_values.reshape(requests, -1, dim)], 1
    )
    q_own = queries.reshape(requests, tokens * heads, dim)
    v_par = swapped(v_own, "core")
    q_other = swapped(q_own, "y")
    near = [swapped(q_own, "z", flip) for flip in (1, 3)]
    k_par = swapped(k_own, "core")
    n_par = swapped(n_own, "core")
    vt = prepare(cached_len, v_own, v_par)
    q_other, vt, near = lax.optimization_barrier((q_other, vt, near))
    next_to = [swapped(q_other, "z", flip) for flip in (1, 3)]
    far = swapped(jnp.stack([q_own, q_other]), "z", 2)

    common = (cached_len, span_order)
    keys = (k_own, k_par, n_own, n_par, vt)
    here = ((0, None), (1, None))
    partials = attend(
        tuple((r, 0, here) for r in range(requests)), *common, [q_own, q_other], *keys, []
    )
    hops = [near[0], next_to[0], near[1], next_to[1], far]
    received = []
    for r in range(requests):
        tiles = (
            (r, 1, ((0, None), (1, None))),
            (r, 3, ((2, None), (3, None))),
            (r, 2, ((4, 0), (4, 1))),
        )
        (parts,) = attend(tiles, *common, hops, *keys, [partials[r]])
        sent = parts.reshape((64,) + parts.shape[3:])
        got = lax.all_to_all(sent, ("z", "y", "kv"), 0, 0, tiled=True)
        received.append(got.reshape((8, 8) + parts.shape[3:]))
    results = []
    for r in range(requests):
        results = combine(r, requests, received[r], results)
    attention, norm = results
    return attention.reshape(requests, tokens // 8, 8 * heads, dim), norm


def solution(mesh):
    split = Mesh(mesh.devices.reshape(2, 4, 2, 8), ("y", "z", "core", "kv"))
    ctx = ("y", "z", "core")
    placed = P(None, ctx, "kv", None)
    return jax.shard_map(
        on_device,
        mesh=split,
        in_specs=(placed,) * 5 + (P(), P()),
        out_specs=(
            P(None, ctx + ("kv",), None, None),
            P(None, ctx + ("kv",), None),
        ),
        check_vma=False,
    )
```

time: 418 us -> 226 us (0.54)
  waiting for transfers between devices: 241 us -> 19.2 us
  Pallas kernels: 0 us -> 172 us
  matrix products: 71.7 us -> 0 us
  other arithmetic: 43.9 us -> 0.06 us
  local copies, waits for them, and re-layouts: 31.5 us -> 4.52 us
  starting transfers between devices: 19.7 us -> 25.4 us
    pallas_call x0 -> x6, Pallas kernels: none -> 172 us  [the longest x3 163 us: attend(): pl.pallas_call(functools.partial(attend_kernel, tiles, len(q_arrays), len...]
    ppermute x15 -> x9, waiting for transfers between devices: 130 us -> 1.9 us  [swapped(): return lax.ppermute(x, axis, [(n, n ^ flip) for n in range(size)])]
    all_to_all x4 -> x2, waiting for transfers between devices: 111 us -> 17.3 us  [on_device(): got = lax.all_to_all(sent, ('z', 'y', 'kv'), 0, 0, tiled=True)]
    dot_general x32 -> x0, matrix products: 71.7 us -> none  [the longest x16 44.2 us: shard_partial(): jnp.einsum('rkgts,rskd->rtkgd', weights, value_rows, preferred_element_ty...]
    reduce_sum x18 -> x0, other arithmetic: 30.7 us -> none  [the longest x16 21.2 us: shard_partial(): totals = jnp.sum(exponent, -1, keepdims=True)]
    ppermute x15 -> x9, starting transfers between devices: 1.12 us -> 12.6 us  [swapped(): return lax.ppermute(x, axis, [(n, n ^ flip) for n in range(size)])]
    all_to_all x4 -> x0, local copies, waits for them, and re-layouts: 6.45 us -> none  [the longest x1 5.42 us: on_device(): lax.all_to_all(buffers[0].astype(jnp.float32), 'ctx', split_axis=0, conca...]
    while x16 -> x0, local copies, waits for them, and re-layouts: 6.19 us -> none  [the longest x1 5.92 us: on_device(): _, buffers = lax.fori_loop(1, cycle_size, cycle_step, (queries, buffers))]
  transfers between devices with their start and end apart: 19 -> 11, of which waited for: 19 -> 3; matrix products, arithmetic and copies ran while one was open for 7% -> 0% of each run, Pallas kernels for 0% -> 46%
where the time goes in v2:
time: 226 us; the launch traced here: 222 us
  Pallas kernels  172 us (76%)
  starting transfers between devices  25.4 us (11%)
  waiting for transfers between devices  19.2 us (8%)
  local copies, waits for them, and re-layouts  4.52 us (2%)
    pallas_call x3, Pallas kernels, attend(): pl.pallas_call(functools.partial(attend_kernel, tiles, len(q_arrays), len...  163 us
    all_to_all x2, waiting for transfers between devices, on_device(): got = lax.all_to_all(sent, ('z', 'y', 'kv'), 0, 0, tiled=True)  17.3 us
    all_to_all x2, starting transfers between devices, on_device(): got = lax.all_to_all(sent, ('z', 'y', 'kv'), 0, 0, tiled=True)  12.8 us
    ppermute x9, starting transfers between devices, swapped(): return lax.ppermute(x, axis, [(n, n ^ flip) for n in range(size)])  12.6 us
    pallas_call x2, Pallas kernels, combine(): pl.pallas_call(functools.partial(combine_kernel, request), grid=(1,), in_...  5.02 us
  transfers between devices with their start and end apart: 11, of which 3 were waited for; matrix products, arithmetic and copies ran while one was open for 0% of the time, Pallas kernels for 46%

profile of v2, /device:TPU:0, one launch (start us, length us, event | category | flops | bytes accessed | tf_op | source)
XLA Modules:
  0.0 222.1 jit_solution(4898214819319523822)
XLA Ops:
  0.6 0.1 collective-permute-start.1
  0.7 0.5 collective-permute-start.7
  1.2 4.1 %collective-permute-start.3 = (bf16[2,512,128]{2,1,0:T(8,128)(2,1)}, bf16[2,512,128]{2,1,0:T(8,128)(2,1)S(1)}, u32[]{:S(2)}, u32[]{:S(2)}) collective-permute-start(bf16[2,512,128]{2,1,0:T(8,128)(2,1)} %bitcast.17), channel_id=1, source_target_pairs={{0,48},{16,32},{32,16},{48,0},{1,49},{17,33},{33,17},{49,1},{2,50}... | collective-permute-start | bytes 786440 | tf_op jit(solution)/shard_map/ppermute | solution.py:380
  5.3 0.0 collective-permute-start.2
  5.4 3.2 %collective-permute-start = (bf16[2,512,128]{2,1,0:T(8,128)(2,1)}, bf16[2,512,128]{2,1,0:T(8,128)(2,1)S(1)}, u32[]{:S(2)}, u32[]{:S(2)}) collective-permute-start(bf16[2,512,128]{2,1,0:T(8,128)(2,1)} %bitcast.19), channel_id=1, source_target_pairs={{0,64},{64,0},{1,65},{65,1},{2,66},{66,2},{3,67},{67,3},{4,68},{68... | collective-permute-start | bytes 786440 | tf_op jit(solution)/shard_map/ppermute | solution.py:380
  8.5 0.0 collective-permute-done.1.vp_ref
  8.6 1.0 copy-done.1
  9.5 3.7 %shard_map.86.refs_6_.refs_9_ = bf16[2,144,4096]{2,1,0:T(8,128)(2,1)} custom-call(s32[2]{0:T(128)} %len_ref.7, bf16[2,2048,128]{2,1,0:T(8,128)(2,1)} %bitcast.16, bf16[2,2048,128]{2,1,0:T(8,128)(2,1)} %copy-done.1), custom_call_target="tpu_custom_call" | custom-call | flops 1000000 | bytes 4194304 | tf_op jit(solution)/shard_map/pallas_call | solution.py:48
  13.2 0.0 collective-permute-done.3.refs_2_
  13.2 0.4 collective-permute-done.2.refs_0_
  13.6 1.5 collective-permute-done.refs_1_
  15.1 0.0 copy-done.2
  15.1 0.1 pad_maximum_fusion
  15.2 1.6 collective-permute-start.6
  16.8 0.0 copy-done.5
  16.8 0.0 copy-done.6
  16.8 0.0 copy-start.4
  16.8 0.1 collective-permute-start.8
  16.9 2.9 %collective-permute-start.5 = (bf16[2,512,128]{2,1,0:T(8,128)(2,1)S(1)}, bf16[2,512,128]{2,1,0:T(8,128)(2,1)S(1)}, u32[]{:S(2)}, u32[]{:S(2)}) collective-permute-start(bf16[2,512,128]{2,1,0:T(8,128)(2,1)S(1)} %collective-permute-done.refs_1_), channel_id=1, source_target_pairs={{0,48},{16,32},{32,16},{48,0},{1,49},{17,33},{33,17},{49,1},{2,50}... | collective-permute-start | bytes 786440 | tf_op jit(solution)/shard_map/ppermute | solution.py:380
  19.9 0.0 collective-permute-start.4
  19.9 0.0 collective-permute-done.8.refs_5_.refs_8_
  19.9 0.0 collective-permute-done.7.refs_3_.refs_6_
  19.9 0.0 copy-done.3
  19.9 0.0 copy-done.4
  19.9 0.6 copy-done.13
  20.5 1.0 copy-done.7
  21.5 39.4 %shard_map.87 = (bf16[4,2,8,72,128]{4,3,2,1,0:T(8,128)(2,1)}, bf16[4,2,8,72,128]{4,3,2,1,0:T(8,128)(2,1)}) custom-call(s32[2]{0:T(128)} %len_ref.7, s32[2,32]{1,0:T(2,128)} %span_ref.5, bf16[2,512,128]{2,1,0:T(8,128)(2,1)} %bitcast.20, bf16[2,512,128]{2,1,0:T(8,128)(2,1)} %copy-done.3, bf16[2,2048,128]{2,1,0:T(8,128)(2,1)} %bitcast.27, ...), custom_call_target="tpu_custom_call" | custom-call | flops 4294967296 | bytes 6291456 | tf_op jit(solution)/shard_map/pallas_call | solution.py:274
  60.9 0.0 copy-done.9
  60.9 0.0 copy-done.10
  60.9 0.0 collective-permute-done.5.refs_3_
  60.9 0.0 copy-start.11
  60.9 0.0 collective-permute-done.4.refs_1_
  61.0 0.0 copy-start.12
  61.0 0.0 collective-permute-done.6.refs_4_
  61.0 0.0 copy-start.8
  61.0 0.7 copy-done.11
  61.6 0.1 copy-done.12
  61.7 0.2 copy-done.8
  61.9 66.7 %shard_map.89 = bf16[4,2,8,72,128]{4,3,2,1,0:T(8,128)(2,1)} custom-call(s32[2]{0:T(128)} %len_ref.7, s32[2,32]{1,0:T(2,128)} %span_ref.5, bf16[2,512,128]{2,1,0:T(8,128)(2,1)} %copy-done.10, bf16[2,512,128]{2,1,0:T(8,128)(2,1)} %copy-done.12, bf16[2,512,128]{2,1,0:T(8,128)(2,1)} %copy-done.9, ...), custom_call_target="tpu_custom_call", output_to_operand_aliasing={{}: (12, {})} | custom-call | flops 6442450944 | bytes 6291456 | tf_op jit(solution)/shard_map/pallas_call | solution.py:274
  128.6 6.3 %all-to-all-start.1 = ((bf16[64,72,128]{2,1,0:T(8,128)(2,1)}), bf16[64,72,128]{2,1,0:T(8,128)(2,1)S(1)}, u32[]{:S(2)}, u32[]{:S(2)}) async-start(bf16[64,72,128]{2,1,0:T(8,128)(2,1)} %bitcast.14), calls=%async_computation.1 | async-start | bytes 2359296 | tf_op jit(solution)/shard_map/all_to_all | solution.py:414
  134.9 57.0 %shard_map.88 = bf16[4,2,8,72,128]{4,3,2,1,0:T(8,128)(2,1)} custom-call(s32[2]{0:T(128)} %len_ref.7, s32[2,32]{1,0:T(2,128)} %span_ref.5, bf16[2,512,128]{2,1,0:T(8,128)(2,1)} %copy-done.10, bf16[2,512,128]{2,1,0:T(8,128)(2,1)} %copy-done.12, bf16[2,512,128]{2,1,0:T(8,128)(2,1)} %copy-done.9, ...), custom_call_target="tpu_custom_call", output_to_operand_aliasing={{}: (12, {})} | custom-call | flops 6442450944 | bytes 6291456 | tf_op jit(solution)/shard_map/pallas_call | solution.py:274
  191.9 0.0 all-to-all-done.1
  191.9 0.0 copy-start
  191.9 1.0 copy-done
  193.0 6.5 %all-to-all-start = ((bf16[64,72,128]{2,1,0:T(8,128)(2,1)}), bf16[64,72,128]{2,1,0:T(8,128)(2,1)}, u32[]{:S(2)}, u32[]{:S(2)}) async-start(bf16[64,72,128]{2,1,0:T(8,128)(2,1)} %bitcast.13), calls=%async_computation | async-start | bytes 2359296 | tf_op jit(solution)/shard_map/all_to_all | solution.py:414
  199.5 2.5 %shard_map.90 = (bf16[2,4,8,16,128]{4,3,2,1,0:T(8,128)(2,1)}, f32[2,4,128]{2,1,0:T(4,128)}) custom-call(bf16[8,8,72,128]{3,2,1,0:T(8,128)(2,1)} %bitcast.12), custom_call_target="tpu_custom_call" | custom-call | flops 10000000 | bytes 2097152 | tf_op jit(solution)/shard_map/pallas_call | solution.py:353
  202.0 17.3 %all-to-all-done = bf16[64,72,128]{2,1,0:T(8,128)(2,1)} async-done(((bf16[64,72,128]{2,1,0:T(8,128)(2,1)}), bf16[64,72,128]{2,1,0:T(8,128)(2,1)}, u32[]{:S(2)}, u32[]{:S(2)}) %all-to-all-start) | async-done | bytes 1179680 | tf_op jit(solution)/shard_map/all_to_all | solution.py:414
  219.3 2.5 %shard_map.91 = (bf16[2,4,8,16,128]{4,3,2,1,0:T(8,128)(2,1)}, f32[2,4,128]{2,1,0:T(4,128)}) custom-call(bf16[8,8,72,128]{3,2,1,0:T(8,128)(2,1)} %bitcast.8.in_ref, bf16[2,4,8,16,128]{4,3,2,1,0:T(8,128)(2,1)} %get-tuple-element.18.refs_0_, f32[2,4,128]{2,1,0:T(4,128)} %get-tuple-element.19.refs_1_), custom_call_target="tpu_custom_call", output_to_operand_aliasing={{0}: (1, {}), {1}: (2, {})} | custom-call | flops 10000000 | bytes 2097152 | tf_op jit(solution)/shard_map/pallas_call | solution.py:353
  (10 shorter events, 0.0 us)
Async XLA Ops:
  0.6 7.9 %collective-permute-start.1 = (bf16[2,2048,128]{2,1,0:T(8,128)(2,1)}, bf16[2,2048,128]{2,1,0:T(8,128)(2,1)S(1)}, u32[]{:S(2)}, u32[]{:S(2)}) collective-permute-start(bf16[2,2048,128]{2,1,0:T(8,128)(2,1)} %bitcast.15), channel_id=1, source_target_pairs={{0,8},{8,0},{1,9},{9,1},{2,10},{10,2},{3,11},{11,3},{4,12},{12,4},... | collective-permute-start | bytes 3145736 | tf_op jit(solution)/shard_map/ppermute | solution.py:380
  0.7 19.2 %collective-permute-start.7 = (bf16[2,2048,128]{2,1,0:T(8,128)(2,1)}, bf16[2,2048,128]{2,1,0:T(8,128)(2,1)S(1)}, u32[]{:S(2)}, u32[]{:S(2)}) collective-permute-start(bf16[2,2048,128]{2,1,0:T(8,128)(2,1)} %bitcast.26), channel_id=1, source_target_pairs={{0,8},{8,0},{1,9},{9,1},{2,10},{10,2},{3,11},{11,3},{4,12},{12,4},... | collective-permute-start | bytes 3145736 | tf_op jit(solution)/shard_map/ppermute | solution.py:380
  1.2 13.9 %copy-start.2 = (bf16[2,32,16,128]{3,2,1,0:T(8,128)(2,1)S(1)}, bf16[2,32,16,128]{3,2,1,0:T(8,128)(2,1)}, u32[]{:S(2)}) copy-start(bf16[2,32,16,128]{3,2,1,0:T(8,128)(2,1)} %param.7) | copy-start | bytes 786436
  1.2 15.6 %copy-start.5 = (bf16[2,32,1,128]{3,1,2,0:T(8,128)(2,1)S(1)}, bf16[2,32,1,128]{3,1,2,0:T(8,128)(2,1)}, u32[]{:S(2)}) copy-start(bf16[2,32,1,128]{3,1,2,0:T(8,128)(2,1)} %param.9) | copy-start | bytes 49156
  1.2 15.6 %copy-start.6 = (bf16[2,32,1,128]{3,1,2,0:T(8,128)(2,1)S(1)}, bf16[2,32,1,128]{3,1,2,0:T(8,128)(2,1)}, u32[]{:S(2)}) copy-start(bf16[2,32,1,128]{3,1,2,0:T(8,128)(2,1)} %param.8) | copy-start | bytes 49156
  1.2 12.0 %collective-permute-start.3 = (bf16[2,512,128]{2,1,0:T(8,128)(2,1)}, bf16[2,512,128]{2,1,0:T(8,128)(2,1)S(1)}, u32[]{:S(2)}, u32[]{:S(2)}) collective-permute-start(bf16[2,512,128]{2,1,0:T(8,128)(2,1)} %bitcast.17), channel_id=1, source_target_pairs={{0,48},{16,32},{32,16},{48,0},{1,49},{17,33},{33,17},{49,1},{2,50}... | collective-permute-start | bytes 786440 | tf_op jit(solution)/shard_map/ppermute | solution.py:380
  5.3 8.2 %collective-permute-start.2 = (bf16[2,512,128]{2,1,0:T(8,128)(2,1)}, bf16[2,512,128]{2,1,0:T(8,128)(2,1)S(1)}, u32[]{:S(2)}, u32[]{:S(2)}) collective-permute-start(bf16[2,512,128]{2,1,0:T(8,128)(2,1)} %bitcast.18), channel_id=1, source_target_pairs={{0,16},{16,0},{32,48},{48,32},{1,17},{17,1},{33,49},{49,33},{2,18}... | collective-permute-start | bytes 786440 | tf_op jit(solution)/shard_map/ppermute | solution.py:380
  5.4 9.8 %collective-permute-start = (bf16[2,512,128]{2,1,0:T(8,128)(2,1)}, bf16[2,512,128]{2,1,0:T(8,128)(2,1)S(1)}, u32[]{:S(2)}, u32[]{:S(2)}) collective-permute-start(bf16[2,512,128]{2,1,0:T(8,128)(2,1)} %bitcast.19), channel_id=1, source_target_pairs={{0,64},{64,0},{1,65},{65,1},{2,66},{66,2},{3,67},{67,3},{4,68},{68... | collective-permute-start | bytes 786440 | tf_op jit(solution)/shard_map/ppermute | solution.py:380
  8.5 1.0 copy-start.1
  13.2 47.7 %copy-start.9 = (bf16[2,512,128]{2,1,0:T(8,128)(2,1)}, bf16[2,512,128]{2,1,0:T(8,128)(2,1)S(1)}, u32[]{:S(2)}) copy-start(bf16[2,512,128]{2,1,0:T(8,128)(2,1)S(1)} %collective-permute-done.3.refs_2_) | copy-start | bytes 786436
  13.6 47.3 %copy-start.10 = (bf16[2,512,128]{2,1,0:T(8,128)(2,1)}, bf16[2,512,128]{2,1,0:T(8,128)(2,1)S(1)}, u32[]{:S(2)}) copy-start(bf16[2,512,128]{2,1,0:T(8,128)(2,1)S(1)} %collective-permute-done.2.refs_0_) | copy-start | bytes 786436
  15.1 4.8 %copy-start.3 = (bf16[2,512,128]{2,1,0:T(8,128)(2,1)}, bf16[2,512,128]{2,1,0:T(8,128)(2,1)S(1)}, u32[]{:S(2)}) copy-start(bf16[2,512,128]{2,1,0:T(8,128)(2,1)S(1)} %collective-permute-done.refs_1_) | copy-start | bytes 786436
  15.2 45.8 %collective-permute-start.6 = (bf16[2,2,512,128]{3,2,1,0:T(8,128)(2,1)S(1)}, bf16[2,2,512,128]{3,2,1,0:T(8,128)(2,1)S(1)}, u32[]{:S(2)}, u32[]{:S(2)}) collective-permute-start(bf16[2,2,512,128]{3,2,1,0:T(8,128)(2,1)S(1)} %pad_maximum_fusion), channel_id=1, source_target_pairs={{0,32},{16,48},{32,0},{48,16},{1,33},{17,49},{33,1},{49,17},{2,34}... | collective-permute-start | bytes 1572872 | tf_op jit(solution)/shard_map/ppermute | solution.py:380
  16.8 3.1 %copy-start.4 = (bf16[2,2,32,128]{3,2,1,0:T(8,128)(2,1)}, bf16[2,2,32,128]{3,2,1,0:T(8,128)(2,1)S(1)}, u32[]{:S(2)}) copy-start(bf16[2,2,32,128]{3,2,1,0:T(8,128)(2,1)S(1)} %pad_maximum_fusion.1.refs_4_.refs_7_) | copy-start | bytes 98308
  16.8 3.0 %collective-permute-start.8 = (bf16[2,2,32,128]{3,2,1,0:T(8,128)(2,1)S(1)}, bf16[2,2,32,128]{3,2,1,0:T(8,128)(2,1)S(1)}, u32[]{:S(2)}, u32[]{:S(2)}) collective-permute-start(bf16[2,2,32,128]{3,2,1,0:T(8,128)(2,1)S(1)} %pad_maximum_fusion.1.refs_4_.refs_7_), channel_id=1, source_target_pairs={{0,8},{8,0},{1,9},{9,1},{2,10},{10,2},{3,11},{11,3},{4,12},{12,4},... | collective-permute-start | bytes 98312 | tf_op jit(solution)/shard_map/ppermute | solution.py:380
  16.9 44.0 %collective-permute-start.5 = (bf16[2,512,128]{2,1,0:T(8,128)(2,1)S(1)}, bf16[2,512,128]{2,1,0:T(8,128)(2,1)S(1)}, u32[]{:S(2)}, u32[]{:S(2)}) collective-permute-start(bf16[2,512,128]{2,1,0:T(8,128)(2,1)S(1)} %collective-permute-done.refs_1_), channel_id=1, source_target_pairs={{0,48},{16,32},{32,16},{48,0},{1,49},{17,33},{33,17},{49,1},{2,50}... | collective-permute-start | bytes 786440 | tf_op jit(solution)/shard_map/ppermute | solution.py:380
  19.9 41.1 %collective-permute-start.4 = (bf16[2,512,128]{2,1,0:T(8,128)(2,1)S(1)}, bf16[2,512,128]{2,1,0:T(8,128)(2,1)S(1)}, u32[]{:S(2)}, u32[]{:S(2)}) collective-permute-start(bf16[2,512,128]{2,1,0:T(8,128)(2,1)S(1)} %collective-permute-done.refs_1_), channel_id=1, source_target_pairs={{0,16},{16,0},{32,48},{48,32},{1,17},{17,1},{33,49},{49,33},{2,18}... | collective-permute-start | bytes 786440 | tf_op jit(solution)/shard_map/ppermute | solution.py:380
  19.9 0.6 copy-start.13
  20.5 1.0 copy-start.7
  60.9 0.7 copy-start.11
  61.0 0.8 copy-start.12
  61.0 0.9 copy-start.8
  128.6 63.3 %all-to-all-start.1 = ((bf16[64,72,128]{2,1,0:T(8,128)(2,1)}), bf16[64,72,128]{2,1,0:T(8,128)(2,1)S(1)}, u32[]{:S(2)}, u32[]{:S(2)}) async-start(bf16[64,72,128]{2,1,0:T(8,128)(2,1)} %bitcast.14), calls=%async_computation.1 | async-start | bytes 2359296 | tf_op jit(solution)/shard_map/all_to_all | solution.py:414
  191.9 1.0 copy-start
  193.0 26.3 %all-to-all-start = ((bf16[64,72,128]{2,1,0:T(8,128)(2,1)}), bf16[64,72,128]{2,1,0:T(8,128)(2,1)}, u32[]{:S(2)}, u32[]{:S(2)}) async-start(bf16[64,72,128]{2,1,0:T(8,128)(2,1)} %bitcast.13), calls=%async_computation | async-start | bytes 2359296 | tf_op jit(solution)/shard_map/all_to_all | solution.py:414

commit v3 on v2

--- a/solution.py
+++ b/solution.py
@@ -65,7 +65,7 @@
     first_out = n_q + 5 + n_aliased
     out_refs = refs[first_out : first_out + n_out]
     scratch = refs[first_out + n_out :]
-    ko_ref, kp_ref, no_ref, np_ref, vt_ref, q_buf, acc_ref, top_ref, stage, sem, in_sem = scratch
+    ko_ref, kp_ref, no_ref, np_ref, vt_ref, q_buf, acc_ref, top_ref, stage, sem, in_sem, q_sem = scratch
     requests = sorted({tile[0] for tile in tiles})
     lowest = requests[0]
     rows = ko_ref.shape[1]
@@ -76,10 +76,13 @@
         loads[name] = pltpu.make_async_copy(source, target, in_sem.at[len(loads)])
         loads[name].start()
 
+    def fetch(request, t, half, source=0, part=None):
+        array = inputs[source] if part is None else inputs[source].at[part]
+        return pltpu.make_async_copy(array.at[request], q_buf.at[t, half], q_sem.at[2 * t + half])
+
     def load_q(t):
         for half, (source, part) in enumerate(tiles[t][2]):
-            array = inputs[source] if part is None else inputs[source].at[part]
-            load(("q", t, half), array.at[tiles[t][0]], q_buf.at[t, half])
+            fetch(tiles[t][0], t, half, source, part).start()
 
     def load_v(n):
         for r in requests:
@@ -99,14 +102,6 @@
     load_k("np", 3, np_ref)
     for t in range(1, len(tiles)):
         load_q(t)
-    arrived = set()
-
-    def need(*names):
-        for name in names:
-            if name not in arrived:
-                arrived.add(name)
-                loads[name].wait()
-
     me, core, my_y, my_z, _ = my_place()
     partner = me + 1 - 2 * core
     n_new = 2 * no_ref.shape[2]
@@ -189,31 +184,31 @@
                 start = n * block + owner * share // 128 * 128
                 stage[t, place, owner, share:, :] = logs[:, start : start + 128]
 
-    worst = jnp.ones((1, width), jnp.int32)
-    for t, (request, hop, source) in enumerate(tiles):
+    for r in requests:
+        for name, n in (("ko", 0), ("v", 0), ("kp", 0), ("v", 1), ("no", 0), ("np", 0)):
+            loads[name, n, r].wait()
+
+    def whole_tile(t, worst):
+        request = of_tile(t, 0)
         at = request - lowest
-        need(("q", t, 0), ("q", t, 1), ("ko", 0, request))
+        for half in range(2):
+            fetch(0, t, half).wait()
         q = q_buf[t].reshape(width, 128)
-        p = jnp.exp2(dot_nt(ko_ref[at], q) * scale)
-        need(("v", 0, request))
-        acc = values(request, p, 0, rows)
-        need(("kp", 0, request), ("v", 1, request))
+        acc = values(request, jnp.exp2(dot_nt(ko_ref[at], q) * scale), 0, rows)
         acc = acc + values(request, jnp.exp2(dot_nt(kp_ref[at], q) * scale), rows, rows)
-        need(("no", 0, request), ("np", 0, request))
         shown, has_key = new_visible(t)
         s_new = jnp.where(shown, dot_nt(new_keys(at), q) * scale, MASKED)
         acc = acc + new_values(at, jnp.exp2(s_new))
         total = acc[128:129, :]
         fine = (total < SUM_HIGH) & ((total > SUM_LOW) | jnp.logical_not(has_key))
-        worst = jnp.minimum(worst, jnp.where(fine, 1, 0))
         finish(t, acc, jnp.zeros((1, width), jnp.float32))
-        send(t, request, hop).start()
+        return jnp.minimum(worst, jnp.where(fine, 1, 0))
+
+    worst = lax.fori_loop(0, len(tiles), whole_tile, jnp.ones((1, width), jnp.int32))
 
     @pl.when(jnp.min(worst) == 0)
     def _():
         part = 256
-        for t, (request, hop, _) in enumerate(tiles):
-            send(t, request, hop).wait()
 
         def again(t, carry):
             request = of_tile(t, 0)
@@ -254,9 +249,9 @@
             return carry
 
         lax.fori_loop(0, len(tiles), again, 0)
-        for t, (request, hop, _) in enumerate(tiles):
-            send(t, request, hop).start()
-
+
+    for t, (request, hop, _) in enumerate(tiles):
+        send(t, request, hop).start()
     for t, (request, hop, _) in enumerate(tiles):
         send(t, request, hop).wait()
 
@@ -283,7 +278,8 @@
             pltpu.VMEM((8, width), jnp.float32),
             pltpu.VMEM((len(tiles), 2, owners, share + 8, 128), jnp.bfloat16),
             pltpu.SemaphoreType.DMA((len(tiles),)),
-            pltpu.SemaphoreType.DMA((len(requests) * 6 + 2 * len(tiles),)),
+            pltpu.SemaphoreType.DMA((len(requests) * 6,)),
+            pltpu.SemaphoreType.DMA((2 * len(tiles),)),
         ],
         out_shape=[result] * len(requests),
         input_output_aliases={2 + n_in + n: n for n in range(len(partials))},

time: 226 us -> 212 us (0.938); the launches traced: 222 us -> 211 us
  Pallas kernels: 172 us -> 161 us
    pallas_call x3, Pallas kernels: 163 us -> 152 us  [attend(): pl.pallas_call(functools.partial(attend_kernel, tiles, len(q_arrays), len...]
  transfers between devices with their start and end apart: 11 -> 11, of which waited for: 3 -> 3; matrix products, arithmetic and copies ran while one was open for 0% -> 0% of each run, Pallas kernels for 46% -> 48%
where the time goes in v3:
time: 212 us; the launch traced here: 211 us
  Pallas kernels  161 us (76%)
  starting transfers between devices  25.4 us (12%)
  waiting for transfers between devices  19.2 us (9%)
  local copies, waits for them, and re-layouts  4.52 us (2%)
    pallas_call x3, Pallas kernels, attend(): pl.pallas_call(functools.partial(attend_kernel, tiles, len(q_arrays), len...  152 us
    all_to_all x2, waiting for transfers between devices, on_device(): got = lax.all_to_all(sent, ('z', 'y', 'kv'), 0, 0, tiled=True)  17.3 us
    all_to_all x2, starting transfers between devices, on_device(): got = lax.all_to_all(sent, ('z', 'y', 'kv'), 0, 0, tiled=True)  12.8 us
    ppermute x9, starting transfers between devices, swapped(): return lax.ppermute(x, axis, [(n, n ^ flip) for n in range(size)])  12.6 us
    pallas_call x2, Pallas kernels, combine(): pl.pallas_call(functools.partial(combine_kernel, request), grid=(1,), in_...  5.02 us
    unnamed x28, local copies, waits for them, and re-layouts  4.52 us
  transfers between devices with their start and end apart: 11, of which 3 were waited for; matrix products, arithmetic and copies ran while one was open for 0% of the time, Pallas kernels for 48%

profile of v3, /device:TPU:0, one launch (start us, length us, event | category | flops | bytes accessed | tf_op | source)
XLA Modules:
  0.0 211.3 jit_solution(1650578817675580303)
XLA Ops:
  0.6 0.1 collective-permute-start.1
  0.7 0.5 collective-permute-start.7
  1.2 4.1 %collective-permute-start.3 = (bf16[2,512,128]{2,1,0:T(8,128)(2,1)}, bf16[2,512,128]{2,1,0:T(8,128)(2,1)S(1)}, u32[]{:S(2)}, u32[]{:S(2)}) collective-permute-start(bf16[2,512,128]{2,1,0:T(8,128)(2,1)} %bitcast.17), channel_id=1, source_target_pairs={{0,48},{16,32},{32,16},{48,0},{1,49},{17,33},{33,17},{49,1},{2,50}... | collective-permute-start | bytes 786440 | tf_op jit(solution)/shard_map/ppermute | solution.py:376
  5.3 0.0 collective-permute-start.2
  5.4 3.2 %collective-permute-start = (bf16[2,512,128]{2,1,0:T(8,128)(2,1)}, bf16[2,512,128]{2,1,0:T(8,128)(2,1)S(1)}, u32[]{:S(2)}, u32[]{:S(2)}) collective-permute-start(bf16[2,512,128]{2,1,0:T(8,128)(2,1)} %bitcast.19), channel_id=1, source_target_pairs={{0,64},{64,0},{1,65},{65,1},{2,66},{66,2},{3,67},{67,3},{4,68},{68... | collective-permute-start | bytes 786440 | tf_op jit(solution)/shard_map/ppermute | solution.py:376
  8.5 0.0 collective-permute-done.1.vp_ref
  8.6 1.0 copy-done.1
  9.5 3.7 %shard_map.86.refs_6_.refs_9_ = bf16[2,144,4096]{2,1,0:T(8,128)(2,1)} custom-call(s32[2]{0:T(128)} %len_ref.7, bf16[2,2048,128]{2,1,0:T(8,128)(2,1)} %bitcast.16, bf16[2,2048,128]{2,1,0:T(8,128)(2,1)} %copy-done.1), custom_call_target="tpu_custom_call" | custom-call | flops 1000000 | bytes 4194304 | tf_op jit(solution)/shard_map/pallas_call | solution.py:48
  13.2 0.0 collective-permute-done.3.refs_2_
  13.2 0.4 collective-permute-done.2.refs_0_
  13.6 1.5 collective-permute-done.refs_1_
  15.1 0.0 copy-done.2
  15.1 0.1 pad_maximum_fusion
  15.2 1.6 collective-permute-start.6
  16.8 0.0 copy-done.5
  16.8 0.0 copy-done.6
  16.8 0.0 copy-start.4
  16.8 0.1 collective-permute-start.8
  16.9 2.9 %collective-permute-start.5 = (bf16[2,512,128]{2,1,0:T(8,128)(2,1)S(1)}, bf16[2,512,128]{2,1,0:T(8,128)(2,1)S(1)}, u32[]{:S(2)}, u32[]{:S(2)}) collective-permute-start(bf16[2,512,128]{2,1,0:T(8,128)(2,1)S(1)} %collective-permute-done.refs_1_), channel_id=1, source_target_pairs={{0,48},{16,32},{32,16},{48,0},{1,49},{17,33},{33,17},{49,1},{2,50}... | collective-permute-start | bytes 786440 | tf_op jit(solution)/shard_map/ppermute | solution.py:376
  19.9 0.0 collective-permute-start.4
  19.9 0.0 collective-permute-done.8.refs_5_.refs_8_
  19.9 0.0 collective-permute-done.7.refs_3_.refs_6_
  19.9 0.0 copy-done.3
  19.9 0.0 copy-done.4
  19.9 0.6 copy-done.13
  20.5 1.0 copy-done.7
  21.5 39.5 %shard_map.87 = (bf16[4,2,8,72,128]{4,3,2,1,0:T(8,128)(2,1)}, bf16[4,2,8,72,128]{4,3,2,1,0:T(8,128)(2,1)}) custom-call(s32[2]{0:T(128)} %len_ref.7, s32[2,32]{1,0:T(2,128)} %span_ref.5, bf16[2,512,128]{2,1,0:T(8,128)(2,1)} %bitcast.20, bf16[2,512,128]{2,1,0:T(8,128)(2,1)} %copy-done.3, bf16[2,2048,128]{2,1,0:T(8,128)(2,1)} %bitcast.27, ...), custom_call_target="tpu_custom_call" | custom-call | flops 4294967296 | bytes 6291456 | tf_op jit(solution)/shard_map/pallas_call | solution.py:269
  61.0 0.0 copy-done.9
  61.0 0.0 copy-done.10
  61.0 0.0 collective-permute-done.5.refs_3_
  61.0 0.0 copy-start.11
  61.1 0.0 collective-permute-done.4.refs_1_
  61.1 0.0 copy-start.12
  61.1 0.0 collective-permute-done.6.refs_4_
  61.1 0.0 copy-start.8
  61.1 0.7 copy-done.11
  61.8 0.1 copy-done.12
  61.8 0.2 copy-done.8
  62.0 56.4 %shard_map.89 = bf16[4,2,8,72,128]{4,3,2,1,0:T(8,128)(2,1)} custom-call(s32[2]{0:T(128)} %len_ref.7, s32[2,32]{1,0:T(2,128)} %span_ref.5, bf16[2,512,128]{2,1,0:T(8,128)(2,1)} %copy-done.10, bf16[2,512,128]{2,1,0:T(8,128)(2,1)} %copy-done.12, bf16[2,512,128]{2,1,0:T(8,128)(2,1)} %copy-done.9, ...), custom_call_target="tpu_custom_call", output_to_operand_aliasing={{}: (12, {})} | custom-call | flops 6442450944 | bytes 6291456 | tf_op jit(solution)/shard_map/pallas_call | solution.py:269
  118.5 6.3 %all-to-all-start.1 = ((bf16[64,72,128]{2,1,0:T(8,128)(2,1)}), bf16[64,72,128]{2,1,0:T(8,128)(2,1)S(1)}, u32[]{:S(2)}, u32[]{:S(2)}) async-start(bf16[64,72,128]{2,1,0:T(8,128)(2,1)} %bitcast.14), calls=%async_computation.1 | async-start | bytes 2359296 | tf_op jit(solution)/shard_map/all_to_all | solution.py:410
  124.8 56.4 %shard_map.88 = bf16[4,2,8,72,128]{4,3,2,1,0:T(8,128)(2,1)} custom-call(s32[2]{0:T(128)} %len_ref.7, s32[2,32]{1,0:T(2,128)} %span_ref.5, bf16[2,512,128]{2,1,0:T(8,128)(2,1)} %copy-done.10, bf16[2,512,128]{2,1,0:T(8,128)(2,1)} %copy-done.12, bf16[2,512,128]{2,1,0:T(8,128)(2,1)} %copy-done.9, ...), custom_call_target="tpu_custom_call", output_to_operand_aliasing={{}: (12, {})} | custom-call | flops 6442450944 | bytes 6291456 | tf_op jit(solution)/shard_map/pallas_call | solution.py:269
  181.2 0.0 all-to-all-done.1
  181.3 0.0 copy-start
  181.3 1.0 copy-done
  182.3 6.5 %all-to-all-start = ((bf16[64,72,128]{2,1,0:T(8,128)(2,1)}), bf16[64,72,128]{2,1,0:T(8,128)(2,1)}, u32[]{:S(2)}, u32[]{:S(2)}) async-start(bf16[64,72,128]{2,1,0:T(8,128)(2,1)} %bitcast.13), calls=%async_computation | async-start | bytes 2359296 | tf_op jit(solution)/shard_map/all_to_all | solution.py:410
  188.8 2.5 %shard_map.90 = (bf16[2,4,8,16,128]{4,3,2,1,0:T(8,128)(2,1)}, f32[2,4,128]{2,1,0:T(4,128)}) custom-call(bf16[8,8,72,128]{3,2,1,0:T(8,128)(2,1)} %bitcast.12), custom_call_target="tpu_custom_call" | custom-call | flops 10000000 | bytes 2097152 | tf_op jit(solution)/shard_map/pallas_call | solution.py:349
  191.3 17.3 %all-to-all-done = bf16[64,72,128]{2,1,0:T(8,128)(2,1)} async-done(((bf16[64,72,128]{2,1,0:T(8,128)(2,1)}), bf16[64,72,128]{2,1,0:T(8,128)(2,1)}, u32[]{:S(2)}, u32[]{:S(2)}) %all-to-all-start) | async-done | bytes 1179680 | tf_op jit(solution)/shard_map/all_to_all | solution.py:410
  208.6 2.5 %shard_map.91 = (bf16[2,4,8,16,128]{4,3,2,1,0:T(8,128)(2,1)}, f32[2,4,128]{2,1,0:T(4,128)}) custom-call(bf16[8,8,72,128]{3,2,1,0:T(8,128)(2,1)} %bitcast.8.in_ref, bf16[2,4,8,16,128]{4,3,2,1,0:T(8,128)(2,1)} %get-tuple-element.18.refs_0_, f32[2,4,128]{2,1,0:T(4,128)} %get-tuple-element.19.refs_1_), custom_call_target="tpu_custom_call", output_to_operand_aliasing={{0}: (1, {}), {1}: (2, {})} | custom-call | flops 10000000 | bytes 2097152 | tf_op jit(solution)/shard_map/pallas_call | solution.py:349
  (10 shorter events, 0.0 us)
Async XLA Ops:
  0.6 7.9 %collective-permute-start.1 = (bf16[2,2048,128]{2,1,0:T(8,128)(2,1)}, bf16[2,2048,128]{2,1,0:T(8,128)(2,1)S(1)}, u32[]{:S(2)}, u32[]{:S(2)}) collective-permute-start(bf16[2,2048,128]{2,1,0:T(8,128)(2,1)} %bitcast.15), channel_id=1, source_target_pairs={{0,8},{8,0},{1,9},{9,1},{2,10},{10,2},{3,11},{11,3},{4,12},{12,4},... | collective-permute-start | bytes 3145736 | tf_op jit(solution)/shard_map/ppermute | solution.py:376
  0.7 19.2 %collective-permute-start.7 = (bf16[2,2048,128]{2,1,0:T(8,128)(2,1)}, bf16[2,2048,128]{2,1,0:T(8,128)(2,1)S(1)}, u32[]{:S(2)}, u32[]{:S(2)}) collective-permute-start(bf16[2,2048,128]{2,1,0:T(8,128)(2,1)} %bitcast.26), channel_id=1, source_target_pairs={{0,8},{8,0},{1,9},{9,1},{2,10},{10,2},{3,11},{11,3},{4,12},{12,4},... | collective-permute-start | bytes 3145736 | tf_op jit(solution)/shard_map/ppermute | solution.py:376
  1.2 13.9 %copy-start.2 = (bf16[2,32,16,128]{3,2,1,0:T(8,128)(2,1)S(1)}, bf16[2,32,16,128]{3,2,1,0:T(8,128)(2,1)}, u32[]{:S(2)}) copy-start(bf16[2,32,16,128]{3,2,1,0:T(8,128)(2,1)} %param.7) | copy-start | bytes 786436
  1.2 15.6 %copy-start.5 = (bf16[2,32,1,128]{3,1,2,0:T(8,128)(2,1)S(1)}, bf16[2,32,1,128]{3,1,2,0:T(8,128)(2,1)}, u32[]{:S(2)}) copy-start(bf16[2,32,1,128]{3,1,2,0:T(8,128)(2,1)} %param.9) | copy-start | bytes 49156
  1.2 15.6 %copy-start.6 = (bf16[2,32,1,128]{3,1,2,0:T(8,128)(2,1)S(1)}, bf16[2,32,1,128]{3,1,2,0:T(8,128)(2,1)}, u32[]{:S(2)}) copy-start(bf16[2,32,1,128]{3,1,2,0:T(8,128)(2,1)} %param.8) | copy-start | bytes 49156
  1.2 12.0 %collective-permute-start.3 = (bf16[2,512,128]{2,1,0:T(8,128)(2,1)}, bf16[2,512,128]{2,1,0:T(8,128)(2,1)S(1)}, u32[]{:S(2)}, u32[]{:S(2)}) collective-permute-start(bf16[2,512,128]{2,1,0:T(8,128)(2,1)} %bitcast.17), channel_id=1, source_target_pairs={{0,48},{16,32},{32,16},{48,0},{1,49},{17,33},{33,17},{49,1},{2,50}... | collective-permute-start | bytes 786440 | tf_op jit(solution)/shard_map/ppermute | solution.py:376
  5.3 8.2 %collective-permute-start.2 = (bf16[2,512,128]{2,1,0:T(8,128)(2,1)}, bf16[2,512,128]{2,1,0:T(8,128)(2,1)S(1)}, u32[]{:S(2)}, u32[]{:S(2)}) collective-permute-start(bf16[2,512,128]{2,1,0:T(8,128)(2,1)} %bitcast.18), channel_id=1, source_target_pairs={{0,16},{16,0},{32,48},{48,32},{1,17},{17,1},{33,49},{49,33},{2,18}... | collective-permute-start | bytes 786440 | tf_op jit(solution)/shard_map/ppermute | solution.py:376
  5.4 9.8 %collective-permute-start = (bf16[2,512,128]{2,1,0:T(8,128)(2,1)}, bf16[2,512,128]{2,1,0:T(8,128)(2,1)S(1)}, u32[]{:S(2)}, u32[]{:S(2)}) collective-permute-start(bf16[2,512,128]{2,1,0:T(8,128)(2,1)} %bitcast.19), channel_id=1, source_target_pairs={{0,64},{64,0},{1,65},{65,1},{2,66},{66,2},{3,67},{67,3},{4,68},{68... | collective-permute-start | bytes 786440 | tf_op jit(solution)/shard_map/ppermute | solution.py:376
  8.5 1.0 copy-start.1
  13.2 47.8 %copy-start.9 = (bf16[2,512,128]{2,1,0:T(8,128)(2,1)}, bf16[2,512,128]{2,1,0:T(8,128)(2,1)S(1)}, u32[]{:S(2)}) copy-start(bf16[2,512,128]{2,1,0:T(8,128)(2,1)S(1)} %collective-permute-done.3.refs_2_) | copy-start | bytes 786436
  13.6 47.4 %copy-start.10 = (bf16[2,512,128]{2,1,0:T(8,128)(2,1)}, bf16[2,512,128]{2,1,0:T(8,128)(2,1)S(1)}, u32[]{:S(2)}) copy-start(bf16[2,512,128]{2,1,0:T(8,128)(2,1)S(1)} %collective-permute-done.2.refs_0_) | copy-start | bytes 786436
  15.1 4.8 %copy-start.3 = (bf16[2,512,128]{2,1,0:T(8,128)(2,1)}, bf16[2,512,128]{2,1,0:T(8,128)(2,1)S(1)}, u32[]{:S(2)}) copy-start(bf16[2,512,128]{2,1,0:T(8,128)(2,1)S(1)} %collective-permute-done.refs_1_) | copy-start | bytes 786436
  15.2 45.9 %collective-permute-start.6 = (bf16[2,2,512,128]{3,2,1,0:T(8,128)(2,1)S(1)}, bf16[2,2,512,128]{3,2,1,0:T(8,128)(2,1)S(1)}, u32[]{:S(2)}, u32[]{:S(2)}) collective-permute-start(bf16[2,2,512,128]{3,2,1,0:T(8,128)(2,1)S(1)} %pad_maximum_fusion), channel_id=1, source_target_pairs={{0,32},{16,48},{32,0},{48,16},{1,33},{17,49},{33,1},{49,17},{2,34}... | collective-permute-start | bytes 1572872 | tf_op jit(solution)/shard_map/ppermute | solution.py:376
  16.8 3.1 %copy-start.4 = (bf16[2,2,32,128]{3,2,1,0:T(8,128)(2,1)}, bf16[2,2,32,128]{3,2,1,0:T(8,128)(2,1)S(1)}, u32[]{:S(2)}) copy-start(bf16[2,2,32,128]{3,2,1,0:T(8,128)(2,1)S(1)} %pad_maximum_fusion.1.refs_4_.refs_7_) | copy-start | bytes 98308
  16.8 3.0 %collective-permute-start.8 = (bf16[2,2,32,128]{3,2,1,0:T(8,128)(2,1)S(1)}, bf16[2,2,32,128]{3,2,1,0:T(8,128)(2,1)S(1)}, u32[]{:S(2)}, u32[]{:S(2)}) collective-permute-start(bf16[2,2,32,128]{3,2,1,0:T(8,128)(2,1)S(1)} %pad_maximum_fusion.1.refs_4_.refs_7_), channel_id=1, source_target_pairs={{0,8},{8,0},{1,9},{9,1},{2,10},{10,2},{3,11},{11,3},{4,12},{12,4},... | collective-permute-start | bytes 98312 | tf_op jit(solution)/shard_map/ppermute | solution.py:376
  16.9 44.1 %collective-permute-start.5 = (bf16[2,512,128]{2,1,0:T(8,128)(2,1)S(1)}, bf16[2,512,128]{2,1,0:T(8,128)(2,1)S(1)}, u32[]{:S(2)}, u32[]{:S(2)}) collective-permute-start(bf16[2,512,128]{2,1,0:T(8,128)(2,1)S(1)} %collective-permute-done.refs_1_), channel_id=1, source_target_pairs={{0,48},{16,32},{32,16},{48,0},{1,49},{17,33},{33,17},{49,1},{2,50}... | collective-permute-start | bytes 786440 | tf_op jit(solution)/shard_map/ppermute | solution.py:376
  19.9 41.2 %collective-permute-start.4 = (bf16[2,512,128]{2,1,0:T(8,128)(2,1)S(1)}, bf16[2,512,128]{2,1,0:T(8,128)(2,1)S(1)}, u32[]{:S(2)}, u32[]{:S(2)}) collective-permute-start(bf16[2,512,128]{2,1,0:T(8,128)(2,1)S(1)} %collective-permute-done.refs_1_), channel_id=1, source_target_pairs={{0,16},{16,0},{32,48},{48,32},{1,17},{17,1},{33,49},{49,33},{2,18}... | collective-permute-start | bytes 786440 | tf_op jit(solution)/shard_map/ppermute | solution.py:376
  19.9 0.6 copy-start.13
  20.5 1.0 copy-start.7
  61.0 0.7 copy-start.11
  61.1 0.8 copy-start.12
  61.1 0.9 copy-start.8
  118.5 62.8 %all-to-all-start.1 = ((bf16[64,72,128]{2,1,0:T(8,128)(2,1)}), bf16[64,72,128]{2,1,0:T(8,128)(2,1)S(1)}, u32[]{:S(2)}, u32[]{:S(2)}) async-start(bf16[64,72,128]{2,1,0:T(8,128)(2,1)} %bitcast.14), calls=%async_computation.1 | async-start | bytes 2359296 | tf_op jit(solution)/shard_map/all_to_all | solution.py:410
  181.3 1.0 copy-start
  182.3 26.3 %all-to-all-start = ((bf16[64,72,128]{2,1,0:T(8,128)(2,1)}), bf16[64,72,128]{2,1,0:T(8,128)(2,1)}, u32[]{:S(2)}, u32[]{:S(2)}) async-start(bf16[64,72,128]{2,1,0:T(8,128)(2,1)} %bitcast.13), calls=%async_computation | async-start | bytes 2359296 | tf_op jit(solution)/shard_map/all_to_all | solution.py:410

commit v4 on v3

--- a/solution.py
+++ b/solution.py
@@ -65,7 +65,8 @@
     first_out = n_q + 5 + n_aliased
     out_refs = refs[first_out : first_out + n_out]
     scratch = refs[first_out + n_out :]
-    ko_ref, kp_ref, no_ref, np_ref, vt_ref, q_buf, acc_ref, top_ref, stage, sem, in_sem, q_sem = scratch
+    ko_ref, kp_ref, no_ref, np_ref, vt_ref = scratch[:5]
+    q_buf, acc_ref, top_ref, stage, sem, in_sem, q_sem = scratch[5:]
     requests = sorted({tile[0] for tile in tiles})
     lowest = requests[0]
     rows = ko_ref.shape[1]
@@ -81,25 +82,20 @@
         return pltpu.make_async_copy(array.at[request], q_buf.at[t, half], q_sem.at[2 * t + half])
 
     def load_q(t):
-        for half, (source, part) in enumerate(tiles[t][2]):
+        for half in range(2):
+            source, part = tiles[t][1 + half][2:]
             fetch(tiles[t][0], t, half, source, part).start()
 
-    def load_v(n):
-        for r in requests:
+    load_q(0)
+    for r in requests:
+        at = r - lowest
+        load(("ko", 0, r), inputs[n_q].at[r], ko_ref.at[at])
+        for n in range(2):
             part = pl.ds(n * rows, rows)
-            load(("v", n, r), inputs[n_q + 4].at[r, :, part], vt_ref.at[r - lowest, :, part])
-
-    def load_k(name, index, ref):
-        for r in requests:
-            load((name, 0, r), inputs[n_q + index].at[r], ref.at[r - lowest])
-
-    load_q(0)
-    load_k("ko", 0, ko_ref)
-    load_v(0)
-    load_k("kp", 1, kp_ref)
-    load_v(1)
-    load_k("no", 2, no_ref)
-    load_k("np", 3, np_ref)
+            load(("v", n, r), inputs[n_q + 4].at[r, :, part], vt_ref.at[at, :, part])
+        load(("kp", 0, r), inputs[n_q + 1].at[r], kp_ref.at[at])
+        load(("no", 0, r), inputs[n_q + 2].at[r], no_ref.at[at])
+        load(("np", 0, r), inputs[n_q + 3].at[r], np_ref.at[at])
     for t in range(1, len(tiles)):
         load_q(t)
     me, core, my_y, my_z, _ = my_place()
@@ -109,23 +105,26 @@
     width = 2 * block
     scale = LOG2E * 128**-0.5
 
-    def of_tile(t, field):
-        if isinstance(t, int):
-            return tiles[t][field]
-        value = jnp.int32(tiles[0][field])
+    def of_tile(t, choose):
+        value = jnp.int32(choose(tiles[0]))
         for n in range(1, len(tiles)):
-            value = jnp.where(t == n, jnp.int32(tiles[n][field]), value)
+            value = jnp.where(t == n, jnp.int32(choose(tiles[n])), value)
         return value
 
+    def request_of(t):
+        return of_tile(t, lambda tile: tile[0])
+
     def new_visible(t):
-        request, hop = of_tile(t, 0), of_tile(t, 1)
+        request = request_of(t)
         lane = lax.broadcasted_iota(jnp.int32, (1, width), 1)
         key = lax.broadcasted_iota(jnp.int32, (n_new, 1), 0)
         q_span = jnp.zeros((1, width), jnp.int32)
         k_span = jnp.zeros((n_new, 1), jnp.int32)
         first = jnp.int32(1 << 30)
         for n in range(4):
-            source = 2 * ((my_y ^ (n // 2)) * 4 + (my_z ^ hop)) + core
+            hop_z = of_tile(t, lambda tile: tile[1 + n // 2][0])
+            hop_y = of_tile(t, lambda tile: tile[1 + n // 2][1])
+            source = 2 * ((my_y ^ hop_y) * 4 + (my_z ^ hop_z)) + core
             chosen = span_ref[request, 2 * source + n % 2]
             q_span = jnp.where(lane // (block // 2) == n, chosen, q_span)
             held = span_ref[request, 2 * (me if n < 2 else partner) + n % 2]
@@ -156,9 +155,11 @@
             turned[:, :n_new], p.astype(jnp.bfloat16), preferred_element_type=jnp.float32
         )
 
-    def send(t, request, hop):
-        place = out_refs[request - lowest].at[my_z ^ hop]
-        return pltpu.make_async_copy(stage.at[t], place, sem.at[t])
+    def sends():
+        for t, (request, *halves) in enumerate(tiles):
+            for half, (hop_z, hop_y, _, _) in enumerate(halves):
+                place = out_refs[request - lowest].at[my_z ^ hop_z, my_y ^ hop_y]
+                yield pltpu.make_async_copy(stage.at[t, half], place, sem.at[2 * t + half])
 
     def finish(t, acc, top):
         total = acc[128:129, :]
@@ -176,21 +177,23 @@
         owners = stage.shape[2]
         share = block // owners
         for n in range(2):
-            place = my_y ^ n
-            stage[t, place, :, :share, :] = outputs[n * block : (n + 1) * block].reshape(
+            stage[t, n, :, :share, :] = outputs[n * block : (n + 1) * block].reshape(
                 owners, share, 128
             )
             for owner in range(owners):
                 start = n * block + owner * share // 128 * 128
-                stage[t, place, owner, share:, :] = logs[:, start : start + 128]
-
-    for r in requests:
-        for name, n in (("ko", 0), ("v", 0), ("kp", 0), ("v", 1), ("no", 0), ("np", 0)):
-            loads[name, n, r].wait()
+                stage[t, n, owner, share:, :] = logs[:, start : start + 128]
 
     def whole_tile(t, worst):
-        request = of_tile(t, 0)
+        request = request_of(t)
         at = request - lowest
+        for r in requests:
+
+            @pl.when(t == [tile[0] for tile in tiles].index(r))
+            def _(r=r):
+                for name, n in (("ko", 0), ("v", 0), ("kp", 0), ("v", 1), ("no", 0), ("np", 0)):
+                    loads[name, n, r].wait()
+
         for half in range(2):
             fetch(0, t, half).wait()
         q = q_buf[t].reshape(width, 128)
@@ -211,7 +214,7 @@
         part = 256
 
         def again(t, carry):
-            request = of_tile(t, 0)
+            request = request_of(t)
             q = q_buf[t].reshape(width, 128)
             shown, _ = new_visible(t)
             s_new = jnp.where(shown, dot_nt(new_keys(request - lowest), q) * scale, MASKED)
@@ -250,10 +253,10 @@
 
         lax.fori_loop(0, len(tiles), again, 0)
 
-    for t, (request, hop, _) in enumerate(tiles):
-        send(t, request, hop).start()
-    for t, (request, hop, _) in enumerate(tiles):
-        send(t, request, hop).wait()
+    for copy in sends():
+        copy.start()
+    for copy in sends():
+        copy.wait()
 
 
 def attend(tiles, cached_len, span_order, q_arrays, k_own, k_par, n_own, n_par, vt, partials):
@@ -277,7 +280,7 @@
             pltpu.VMEM((144, width), jnp.float32),
             pltpu.VMEM((8, width), jnp.float32),
             pltpu.VMEM((len(tiles), 2, owners, share + 8, 128), jnp.bfloat16),
-            pltpu.SemaphoreType.DMA((len(tiles),)),
+            pltpu.SemaphoreType.DMA((2 * len(tiles),)),
             pltpu.SemaphoreType.DMA((len(requests) * 6,)),
             pltpu.SemaphoreType.DMA((2 * len(tiles),)),
         ],
@@ -363,7 +366,7 @@
             jax.ShapeDtypeStruct((requests, tokens, groups * 16), jnp.float32),
         ],
         input_output_aliases={1 + n: n for n in range(len(earlier))},
-        compiler_params=pltpu.CompilerParams(vmem_limit_bytes=63 << 20),
+        compiler_params=pltpu.CompilerParams(vmem_limit_bytes=24 << 20),
         cost_estimate=pl.CostEstimate(flops=10**7, bytes_accessed=2 << 20, transcendentals=0),
     )(parts, *earlier)
 
@@ -393,19 +396,31 @@
 
     common = (cached_len, span_order)
     keys = (k_own, k_par, n_own, n_par, vt)
-    here = ((0, None), (1, None))
-    partials = attend(
-        tuple((r, 0, here) for r in range(requests)), *common, [q_own, q_other], *keys, []
+    blocks = {(0, 0): 0, (0, 1): 1, (1, 0): 2, (3, 0): 3, (1, 1): 4, (3, 1): 5}
+    arrays = [q_own, q_other, *near, *next_to, far]
+
+    def tile(r, a, b):
+        def half(place):
+            return place + ((6, place[1]) if place[0] == 2 else (blocks[place], None))
+
+        return (r, half(a), half(b))
+
+    here, by_own, by_other, last = (
+        ((0, 0), (0, 1)),
+        ((1, 0), (3, 0)),
+        ((1, 1), (3, 1)),
+        ((2, 0), (2, 1)),
     )
-    hops = [near[0], next_to[0], near[1], next_to[1], far]
+    plan = (
+        ((0, here), (0, by_own), (1, here)),
+        ((0, by_other), (0, last)),
+        ((1, by_own), (1, by_other), (1, last)),
+    )
+    plan = [tuple(tile(r, *pair) for r, pair in call) for call in plan]
+    partials = attend(plan[0], *common, arrays[:4], *keys, [])
     received = []
     for r in range(requests):
-        tiles = (
-            (r, 1, ((0, None), (1, None))),
-            (r, 3, ((2, None), (3, None))),
-            (r, 2, ((4, 0), (4, 1))),
-        )
-        (parts,) = attend(tiles, *common, hops, *keys, [partials[r]])
+        (parts,) = attend(plan[1 + r], *common, arrays, *keys, [partials[r]])
         sent = parts.reshape((64,) + parts.shape[3:])
         got = lax.all_to_all(sent, ("z", "y", "kv"), 0, 0, tiled=True)
         received.append(got.reshape((8, 8) + parts.shape[3:]))

time: 212 us -> 207 us (0.976)
    unnamed x28 -> x22, local copies, waits for them, and re-layouts: 4.52 us -> 3.4 us
  transfers between devices with their start and end apart: 11 -> 11, of which waited for: 3 -> 2; matrix products, arithmetic and copies ran while one was open for 0% -> 0% of each run, Pallas kernels for 48% -> 57%
where the time goes in v4:
time: 207 us
  Pallas kernels  159 us (77%)
  starting transfers between devices  25.3 us (12%)
  waiting for transfers between devices  17.5 us (8%)
  local copies, waits for them, and re-layouts  3.4 us (2%)
    pallas_call x3, Pallas kernels, attend(): pl.pallas_call(functools.partial(attend_kernel, tiles, len(q_arrays), len...  152 us
    all_to_all x2, waiting for transfers between devices, on_device(): got = lax.all_to_all(sent, ('z', 'y', 'kv'), 0, 0, tiled=True)  16.4 us
    ppermute x9, starting transfers between devices, swapped(): return lax.ppermute(x, axis, [(n, n ^ flip) for n in range(size)])  12.8 us
    all_to_all x2, starting transfers between devices, on_device(): got = lax.all_to_all(sent, ('z', 'y', 'kv'), 0, 0, tiled=True)  12.6 us
  transfers between devices with their start and end apart: 11, of which 2 were waited for; matrix products, arithmetic and copies ran while one was open for 0% of the time, Pallas kernels for 57%

profile of v4, /device:TPU:0, one launch (start us, length us, event | category | flops | bytes accessed | tf_op | source)
XLA Modules:
  0.0 206.7 jit_solution(2384113886186918122)
XLA Ops:
  0.6 0.1 collective-permute-start.1
  0.7 0.5 collective-permute-start.7
  1.2 4.1 %collective-permute-start.3 = (bf16[2,512,128]{2,1,0:T(8,128)(2,1)}, bf16[2,512,128]{2,1,0:T(8,128)(2,1)S(1)}, u32[]{:S(2)}, u32[]{:S(2)}) collective-permute-start(bf16[2,512,128]{2,1,0:T(8,128)(2,1)} %bitcast.18), channel_id=1, source_target_pairs={{0,48},{16,32},{32,16},{48,0},{1,49},{17,33},{33,17},{49,1},{2,50}... | collective-permute-start | bytes 786440 | tf_op jit(solution)/shard_map/ppermute | solution.py:379
  5.3 0.0 collective-permute-start.2
  5.3 3.2 %collective-permute-start = (bf16[2,512,128]{2,1,0:T(8,128)(2,1)}, bf16[2,512,128]{2,1,0:T(8,128)(2,1)S(1)}, u32[]{:S(2)}, u32[]{:S(2)}) collective-permute-start(bf16[2,512,128]{2,1,0:T(8,128)(2,1)} %bitcast.20), channel_id=1, source_target_pairs={{0,64},{64,0},{1,65},{65,1},{2,66},{66,2},{3,67},{67,3},{4,68},{68... | collective-permute-start | bytes 786440 | tf_op jit(solution)/shard_map/ppermute | solution.py:379
  8.5 0.7 pad_maximum_fusion.1.refs_6_.refs_9_
  9.3 0.0 copy-start.3
  9.3 0.0 copy-start.1
  9.3 0.0 collective-permute-done.1.vp_ref
  9.3 0.0 copy-start
  9.3 0.1 collective-permute-start.8
  9.4 0.9 copy-done
  10.3 3.7 %shard_map.86.refs_8_.refs_11_ = bf16[2,144,4096]{2,1,0:T(8,128)(2,1)} custom-call(s32[2]{0:T(128)} %len_ref.7, bf16[2,2048,128]{2,1,0:T(8,128)(2,1)} %bitcast.17, bf16[2,2048,128]{2,1,0:T(8,128)(2,1)} %copy-done), custom_call_target="tpu_custom_call" | custom-call | flops 1000000 | bytes 4194304 | tf_op jit(solution)/shard_map/pallas_call | solution.py:48
  14.0 0.0 collective-permute-done.3.refs_3_
  14.0 0.0 collective-permute-done.2.refs_2_
  14.0 0.0 copy-start.7
  14.0 1.1 collective-permute-done.refs_1_
  15.1 0.4 collective-permute-start.5
  15.5 1.3 collective-permute-start.4
  16.9 0.0 copy-done.1
  16.9 0.1 pad_maximum_fusion
  16.9 3.0 %collective-permute-start.6 = (bf16[2,2,512,128]{3,2,1,0:T(8,128)(2,1)S(1)}, bf16[2,2,512,128]{3,2,1,0:T(8,128)(2,1)S(1)}, u32[]{:S(2)}, u32[]{:S(2)}) collective-permute-start(bf16[2,2,512,128]{3,2,1,0:T(8,128)(2,1)S(1)} %pad_maximum_fusion), channel_id=1, source_target_pairs={{0,32},{16,48},{32,0},{48,16},{1,33},{17,49},{33,1},{49,17},{2,34}... | collective-permute-start | bytes 1572872 | tf_op jit(solution)/shard_map/ppermute | solution.py:379
  19.9 0.0 collective-permute-done.8.refs_7_.refs_10_
  19.9 0.0 collective-permute-done.7.refs_5_.refs_8_
  19.9 0.0 copy-done.3
  20.0 0.0 copy-done.6
  20.0 0.0 copy-done.7
  20.0 0.0 copy-done.2
  20.0 0.6 copy-done.10
  20.6 1.0 copy-done.4
  21.5 56.8 %shard_map.87 = (bf16[4,2,8,72,128]{4,3,2,1,0:T(8,128)(2,1)}, bf16[4,2,8,72,128]{4,3,2,1,0:T(8,128)(2,1)}) custom-call(s32[2]{0:T(128)} %len_ref.7, s32[2,32]{1,0:T(2,128)} %span_ref.5, bf16[2,512,128]{2,1,0:T(8,128)(2,1)} %bitcast.21, bf16[2,512,128]{2,1,0:T(8,128)(2,1)} %copy-done.2, bf16[2,512,128]{2,1,0:T(8,128)(2,1)} %copy-done.7, ...), custom_call_target="tpu_custom_call" | custom-call | flops 6442450944 | bytes 6291456 | tf_op jit(solution)/shard_map/pallas_call | solution.py:272
  78.4 0.0 collective-permute-done.5.refs_5_
  78.4 0.0 copy-start.8
  78.4 0.0 collective-permute-done.4.refs_4_
  78.4 0.0 copy-start.9
  78.4 0.0 collective-permute-done.6.refs_6_
  78.4 0.0 copy-start.5
  78.5 0.6 copy-done.8
  79.1 0.1 copy-done.9
  79.2 0.2 copy-done.5
  79.4 38.7 %shard_map.89 = bf16[4,2,8,72,128]{4,3,2,1,0:T(8,128)(2,1)} custom-call(s32[2]{0:T(128)} %len_ref.7, s32[2,32]{1,0:T(2,128)} %span_ref.5, bf16[2,512,128]{2,1,0:T(8,128)(2,1)} %bitcast.22, bf16[2,512,128]{2,1,0:T(8,128)(2,1)} %copy-done.2, bf16[2,512,128]{2,1,0:T(8,128)(2,1)} %copy-done.7, ...), custom_call_target="tpu_custom_call", output_to_operand_aliasing={{}: (14, {})} | custom-call | flops 4294967296 | bytes 6291456 | tf_op jit(solution)/shard_map/pallas_call | solution.py:272
  118.1 6.3 %all-to-all-start.1 = ((bf16[64,72,128]{2,1,0:T(8,128)(2,1)}), bf16[64,72,128]{2,1,0:T(8,128)(2,1)S(1)}, u32[]{:S(2)}, u32[]{:S(2)}) async-start(bf16[64,72,128]{2,1,0:T(8,128)(2,1)} %bitcast.15), calls=%async_computation.1 | async-start | bytes 2359296 | tf_op jit(solution)/shard_map/all_to_all | solution.py:425
  124.4 56.5 %shard_map.88 = bf16[4,2,8,72,128]{4,3,2,1,0:T(8,128)(2,1)} custom-call(s32[2]{0:T(128)} %len_ref.7, s32[2,32]{1,0:T(2,128)} %span_ref.5, bf16[2,512,128]{2,1,0:T(8,128)(2,1)} %bitcast.23, bf16[2,512,128]{2,1,0:T(8,128)(2,1)} %copy-done.2, bf16[2,512,128]{2,1,0:T(8,128)(2,1)} %copy-done.7, ...), custom_call_target="tpu_custom_call", output_to_operand_aliasing={{}: (14, {})} | custom-call | flops 6442450944 | bytes 6291456 | tf_op jit(solution)/shard_map/pallas_call | solution.py:272
  180.9 0.0 all-to-all-done.1
  180.9 6.3 %all-to-all-start = ((bf16[64,72,128]{2,1,0:T(8,128)(2,1)}), bf16[64,72,128]{2,1,0:T(8,128)(2,1)S(1)}, u32[]{:S(2)}, u32[]{:S(2)}) async-start(bf16[64,72,128]{2,1,0:T(8,128)(2,1)} %bitcast.14), calls=%async_computation | async-start | bytes 2359296 | tf_op jit(solution)/shard_map/all_to_all | solution.py:425
  187.2 1.5 shard_map.90
  188.7 16.4 %all-to-all-done = bf16[64,72,128]{2,1,0:T(8,128)(2,1)S(1)} async-done(((bf16[64,72,128]{2,1,0:T(8,128)(2,1)}), bf16[64,72,128]{2,1,0:T(8,128)(2,1)S(1)}, u32[]{:S(2)}, u32[]{:S(2)}) %all-to-all-start) | async-done | bytes 1179680 | tf_op jit(solution)/shard_map/all_to_all | solution.py:425
  205.1 1.5 shard_map.91
  (4 shorter events, 0.0 us)
Async XLA Ops:
  0.6 8.7 %collective-permute-start.1 = (bf16[2,2048,128]{2,1,0:T(8,128)(2,1)}, bf16[2,2048,128]{2,1,0:T(8,128)(2,1)S(1)}, u32[]{:S(2)}, u32[]{:S(2)}) collective-permute-start(bf16[2,2048,128]{2,1,0:T(8,128)(2,1)} %bitcast.16), channel_id=1, source_target_pairs={{0,8},{8,0},{1,9},{9,1},{2,10},{10,2},{3,11},{11,3},{4,12},{12,4},... | collective-permute-start | bytes 3145736 | tf_op jit(solution)/shard_map/ppermute | solution.py:379
  0.7 19.2 %collective-permute-start.7 = (bf16[2,2048,128]{2,1,0:T(8,128)(2,1)}, bf16[2,2048,128]{2,1,0:T(8,128)(2,1)S(1)}, u32[]{:S(2)}, u32[]{:S(2)}) collective-permute-start(bf16[2,2048,128]{2,1,0:T(8,128)(2,1)} %bitcast.29), channel_id=1, source_target_pairs={{0,8},{8,0},{1,9},{9,1},{2,10},{10,2},{3,11},{11,3},{4,12},{12,4},... | collective-permute-start | bytes 3145736 | tf_op jit(solution)/shard_map/ppermute | solution.py:379
  1.2 12.8 %collective-permute-start.3 = (bf16[2,512,128]{2,1,0:T(8,128)(2,1)}, bf16[2,512,128]{2,1,0:T(8,128)(2,1)S(1)}, u32[]{:S(2)}, u32[]{:S(2)}) collective-permute-start(bf16[2,512,128]{2,1,0:T(8,128)(2,1)} %bitcast.18), channel_id=1, source_target_pairs={{0,48},{16,32},{32,16},{48,0},{1,49},{17,33},{33,17},{49,1},{2,50}... | collective-permute-start | bytes 786440 | tf_op jit(solution)/shard_map/ppermute | solution.py:379
  5.3 8.7 %collective-permute-start.2 = (bf16[2,512,128]{2,1,0:T(8,128)(2,1)}, bf16[2,512,128]{2,1,0:T(8,128)(2,1)S(1)}, u32[]{:S(2)}, u32[]{:S(2)}) collective-permute-start(bf16[2,512,128]{2,1,0:T(8,128)(2,1)} %bitcast.19), channel_id=1, source_target_pairs={{0,16},{16,0},{32,48},{48,32},{1,17},{17,1},{33,49},{49,33},{2,18}... | collective-permute-start | bytes 786440 | tf_op jit(solution)/shard_map/ppermute | solution.py:379
  5.3 9.8 %collective-permute-start = (bf16[2,512,128]{2,1,0:T(8,128)(2,1)}, bf16[2,512,128]{2,1,0:T(8,128)(2,1)S(1)}, u32[]{:S(2)}, u32[]{:S(2)}) collective-permute-start(bf16[2,512,128]{2,1,0:T(8,128)(2,1)} %bitcast.20), channel_id=1, source_target_pairs={{0,64},{64,0},{1,65},{65,1},{2,66},{66,2},{3,67},{67,3},{4,68},{68... | collective-permute-start | bytes 786440 | tf_op jit(solution)/shard_map/ppermute | solution.py:379
  9.3 10.7 %copy-start.3 = (bf16[2,2,32,128]{3,2,1,0:T(8,128)(2,1)}, bf16[2,2,32,128]{3,2,1,0:T(8,128)(2,1)S(1)}, u32[]{:S(2)}) copy-start(bf16[2,2,32,128]{3,2,1,0:T(8,128)(2,1)S(1)} %pad_maximum_fusion.1.refs_6_.refs_9_) | copy-start | bytes 98308
  9.3 7.6 %copy-start.1 = (bf16[2,32,16,128]{3,2,1,0:T(8,128)(2,1)S(1)}, bf16[2,32,16,128]{3,2,1,0:T(8,128)(2,1)}, u32[]{:S(2)}) copy-start(bf16[2,32,16,128]{3,2,1,0:T(8,128)(2,1)} %param.7) | copy-start | bytes 786436
  9.3 1.0 copy-start
  9.3 10.6 %collective-permute-start.8 = (bf16[2,2,32,128]{3,2,1,0:T(8,128)(2,1)S(1)}, bf16[2,2,32,128]{3,2,1,0:T(8,128)(2,1)S(1)}, u32[]{:S(2)}, u32[]{:S(2)}) collective-permute-start(bf16[2,2,32,128]{3,2,1,0:T(8,128)(2,1)S(1)} %pad_maximum_fusion.1.refs_6_.refs_9_), channel_id=1, source_target_pairs={{0,8},{8,0},{1,9},{9,1},{2,10},{10,2},{3,11},{11,3},{4,12},{12,4},... | collective-permute-start | bytes 98312 | tf_op jit(solution)/shard_map/ppermute | solution.py:379
  14.0 6.0 %copy-start.6 = (bf16[2,512,128]{2,1,0:T(8,128)(2,1)}, bf16[2,512,128]{2,1,0:T(8,128)(2,1)S(1)}, u32[]{:S(2)}) copy-start(bf16[2,512,128]{2,1,0:T(8,128)(2,1)S(1)} %collective-permute-done.3.refs_3_) | copy-start | bytes 786436
  14.0 6.0 %copy-start.7 = (bf16[2,512,128]{2,1,0:T(8,128)(2,1)}, bf16[2,512,128]{2,1,0:T(8,128)(2,1)S(1)}, u32[]{:S(2)}) copy-start(bf16[2,512,128]{2,1,0:T(8,128)(2,1)S(1)} %collective-permute-done.2.refs_2_) | copy-start | bytes 786436
  15.1 4.9 %copy-start.2 = (bf16[2,512,128]{2,1,0:T(8,128)(2,1)}, bf16[2,512,128]{2,1,0:T(8,128)(2,1)S(1)}, u32[]{:S(2)}) copy-start(bf16[2,512,128]{2,1,0:T(8,128)(2,1)S(1)} %collective-permute-done.refs_1_) | copy-start | bytes 786436
  15.1 63.3 %collective-permute-start.5 = (bf16[2,512,128]{2,1,0:T(8,128)(2,1)S(1)}, bf16[2,512,128]{2,1,0:T(8,128)(2,1)S(1)}, u32[]{:S(2)}, u32[]{:S(2)}) collective-permute-start(bf16[2,512,128]{2,1,0:T(8,128)(2,1)S(1)} %collective-permute-done.refs_1_), channel_id=1, source_target_pairs={{0,48},{16,32},{32,16},{48,0},{1,49},{17,33},{33,17},{49,1},{2,50}... | collective-permute-start | bytes 786440 | tf_op jit(solution)/shard_map/ppermute | solution.py:379
  15.5 62.9 %collective-permute-start.4 = (bf16[2,512,128]{2,1,0:T(8,128)(2,1)S(1)}, bf16[2,512,128]{2,1,0:T(8,128)(2,1)S(1)}, u32[]{:S(2)}, u32[]{:S(2)}) collective-permute-start(bf16[2,512,128]{2,1,0:T(8,128)(2,1)S(1)} %collective-permute-done.refs_1_), channel_id=1, source_target_pairs={{0,16},{16,0},{32,48},{48,32},{1,17},{17,1},{33,49},{49,33},{2,18}... | collective-permute-start | bytes 786440 | tf_op jit(solution)/shard_map/ppermute | solution.py:379
  16.9 61.5 %collective-permute-start.6 = (bf16[2,2,512,128]{3,2,1,0:T(8,128)(2,1)S(1)}, bf16[2,2,512,128]{3,2,1,0:T(8,128)(2,1)S(1)}, u32[]{:S(2)}, u32[]{:S(2)}) collective-permute-start(bf16[2,2,512,128]{3,2,1,0:T(8,128)(2,1)S(1)} %pad_maximum_fusion), channel_id=1, source_target_pairs={{0,32},{16,48},{32,0},{48,16},{1,33},{17,49},{33,1},{49,17},{2,34}... | collective-permute-start | bytes 1572872 | tf_op jit(solution)/shard_map/ppermute | solution.py:379
  19.9 0.6 copy-start.10
  20.6 1.0 copy-start.4
  78.4 0.7 copy-start.8
  78.4 0.8 copy-start.9
  78.4 0.9 copy-start.5
  118.1 62.8 %all-to-all-start.1 = ((bf16[64,72,128]{2,1,0:T(8,128)(2,1)}), bf16[64,72,128]{2,1,0:T(8,128)(2,1)S(1)}, u32[]{:S(2)}, u32[]{:S(2)}) async-start(bf16[64,72,128]{2,1,0:T(8,128)(2,1)} %bitcast.15), calls=%async_computation.1 | async-start | bytes 2359296 | tf_op jit(solution)/shard_map/all_to_all | solution.py:425
  180.9 24.2 %all-to-all-start = ((bf16[64,72,128]{2,1,0:T(8,128)(2,1)}), bf16[64,72,128]{2,1,0:T(8,128)(2,1)S(1)}, u32[]{:S(2)}, u32[]{:S(2)}) async-start(bf16[64,72,128]{2,1,0:T(8,128)(2,1)} %bitcast.14), calls=%async_computation | async-start | bytes 2359296 | tf_op jit(solution)/shard_map/all_to_all | solution.py:425

commit v5 on v4

--- a/solution.py
+++ b/solution.py
@@ -13,7 +13,8 @@
 MASKED = -1e30
 SUM_LOW = 2.0**-60
 SUM_HIGH = 2.0**100
-VMEM = 56 << 20
+VMEM = 40 << 20
+VMEM_ALL = 60 << 20
 
 
 def dot_nt(a, b):
@@ -155,11 +156,26 @@
             turned[:, :n_new], p.astype(jnp.bfloat16), preferred_element_type=jnp.float32
         )
 
-    def sends():
-        for t, (request, *halves) in enumerate(tiles):
-            for half, (hop_z, hop_y, _, _) in enumerate(halves):
-                place = out_refs[request - lowest].at[my_z ^ hop_z, my_y ^ hop_y]
-                yield pltpu.make_async_copy(stage.at[t, half], place, sem.at[2 * t + half])
+    def sends(t, request):
+        for half in range(2):
+            hop_z, hop_y = (
+                of_tile(t, lambda tile: tile[1 + half][axis]) for axis in range(2)
+            )
+            place = out_refs[request - lowest].at[my_z ^ hop_z, my_y ^ hop_y]
+            yield pltpu.make_async_copy(stage.at[t, half], place, sem.at[2 * t + half])
+
+    def start_sends(t):
+        for r in requests:
+
+            @pl.when(request_of(t) == r)
+            def _(r=r):
+                for copy in sends(t, r):
+                    copy.start()
+
+    def wait_for_sends():
+        for t, tile in enumerate(tiles):
+            for copy in sends(t, tile[0]):
+                copy.wait()
 
     def finish(t, acc, top):
         total = acc[128:129, :]
@@ -205,6 +221,7 @@
         total = acc[128:129, :]
         fine = (total < SUM_HIGH) & ((total > SUM_LOW) | jnp.logical_not(has_key))
         finish(t, acc, jnp.zeros((1, width), jnp.float32))
+        start_sends(t)
         return jnp.minimum(worst, jnp.where(fine, 1, 0))
 
     worst = lax.fori_loop(0, len(tiles), whole_tile, jnp.ones((1, width), jnp.int32))
@@ -212,6 +229,7 @@
     @pl.when(jnp.min(worst) == 0)
     def _():
         part = 256
+        wait_for_sends()
 
         def again(t, carry):
             request = request_of(t)
@@ -249,17 +267,17 @@
             add(kp_ref, rows)
             top_ref[...] = jnp.broadcast_to(top, top_ref.shape)
             finish(t, acc_ref[...], top_ref[0:1, :])
+            start_sends(t)
             return carry
 
         lax.fori_loop(0, len(tiles), again, 0)
 
-    for copy in sends():
-        copy.start()
-    for copy in sends():
-        copy.wait()
-
-
-def attend(tiles, cached_len, span_order, q_arrays, k_own, k_par, n_own, n_par, vt, partials):
+    wait_for_sends()
+
+
+def attend(
+    tiles, vmem, cached_len, span_order, q_arrays, k_own, k_par, n_own, n_par, vt, partials
+):
     rows = k_own.shape[1]
     block = q_arrays[0].shape[-2]
     owners = 8
@@ -272,8 +290,9 @@
     return pl.pallas_call(
         functools.partial(attend_kernel, tiles, len(q_arrays), len(partials)),
         in_specs=[pl.BlockSpec(memory_space=pltpu.SMEM)] * 2
-        + [pl.BlockSpec(memory_space=pl.ANY)] * (n_in + len(partials)),
-        out_specs=[pl.BlockSpec(memory_space=pl.ANY)] * len(requests),
+        + [pl.BlockSpec(memory_space=pl.ANY)] * n_in
+        + [pl.BlockSpec(memory_space=pltpu.HBM)] * len(partials),
+        out_specs=[pl.BlockSpec(memory_space=pltpu.HBM)] * len(requests),
         scratch_shapes=[pltpu.VMEM((len(requests),) + x.shape[1:], x.dtype) for x in keys]
         + [
             pltpu.VMEM((len(tiles), 2, block, 128), jnp.bfloat16),
@@ -286,7 +305,7 @@
         ],
         out_shape=[result] * len(requests),
         input_output_aliases={2 + n_in + n: n for n in range(len(partials))},
-        compiler_params=pltpu.CompilerParams(vmem_limit_bytes=VMEM),
+        compiler_params=pltpu.CompilerParams(vmem_limit_bytes=vmem),
         cost_estimate=pl.CostEstimate(
             flops=len(tiles) * width * 2 * rows * 128 * 4,
             bytes_accessed=6 << 20,
@@ -390,9 +409,10 @@
     k_par = swapped(k_own, "core")
     n_par = swapped(n_own, "core")
     vt = prepare(cached_len, v_own, v_par)
-    q_other, vt, near = lax.optimization_barrier((q_other, vt, near))
+    q_other, vt = lax.optimization_barrier((q_other, vt))
     next_to = [swapped(q_other, "z", flip) for flip in (1, 3)]
-    far = swapped(jnp.stack([q_own, q_other]), "z", 2)
+    q_both, near = lax.optimization_barrier((jnp.stack([q_own, q_other]), near))
+    far = swapped(q_both, "z", 2)
 
     common = (cached_len, span_order)
     keys = (k_own, k_par, n_own, n_par, vt)
@@ -417,10 +437,10 @@
         ((1, by_own), (1, by_other), (1, last)),
     )
     plan = [tuple(tile(r, *pair) for r, pair in call) for call in plan]
-    partials = attend(plan[0], *common, arrays[:4], *keys, [])
+    partials = attend(plan[0], VMEM, *common, arrays[:4], *keys, [])
     received = []
     for r in range(requests):
-        (parts,) = attend(plan[1 + r], *common, arrays, *keys, [partials[r]])
+        (parts,) = attend(plan[1 + r], VMEM if r == 0 else VMEM_ALL, *common, arrays, *keys, [partials[r]])
         sent = parts.reshape((64,) + parts.shape[3:])
         got = lax.all_to_all(sent, ("z", "y", "kv"), 0, 0, tiled=True)
         received.append(got.reshape((8, 8) + parts.shape[3:]))

time: 207 us -> 204 us (0.986)
  Pallas kernels: 159 us -> 156 us
    pallas_call x1, Pallas kernels: 3.7 us -> 1.38 us  [prepare(): pl.pallas_call(prepare_kernel, grid_spec=pltpu.PrefetchScalarGridSpec(num...]
where the time goes in v5:
time: 204 us; the launch traced here: 203 us
  Pallas kernels  156 us (76%)
  starting transfers between devices  25.4 us (12%)
  waiting for transfers between devices  17.6 us (9%)
  local copies, waits for them, and re-layouts  2.95 us (1%)
    pallas_call x3, Pallas kernels, attend(): pl.pallas_call(functools.partial(attend_kernel, tiles, len(q_arrays), len...  151 us
    all_to_all x2, waiting for transfers between devices, on_device(): got = lax.all_to_all(sent, ('z', 'y', 'kv'), 0, 0, tiled=True)  16.7 us
    ppermute x9, starting transfers between devices, swapped(): return lax.ppermute(x, axis, [(n, n ^ flip) for n in range(size)])  13.7 us
    all_to_all x2, starting transfers between devices, on_device(): got = lax.all_to_all(sent, ('z', 'y', 'kv'), 0, 0, tiled=True)  11.7 us
  transfers between devices with their start and end apart: 11, of which 2 were waited for; matrix products, arithmetic and copies ran while one was open for 0% of the time, Pallas kernels for 57%

profile of v5, /device:TPU:0, one launch (start us, length us, event | category | flops | bytes accessed | tf_op | source)
XLA Modules:
  0.0 203.4 jit_solution(1982557030763695686)
XLA Ops:
  0.6 0.1 collective-permute-start.1
  0.7 0.5 collective-permute-start.7
  1.2 3.3 %collective-permute-start = (bf16[2,512,128]{2,1,0:T(8,128)(2,1)}, bf16[2,512,128]{2,1,0:T(8,128)(2,1)S(1)}, u32[]{:S(2)}, u32[]{:S(2)}) collective-permute-start(bf16[2,512,128]{2,1,0:T(8,128)(2,1)} %bitcast.17), channel_id=1, source_target_pairs={{0,64},{64,0},{1,65},{65,1},{2,66},{66,2},{3,67},{67,3},{4,68},{68... | collective-permute-start | bytes 786440 | tf_op jit(solution)/shard_map/ppermute | solution.py:398
  4.5 4.0 %collective-permute-start.3 = (bf16[2,512,128]{2,1,0:T(8,128)(2,1)}, bf16[2,512,128]{2,1,0:T(8,128)(2,1)S(1)}, u32[]{:S(2)}, u32[]{:S(2)}) collective-permute-start(bf16[2,512,128]{2,1,0:T(8,128)(2,1)} %bitcast.18), channel_id=1, source_target_pairs={{0,48},{16,32},{32,16},{48,0},{1,49},{17,33},{33,17},{49,1},{2,50}... | collective-permute-start | bytes 786440 | tf_op jit(solution)/shard_map/ppermute | solution.py:398
  8.5 0.0 collective-permute-start.2
  8.5 0.8 pad_maximum_fusion.1.refs_6_.refs_9_
  9.3 0.0 collective-permute-done.1.vp_ref
  9.3 0.1 collective-permute-start.8
  9.4 0.0 copy-start.2
  9.4 1.2 copy-done.2
  10.6 0.7 copy-done.6
  11.3 1.4 shard_map.86.refs_8_.refs_11_
  12.7 0.0 copy-start
  12.7 0.0 collective-permute-done.refs_1_
  12.7 0.0 copy-start.4
  12.7 2.6 %collective-permute-start.5 = (bf16[2,512,128]{2,1,0:T(8,128)(2,1)S(1)}, bf16[2,512,128]{2,1,0:T(8,128)(2,1)S(1)}, u32[]{:S(2)}, u32[]{:S(2)}) collective-permute-start(bf16[2,512,128]{2,1,0:T(8,128)(2,1)S(1)} %collective-permute-done.refs_1_), channel_id=1, source_target_pairs={{0,48},{16,32},{32,16},{48,0},{1,49},{17,33},{33,17},{49,1},{2,50}... | collective-permute-start | bytes 786440 | tf_op jit(solution)/shard_map/ppermute | solution.py:398
  15.4 0.0 copy-done.3
  15.4 0.1 pad_maximum_fusion
  15.4 0.0 collective-permute-done.3.refs_3_
  15.4 0.0 copy-start.11
  15.4 0.1 collective-permute-start.4
  15.5 1.0 collective-permute-done.2.refs_2_
  16.5 3.0 %collective-permute-start.6 = (bf16[2,2,512,128]{3,2,1,0:T(8,128)(2,1)S(1)}, bf16[2,2,512,128]{3,2,1,0:T(8,128)(2,1)S(1)}, u32[]{:S(2)}, u32[]{:S(2)}) collective-permute-start(bf16[2,2,512,128]{3,2,1,0:T(8,128)(2,1)S(1)} %pad_maximum_fusion), channel_id=1, source_target_pairs={{0,32},{16,48},{32,0},{48,16},{1,33},{17,49},{33,1},{49,17},{2,34}... | collective-permute-start | bytes 1572872 | tf_op jit(solution)/shard_map/ppermute | solution.py:398
  19.5 0.0 collective-permute-done.8.refs_7_.refs_10_
  19.5 0.0 collective-permute-done.7.refs_5_.refs_8_
  19.5 0.0 copy-done.7
  19.5 0.0 copy-done.16
  19.5 56.2 %shard_map.87 = (bf16[4,2,8,72,128]{4,3,2,1,0:T(8,128)(2,1)}, bf16[4,2,8,72,128]{4,3,2,1,0:T(8,128)(2,1)S(1)}) custom-call(s32[2]{0:T(128)S(1)} %copy-done.7, s32[2,32]{1,0:T(2,128)S(1)} %copy-done.16, bf16[2,512,128]{2,1,0:T(8,128)(2,1)S(1)} %bitcast.22, bf16[2,512,128]{2,1,0:T(8,128)(2,1)S(1)} %collective-permute-done.refs_1_, ...), custom_call_target="tpu_custom_call" | custom-call | flops 6442450944 | bytes 6291456 | tf_op jit(solution)/shard_map/pallas_call | solution.py:290
  75.7 1.0 copy-done.1
  76.8 0.0 collective-permute-done.5.refs_5_
  76.8 0.0 collective-permute-done.4.refs_4_
  76.8 0.0 collective-permute-done.6.refs_6_
  76.8 0.0 copy-start.10
  76.8 0.0 copy-done.5
  76.8 0.0 copy-done
  76.8 0.0 copy-done.4
  76.8 0.0 copy-done.11
  76.8 0.0 copy-done.12
  76.8 0.0 copy-done.15
  76.9 0.0 copy-done.9
  76.9 38.2 %shard_map.89 = bf16[4,2,8,72,128]{4,3,2,1,0:T(8,128)(2,1)} custom-call(s32[2]{0:T(128)S(1)} %copy-done.7, s32[2,32]{1,0:T(2,128)S(1)} %copy-done.16, bf16[2,512,128]{2,1,0:T(8,128)(2,1)S(1)} %bitcast.23, bf16[2,512,128]{2,1,0:T(8,128)(2,1)S(1)} %collective-permute-done.refs_1_, ...), custom_call_target="tpu_custom_call", output_to_operand_aliasing={{}: (14, {})} | custom-call | flops 4294967296 | bytes 6291456 | tf_op jit(solution)/shard_map/pallas_call | solution.py:290
  115.1 5.4 %all-to-all-start.1 = ((bf16[64,72,128]{2,1,0:T(8,128)(2,1)}), bf16[64,72,128]{2,1,0:T(8,128)(2,1)S(1)}, u32[]{:S(2)}, u32[]{:S(2)}) async-start(bf16[64,72,128]{2,1,0:T(8,128)(2,1)} %bitcast.9), calls=%async_computation.1 | async-start | bytes 2359296 | tf_op jit(solution)/shard_map/all_to_all | solution.py:445
  120.6 56.8 %shard_map.88 = bf16[4,2,8,72,128]{4,3,2,1,0:T(8,128)(2,1)} custom-call(s32[2]{0:T(128)} %len_ref.7, s32[2,32]{1,0:T(2,128)} %span_ref.5, bf16[2,512,128]{2,1,0:T(8,128)(2,1)} %bitcast.20, bf16[2,512,128]{2,1,0:T(8,128)(2,1)} %copy-done.4, bf16[2,512,128]{2,1,0:T(8,128)(2,1)} %copy-done.12, ...), custom_call_target="tpu_custom_call", output_to_operand_aliasing={{}: (14, {})} | custom-call | flops 6442450944 | bytes 6291456 | tf_op jit(solution)/shard_map/pallas_call | solution.py:290
  177.3 0.0 all-to-all-done.1
  177.4 6.3 %all-to-all-start = ((bf16[64,72,128]{2,1,0:T(8,128)(2,1)}), bf16[64,72,128]{2,1,0:T(8,128)(2,1)S(1)}, u32[]{:S(2)}, u32[]{:S(2)}) async-start(bf16[64,72,128]{2,1,0:T(8,128)(2,1)} %bitcast.14), calls=%async_computation | async-start | bytes 2359296 | tf_op jit(solution)/shard_map/all_to_all | solution.py:445
  183.6 1.5 shard_map.90
  185.1 16.7 %all-to-all-done = bf16[64,72,128]{2,1,0:T(8,128)(2,1)S(1)} async-done(((bf16[64,72,128]{2,1,0:T(8,128)(2,1)}), bf16[64,72,128]{2,1,0:T(8,128)(2,1)S(1)}, u32[]{:S(2)}, u32[]{:S(2)}) %all-to-all-start) | async-done | bytes 1179680 | tf_op jit(solution)/shard_map/all_to_all | solution.py:445
  201.8 1.5 shard_map.91
  (16 shorter events, 0.0 us)
Async XLA Ops:
  0.6 8.7 %collective-permute-start.1 = (bf16[2,2048,128]{2,1,0:T(8,128)(2,1)}, bf16[2,2048,128]{2,1,0:T(8,128)(2,1)S(1)}, u32[]{:S(2)}, u32[]{:S(2)}) collective-permute-start(bf16[2,2048,128]{2,1,0:T(8,128)(2,1)} %bitcast.15), channel_id=1, source_target_pairs={{0,8},{8,0},{1,9},{9,1},{2,10},{10,2},{3,11},{11,3},{4,12},{12,4},... | collective-permute-start | bytes 3145736 | tf_op jit(solution)/shard_map/ppermute | solution.py:398
  0.7 18.7 %collective-permute-start.7 = (bf16[2,2048,128]{2,1,0:T(8,128)(2,1)}, bf16[2,2048,128]{2,1,0:T(8,128)(2,1)S(1)}, u32[]{:S(2)}, u32[]{:S(2)}) collective-permute-start(bf16[2,2048,128]{2,1,0:T(8,128)(2,1)} %bitcast.25), channel_id=1, source_target_pairs={{0,8},{8,0},{1,9},{9,1},{2,10},{10,2},{3,11},{11,3},{4,12},{12,4},... | collective-permute-start | bytes 3145736 | tf_op jit(solution)/shard_map/ppermute | solution.py:398
  1.2 11.5 %collective-permute-start = (bf16[2,512,128]{2,1,0:T(8,128)(2,1)}, bf16[2,512,128]{2,1,0:T(8,128)(2,1)S(1)}, u32[]{:S(2)}, u32[]{:S(2)}) collective-permute-start(bf16[2,512,128]{2,1,0:T(8,128)(2,1)} %bitcast.17), channel_id=1, source_target_pairs={{0,64},{64,0},{1,65},{65,1},{2,66},{66,2},{3,67},{67,3},{4,68},{68... | collective-permute-start | bytes 786440 | tf_op jit(solution)/shard_map/ppermute | solution.py:398
  4.5 10.9 %collective-permute-start.3 = (bf16[2,512,128]{2,1,0:T(8,128)(2,1)}, bf16[2,512,128]{2,1,0:T(8,128)(2,1)S(1)}, u32[]{:S(2)}, u32[]{:S(2)}) collective-permute-start(bf16[2,512,128]{2,1,0:T(8,128)(2,1)} %bitcast.18), channel_id=1, source_target_pairs={{0,48},{16,32},{32,16},{48,0},{1,49},{17,33},{33,17},{49,1},{2,50}... | collective-permute-start | bytes 786440 | tf_op jit(solution)/shard_map/ppermute | solution.py:398
  8.5 8.0 %collective-permute-start.2 = (bf16[2,512,128]{2,1,0:T(8,128)(2,1)}, bf16[2,512,128]{2,1,0:T(8,128)(2,1)S(1)}, u32[]{:S(2)}, u32[]{:S(2)}) collective-permute-start(bf16[2,512,128]{2,1,0:T(8,128)(2,1)} %bitcast.19), channel_id=1, source_target_pairs={{0,16},{16,0},{32,48},{48,32},{1,17},{17,1},{33,49},{49,33},{2,18}... | collective-permute-start | bytes 786440 | tf_op jit(solution)/shard_map/ppermute | solution.py:398
  8.5 10.9 %copy-start.7 = (s32[2]{0:T(128)S(1)}, s32[2]{0:T(128)}, u32[]{:S(2)}) copy-start(s32[2]{0:T(128)} %len_ref.7) | copy-start | bytes 28
  8.5 10.9 %copy-start.16 = (s32[2,32]{1,0:T(2,128)S(1)}, s32[2,32]{1,0:T(2,128)}, u32[]{:S(2)}) copy-start(s32[2,32]{1,0:T(2,128)} %span_ref.5) | copy-start | bytes 772
  9.3 67.5 %copy-start.5 = (bf16[2,2,32,128]{3,2,1,0:T(8,128)(2,1)}, bf16[2,2,32,128]{3,2,1,0:T(8,128)(2,1)S(1)}, u32[]{:S(2)}) copy-start(bf16[2,2,32,128]{3,2,1,0:T(8,128)(2,1)S(1)} %pad_maximum_fusion.1.refs_6_.refs_9_) | copy-start | bytes 98308
  9.3 10.1 %collective-permute-start.8 = (bf16[2,2,32,128]{3,2,1,0:T(8,128)(2,1)S(1)}, bf16[2,2,32,128]{3,2,1,0:T(8,128)(2,1)S(1)}, u32[]{:S(2)}, u32[]{:S(2)}) collective-permute-start(bf16[2,2,32,128]{3,2,1,0:T(8,128)(2,1)S(1)} %pad_maximum_fusion.1.refs_6_.refs_9_), channel_id=1, source_target_pairs={{0,8},{8,0},{1,9},{9,1},{2,10},{10,2},{3,11},{11,3},{4,12},{12,4},... | collective-permute-start | bytes 98312 | tf_op jit(solution)/shard_map/ppermute | solution.py:398
  9.4 1.2 copy-start.2
  10.6 0.7 copy-start.6
  11.3 4.1 %copy-start.3 = (bf16[2,32,16,128]{3,2,1,0:T(8,128)(2,1)S(1)}, bf16[2,32,16,128]{3,2,1,0:T(8,128)(2,1)}, u32[]{:S(2)}) copy-start(bf16[2,32,16,128]{3,2,1,0:T(8,128)(2,1)} %param.7) | copy-start | bytes 786436
  11.3 8.2 %copy-start.8 = (bf16[2,2048,1,128]{3,1,2,0:T(8,128)(2,1)S(1)}, bf16[2,2048,1,128]{3,1,2,0:T(8,128)(2,1)}, u32[]{:S(2)}) copy-start(bf16[2,2048,1,128]{3,1,2,0:T(8,128)(2,1)} %param.10) | copy-start | bytes 3145732
  12.7 64.1 %copy-start = (bf16[2,144,4096]{2,1,0:T(8,128)(2,1)}, bf16[2,144,4096]{2,1,0:T(8,128)(2,1)S(1)}, u32[]{:S(2)}) copy-start(bf16[2,144,4096]{2,1,0:T(8,128)(2,1)S(1)} %shard_map.86.refs_8_.refs_11_) | copy-start | bytes 7077892
  12.7 64.1 %copy-start.4 = (bf16[2,512,128]{2,1,0:T(8,128)(2,1)}, bf16[2,512,128]{2,1,0:T(8,128)(2,1)S(1)}, u32[]{:S(2)}) copy-start(bf16[2,512,128]{2,1,0:T(8,128)(2,1)S(1)} %collective-permute-done.refs_1_) | copy-start | bytes 786436
  12.7 64.0 %collective-permute-start.5 = (bf16[2,512,128]{2,1,0:T(8,128)(2,1)S(1)}, bf16[2,512,128]{2,1,0:T(8,128)(2,1)S(1)}, u32[]{:S(2)}, u32[]{:S(2)}) collective-permute-start(bf16[2,512,128]{2,1,0:T(8,128)(2,1)S(1)} %collective-permute-done.refs_1_), channel_id=1, source_target_pairs={{0,48},{16,32},{32,16},{48,0},{1,49},{17,33},{33,17},{49,1},{2,50}... | collective-permute-start | bytes 786440 | tf_op jit(solution)/shard_map/ppermute | solution.py:398
  15.4 61.4 %copy-start.11 = (bf16[2,512,128]{2,1,0:T(8,128)(2,1)}, bf16[2,512,128]{2,1,0:T(8,128)(2,1)S(1)}, u32[]{:S(2)}) copy-start(bf16[2,512,128]{2,1,0:T(8,128)(2,1)S(1)} %collective-permute-done.3.refs_3_) | copy-start | bytes 786436
  15.4 61.3 %collective-permute-start.4 = (bf16[2,512,128]{2,1,0:T(8,128)(2,1)S(1)}, bf16[2,512,128]{2,1,0:T(8,128)(2,1)S(1)}, u32[]{:S(2)}, u32[]{:S(2)}) collective-permute-start(bf16[2,512,128]{2,1,0:T(8,128)(2,1)S(1)} %collective-permute-done.refs_1_), channel_id=1, source_target_pairs={{0,16},{16,0},{32,48},{48,32},{1,17},{17,1},{33,49},{49,33},{2,18}... | collective-permute-start | bytes 786440 | tf_op jit(solution)/shard_map/ppermute | solution.py:398
  16.5 60.3 %copy-start.12 = (bf16[2,512,128]{2,1,0:T(8,128)(2,1)}, bf16[2,512,128]{2,1,0:T(8,128)(2,1)S(1)}, u32[]{:S(2)}) copy-start(bf16[2,512,128]{2,1,0:T(8,128)(2,1)S(1)} %collective-permute-done.2.refs_2_) | copy-start | bytes 786436
  16.5 60.3 %collective-permute-start.6 = (bf16[2,2,512,128]{3,2,1,0:T(8,128)(2,1)S(1)}, bf16[2,2,512,128]{3,2,1,0:T(8,128)(2,1)S(1)}, u32[]{:S(2)}, u32[]{:S(2)}) collective-permute-start(bf16[2,2,512,128]{3,2,1,0:T(8,128)(2,1)S(1)} %pad_maximum_fusion), channel_id=1, source_target_pairs={{0,32},{16,48},{32,0},{48,16},{1,33},{17,49},{33,1},{49,17},{2,34}... | collective-permute-start | bytes 1572872 | tf_op jit(solution)/shard_map/ppermute | solution.py:398
  19.5 57.4 %copy-start.15 = (bf16[2,2,32,128]{3,2,1,0:T(8,128)(2,1)}, bf16[2,2,32,128]{3,2,1,0:T(8,128)(2,1)S(1)}, u32[]{:S(2)}) copy-start(bf16[2,2,32,128]{3,2,1,0:T(8,128)(2,1)S(1)} %collective-permute-done.8.refs_7_.refs_10_) | copy-start | bytes 98308
  19.5 57.4 %copy-start.9 = (bf16[2,2048,128]{2,1,0:T(8,128)(2,1)}, bf16[2,2048,128]{2,1,0:T(8,128)(2,1)S(1)}, u32[]{:S(2)}) copy-start(bf16[2,2048,128]{2,1,0:T(8,128)(2,1)S(1)} %collective-permute-done.7.refs_5_.refs_8_) | copy-start | bytes 3145732
  75.7 1.0 copy-start.1
  76.8 38.3 %copy-start.13 = (bf16[2,512,128]{2,1,0:T(8,128)(2,1)}, bf16[2,512,128]{2,1,0:T(8,128)(2,1)S(1)}, u32[]{:S(2)}) copy-start(bf16[2,512,128]{2,1,0:T(8,128)(2,1)S(1)} %collective-permute-done.5.refs_5_) | copy-start | bytes 786436
  76.8 38.3 %copy-start.14 = (bf16[2,512,128]{2,1,0:T(8,128)(2,1)}, bf16[2,512,128]{2,1,0:T(8,128)(2,1)S(1)}, u32[]{:S(2)}) copy-start(bf16[2,512,128]{2,1,0:T(8,128)(2,1)S(1)} %collective-permute-done.4.refs_4_) | copy-start | bytes 786436
  76.8 38.3 %copy-start.10 = (bf16[2,2,512,128]{3,2,1,0:T(8,128)(2,1)}, bf16[2,2,512,128]{3,2,1,0:T(8,128)(2,1)S(1)}, u32[]{:S(2)}) copy-start(bf16[2,2,512,128]{3,2,1,0:T(8,128)(2,1)S(1)} %collective-permute-done.6.refs_6_) | copy-start | bytes 1572868
  115.1 62.2 %all-to-all-start.1 = ((bf16[64,72,128]{2,1,0:T(8,128)(2,1)}), bf16[64,72,128]{2,1,0:T(8,128)(2,1)S(1)}, u32[]{:S(2)}, u32[]{:S(2)}) async-start(bf16[64,72,128]{2,1,0:T(8,128)(2,1)} %bitcast.9), calls=%async_computation.1 | async-start | bytes 2359296 | tf_op jit(solution)/shard_map/all_to_all | solution.py:445
  177.4 24.4 %all-to-all-start = ((bf16[64,72,128]{2,1,0:T(8,128)(2,1)}), bf16[64,72,128]{2,1,0:T(8,128)(2,1)S(1)}, u32[]{:S(2)}, u32[]{:S(2)}) async-start(bf16[64,72,128]{2,1,0:T(8,128)(2,1)} %bitcast.14), calls=%async_computation | async-start | bytes 2359296 | tf_op jit(solution)/shard_map/all_to_all | solution.py:445

commit v6 on v5

--- a/solution.py
+++ b/solution.py
@@ -161,7 +161,7 @@
             hop_z, hop_y = (
                 of_tile(t, lambda tile: tile[1 + half][axis]) for axis in range(2)
             )
-            place = out_refs[request - lowest].at[my_z ^ hop_z, my_y ^ hop_y]
+            place = out_refs[request - lowest].at[my_z ^ hop_z ^ (2 * core), my_y ^ hop_y ^ core]
             yield pltpu.make_async_copy(stage.at[t, half], place, sem.at[2 * t + half])
 
     def start_sends(t):
@@ -438,11 +438,22 @@
     )
     plan = [tuple(tile(r, *pair) for r, pair in call) for call in plan]
     partials = attend(plan[0], VMEM, *common, arrays[:4], *keys, [])
+    groups = [
+        [
+            (((y ^ core) * 4 + (z ^ (2 * core))) * 2 + core) * 8 + kv
+            for z in range(4)
+            for y in range(2)
+            for kv in range(8)
+        ]
+        for core in range(2)
+    ]
     received = []
     for r in range(requests):
         (parts,) = attend(plan[1 + r], VMEM if r == 0 else VMEM_ALL, *common, arrays, *keys, [partials[r]])
         sent = parts.reshape((64,) + parts.shape[3:])
-        got = lax.all_to_all(sent, ("z", "y", "kv"), 0, 0, tiled=True)
+        got = lax.all_to_all(
+            sent, ("y", "z", "core", "kv"), 0, 0, axis_index_groups=groups, tiled=True
+        )
         received.append(got.reshape((8, 8) + parts.shape[3:]))
     results = []
     for r in range(requests):

time: 204 us -> 208 us (1.020)
  waiting for transfers between devices: 17.6 us -> 20.5 us
    all_to_all x2, waiting for transfers between devices: 16.7 us -> 19.5 us  [on_device(): lax.all_to_all(sent, ('y', 'z', 'core', 'kv'), 0, 0, axis_index_groups=gr...]
  transfers between devices with their start and end apart: 11 -> 11, of which waited for: 2 -> 2; matrix products, arithmetic and copies ran while one was open for 0% -> 0% of each run, Pallas kernels for 57% -> 56%
where the time goes in v6:
time: 208 us; the launch traced here: 206 us
  Pallas kernels  156 us (75%)
  starting transfers between devices  25.4 us (12%)
  waiting for transfers between devices  20.5 us (10%)
  local copies, waits for them, and re-layouts  2.95 us (1%)
    pallas_call x3, Pallas kernels, attend(): pl.pallas_call(functools.partial(attend_kernel, tiles, len(q_arrays), len...  151 us
    all_to_all x2, waiting for transfers between devices, on_device(): lax.all_to_all(sent, ('y', 'z', 'core', 'kv'), 0, 0, axis_index_groups=gr...  19.5 us
    ppermute x9, starting transfers between devices, swapped(): return lax.ppermute(x, axis, [(n, n ^ flip) for n in range(size)])  13.7 us
    all_to_all x2, starting transfers between devices, on_device(): lax.all_to_all(sent, ('y', 'z', 'core', 'kv'), 0, 0, axis_index_groups=gr...  11.7 us
  transfers between devices with their start and end apart: 11, of which 2 were waited for; matrix products, arithmetic and copies ran while one was open for 0% of the time, Pallas kernels for 56%

profile of v6, /device:TPU:0, one launch (start us, length us, event | category | flops | bytes accessed | tf_op | source)
XLA Modules:
  0.0 206.3 jit_solution(5962096571774966778)
XLA Ops:
  0.6 0.1 collective-permute-start.1
  0.7 0.5 collective-permute-start.7
  1.2 3.3 %collective-permute-start = (bf16[2,512,128]{2,1,0:T(8,128)(2,1)}, bf16[2,512,128]{2,1,0:T(8,128)(2,1)S(1)}, u32[]{:S(2)}, u32[]{:S(2)}) collective-permute-start(bf16[2,512,128]{2,1,0:T(8,128)(2,1)} %bitcast.17), channel_id=1, source_target_pairs={{0,64},{64,0},{1,65},{65,1},{2,66},{66,2},{3,67},{67,3},{4,68},{68... | collective-permute-start | bytes 786440 | tf_op jit(solution)/shard_map/ppermute | solution.py:398
  4.5 4.0 %collective-permute-start.3 = (bf16[2,512,128]{2,1,0:T(8,128)(2,1)}, bf16[2,512,128]{2,1,0:T(8,128)(2,1)S(1)}, u32[]{:S(2)}, u32[]{:S(2)}) collective-permute-start(bf16[2,512,128]{2,1,0:T(8,128)(2,1)} %bitcast.18), channel_id=1, source_target_pairs={{0,48},{16,32},{32,16},{48,0},{1,49},{17,33},{33,17},{49,1},{2,50}... | collective-permute-start | bytes 786440 | tf_op jit(solution)/shard_map/ppermute | solution.py:398
  8.5 0.0 collective-permute-start.2
  8.5 0.8 pad_maximum_fusion.1.refs_6_.refs_9_
  9.3 0.0 collective-permute-done.1.vp_ref
  9.3 0.1 collective-permute-start.8
  9.4 0.0 copy-start.2
  9.4 1.2 copy-done.2
  10.6 0.7 copy-done.6
  11.3 1.4 shard_map.86.refs_8_.refs_11_
  12.7 0.0 copy-start
  12.7 0.0 collective-permute-done.refs_1_
  12.7 0.0 copy-start.4
  12.7 2.6 %collective-permute-start.5 = (bf16[2,512,128]{2,1,0:T(8,128)(2,1)S(1)}, bf16[2,512,128]{2,1,0:T(8,128)(2,1)S(1)}, u32[]{:S(2)}, u32[]{:S(2)}) collective-permute-start(bf16[2,512,128]{2,1,0:T(8,128)(2,1)S(1)} %collective-permute-done.refs_1_), channel_id=1, source_target_pairs={{0,48},{16,32},{32,16},{48,0},{1,49},{17,33},{33,17},{49,1},{2,50}... | collective-permute-start | bytes 786440 | tf_op jit(solution)/shard_map/ppermute | solution.py:398
  15.4 0.0 copy-done.3
  15.4 0.1 pad_maximum_fusion
  15.4 0.0 collective-permute-done.3.refs_3_
  15.4 0.1 collective-permute-start.4
  15.5 1.0 collective-permute-done.2.refs_2_
  16.5 3.0 %collective-permute-start.6 = (bf16[2,2,512,128]{3,2,1,0:T(8,128)(2,1)S(1)}, bf16[2,2,512,128]{3,2,1,0:T(8,128)(2,1)S(1)}, u32[]{:S(2)}, u32[]{:S(2)}) collective-permute-start(bf16[2,2,512,128]{3,2,1,0:T(8,128)(2,1)S(1)} %pad_maximum_fusion), channel_id=1, source_target_pairs={{0,32},{16,48},{32,0},{48,16},{1,33},{17,49},{33,1},{49,17},{2,34}... | collective-permute-start | bytes 1572872 | tf_op jit(solution)/shard_map/ppermute | solution.py:398
  19.5 0.0 collective-permute-done.8.refs_7_.refs_10_
  19.5 0.0 collective-permute-done.7.refs_5_.refs_8_
  19.5 56.2 %shard_map.87 = (bf16[4,2,8,72,128]{4,3,2,1,0:T(8,128)(2,1)}, bf16[4,2,8,72,128]{4,3,2,1,0:T(8,128)(2,1)S(1)}) custom-call(s32[2]{0:T(128)S(1)} %copy-done.7, s32[2,32]{1,0:T(2,128)S(1)} %copy-done.16, bf16[2,512,128]{2,1,0:T(8,128)(2,1)S(1)} %bitcast.22, bf16[2,512,128]{2,1,0:T(8,128)(2,1)S(1)} %collective-permute-done.refs_1_, ...), custom_call_target="tpu_custom_call" | custom-call | flops 6442450944 | bytes 6291456 | tf_op jit(solution)/shard_map/pallas_call | solution.py:290
  75.7 1.0 copy-done.1
  76.8 0.0 collective-permute-done.5.refs_5_
  76.8 0.0 collective-permute-done.4.refs_4_
  76.8 0.0 collective-permute-done.6.refs_6_
  76.8 0.0 copy-start.10
  76.8 0.0 copy-done.5
  76.8 0.0 copy-done
  76.8 0.0 copy-done.4
  76.8 0.0 copy-done.11
  76.8 0.0 copy-done.12
  76.9 0.0 copy-done.15
  76.9 0.0 copy-done.9
  76.9 38.2 %shard_map.89 = bf16[4,2,8,72,128]{4,3,2,1,0:T(8,128)(2,1)} custom-call(s32[2]{0:T(128)S(1)} %copy-done.7, s32[2,32]{1,0:T(2,128)S(1)} %copy-done.16, bf16[2,512,128]{2,1,0:T(8,128)(2,1)S(1)} %bitcast.23, bf16[2,512,128]{2,1,0:T(8,128)(2,1)S(1)} %collective-permute-done.refs_1_, ...), custom_call_target="tpu_custom_call", output_to_operand_aliasing={{}: (14, {})} | custom-call | flops 4294967296 | bytes 6291456 | tf_op jit(solution)/shard_map/pallas_call | solution.py:290
  115.1 0.0 copy-done.13
  115.1 0.0 copy-done.14
  115.1 0.0 copy-done.10
  115.1 5.4 %all-to-all-start.1 = ((bf16[64,72,128]{2,1,0:T(8,128)(2,1)}), bf16[64,72,128]{2,1,0:T(8,128)(2,1)S(1)}, u32[]{:S(2)}, u32[]{:S(2)}) async-start(bf16[64,72,128]{2,1,0:T(8,128)(2,1)} %bitcast.9), calls=%async_computation.1 | async-start | bytes 2359296 | tf_op jit(solution)/shard_map/all_to_all | solution.py:454
  120.6 56.8 %shard_map.88 = bf16[4,2,8,72,128]{4,3,2,1,0:T(8,128)(2,1)} custom-call(s32[2]{0:T(128)} %len_ref.7, s32[2,32]{1,0:T(2,128)} %span_ref.5, bf16[2,512,128]{2,1,0:T(8,128)(2,1)} %bitcast.20, bf16[2,512,128]{2,1,0:T(8,128)(2,1)} %copy-done.4, bf16[2,512,128]{2,1,0:T(8,128)(2,1)} %copy-done.12, ...), custom_call_target="tpu_custom_call", output_to_operand_aliasing={{}: (14, {})} | custom-call | flops 6442450944 | bytes 6291456 | tf_op jit(solution)/shard_map/pallas_call | solution.py:290
  177.4 0.0 all-to-all-done.1
  177.4 6.3 %all-to-all-start = ((bf16[64,72,128]{2,1,0:T(8,128)(2,1)}), bf16[64,72,128]{2,1,0:T(8,128)(2,1)S(1)}, u32[]{:S(2)}, u32[]{:S(2)}) async-start(bf16[64,72,128]{2,1,0:T(8,128)(2,1)} %bitcast.14), calls=%async_computation | async-start | bytes 2359296 | tf_op jit(solution)/shard_map/all_to_all | solution.py:454
  183.6 1.5 shard_map.90
  185.2 19.5 %all-to-all-done = bf16[64,72,128]{2,1,0:T(8,128)(2,1)S(1)} async-done(((bf16[64,72,128]{2,1,0:T(8,128)(2,1)}), bf16[64,72,128]{2,1,0:T(8,128)(2,1)S(1)}, u32[]{:S(2)}, u32[]{:S(2)}) %all-to-all-start) | async-done | bytes 1179680 | tf_op jit(solution)/shard_map/all_to_all | solution.py:454
  204.6 1.5 shard_map.91
  (16 shorter events, 0.0 us)
Async XLA Ops:
  0.6 8.7 %collective-permute-start.1 = (bf16[2,2048,128]{2,1,0:T(8,128)(2,1)}, bf16[2,2048,128]{2,1,0:T(8,128)(2,1)S(1)}, u32[]{:S(2)}, u32[]{:S(2)}) collective-permute-start(bf16[2,2048,128]{2,1,0:T(8,128)(2,1)} %bitcast.15), channel_id=1, source_target_pairs={{0,8},{8,0},{1,9},{9,1},{2,10},{10,2},{3,11},{11,3},{4,12},{12,4},... | collective-permute-start | bytes 3145736 | tf_op jit(solution)/shard_map/ppermute | solution.py:398
  0.7 18.7 %collective-permute-start.7 = (bf16[2,2048,128]{2,1,0:T(8,128)(2,1)}, bf16[2,2048,128]{2,1,0:T(8,128)(2,1)S(1)}, u32[]{:S(2)}, u32[]{:S(2)}) collective-permute-start(bf16[2,2048,128]{2,1,0:T(8,128)(2,1)} %bitcast.25), channel_id=1, source_target_pairs={{0,8},{8,0},{1,9},{9,1},{2,10},{10,2},{3,11},{11,3},{4,12},{12,4},... | collective-permute-start | bytes 3145736 | tf_op jit(solution)/shard_map/ppermute | solution.py:398
  1.2 11.5 %collective-permute-start = (bf16[2,512,128]{2,1,0:T(8,128)(2,1)}, bf16[2,512,128]{2,1,0:T(8,128)(2,1)S(1)}, u32[]{:S(2)}, u32[]{:S(2)}) collective-permute-start(bf16[2,512,128]{2,1,0:T(8,128)(2,1)} %bitcast.17), channel_id=1, source_target_pairs={{0,64},{64,0},{1,65},{65,1},{2,66},{66,2},{3,67},{67,3},{4,68},{68... | collective-permute-start | bytes 786440 | tf_op jit(solution)/shard_map/ppermute | solution.py:398
  4.5 10.9 %collective-permute-start.3 = (bf16[2,512,128]{2,1,0:T(8,128)(2,1)}, bf16[2,512,128]{2,1,0:T(8,128)(2,1)S(1)}, u32[]{:S(2)}, u32[]{:S(2)}) collective-permute-start(bf16[2,512,128]{2,1,0:T(8,128)(2,1)} %bitcast.18), channel_id=1, source_target_pairs={{0,48},{16,32},{32,16},{48,0},{1,49},{17,33},{33,17},{49,1},{2,50}... | collective-permute-start | bytes 786440 | tf_op jit(solution)/shard_map/ppermute | solution.py:398
  8.5 8.0 %collective-permute-start.2 = (bf16[2,512,128]{2,1,0:T(8,128)(2,1)}, bf16[2,512,128]{2,1,0:T(8,128)(2,1)S(1)}, u32[]{:S(2)}, u32[]{:S(2)}) collective-permute-start(bf16[2,512,128]{2,1,0:T(8,128)(2,1)} %bitcast.19), channel_id=1, source_target_pairs={{0,16},{16,0},{32,48},{48,32},{1,17},{17,1},{33,49},{49,33},{2,18}... | collective-permute-start | bytes 786440 | tf_op jit(solution)/shard_map/ppermute | solution.py:398
  8.5 10.9 %copy-start.7 = (s32[2]{0:T(128)S(1)}, s32[2]{0:T(128)}, u32[]{:S(2)}) copy-start(s32[2]{0:T(128)} %len_ref.7) | copy-start | bytes 28
  8.5 10.9 %copy-start.16 = (s32[2,32]{1,0:T(2,128)S(1)}, s32[2,32]{1,0:T(2,128)}, u32[]{:S(2)}) copy-start(s32[2,32]{1,0:T(2,128)} %span_ref.5) | copy-start | bytes 772
  9.3 67.5 %copy-start.5 = (bf16[2,2,32,128]{3,2,1,0:T(8,128)(2,1)}, bf16[2,2,32,128]{3,2,1,0:T(8,128)(2,1)S(1)}, u32[]{:S(2)}) copy-start(bf16[2,2,32,128]{3,2,1,0:T(8,128)(2,1)S(1)} %pad_maximum_fusion.1.refs_6_.refs_9_) | copy-start | bytes 98308
  9.3 10.1 %collective-permute-start.8 = (bf16[2,2,32,128]{3,2,1,0:T(8,128)(2,1)S(1)}, bf16[2,2,32,128]{3,2,1,0:T(8,128)(2,1)S(1)}, u32[]{:S(2)}, u32[]{:S(2)}) collective-permute-start(bf16[2,2,32,128]{3,2,1,0:T(8,128)(2,1)S(1)} %pad_maximum_fusion.1.refs_6_.refs_9_), channel_id=1, source_target_pairs={{0,8},{8,0},{1,9},{9,1},{2,10},{10,2},{3,11},{11,3},{4,12},{12,4},... | collective-permute-start | bytes 98312 | tf_op jit(solution)/shard_map/ppermute | solution.py:398
  9.4 1.2 copy-start.2
  10.6 0.7 copy-start.6
  11.3 4.1 %copy-start.3 = (bf16[2,32,16,128]{3,2,1,0:T(8,128)(2,1)S(1)}, bf16[2,32,16,128]{3,2,1,0:T(8,128)(2,1)}, u32[]{:S(2)}) copy-start(bf16[2,32,16,128]{3,2,1,0:T(8,128)(2,1)} %param.7) | copy-start | bytes 786436
  11.3 8.2 %copy-start.8 = (bf16[2,2048,1,128]{3,1,2,0:T(8,128)(2,1)S(1)}, bf16[2,2048,1,128]{3,1,2,0:T(8,128)(2,1)}, u32[]{:S(2)}) copy-start(bf16[2,2048,1,128]{3,1,2,0:T(8,128)(2,1)} %param.10) | copy-start | bytes 3145732
  12.7 64.1 %copy-start = (bf16[2,144,4096]{2,1,0:T(8,128)(2,1)}, bf16[2,144,4096]{2,1,0:T(8,128)(2,1)S(1)}, u32[]{:S(2)}) copy-start(bf16[2,144,4096]{2,1,0:T(8,128)(2,1)S(1)} %shard_map.86.refs_8_.refs_11_) | copy-start | bytes 7077892
  12.7 64.1 %copy-start.4 = (bf16[2,512,128]{2,1,0:T(8,128)(2,1)}, bf16[2,512,128]{2,1,0:T(8,128)(2,1)S(1)}, u32[]{:S(2)}) copy-start(bf16[2,512,128]{2,1,0:T(8,128)(2,1)S(1)} %collective-permute-done.refs_1_) | copy-start | bytes 786436
  12.7 64.0 %collective-permute-start.5 = (bf16[2,512,128]{2,1,0:T(8,128)(2,1)S(1)}, bf16[2,512,128]{2,1,0:T(8,128)(2,1)S(1)}, u32[]{:S(2)}, u32[]{:S(2)}) collective-permute-start(bf16[2,512,128]{2,1,0:T(8,128)(2,1)S(1)} %collective-permute-done.refs_1_), channel_id=1, source_target_pairs={{0,48},{16,32},{32,16},{48,0},{1,49},{17,33},{33,17},{49,1},{2,50}... | collective-permute-start | bytes 786440 | tf_op jit(solution)/shard_map/ppermute | solution.py:398
  15.4 61.4 %copy-start.11 = (bf16[2,512,128]{2,1,0:T(8,128)(2,1)}, bf16[2,512,128]{2,1,0:T(8,128)(2,1)S(1)}, u32[]{:S(2)}) copy-start(bf16[2,512,128]{2,1,0:T(8,128)(2,1)S(1)} %collective-permute-done.3.refs_3_) | copy-start | bytes 786436
  15.4 61.3 %collective-permute-start.4 = (bf16[2,512,128]{2,1,0:T(8,128)(2,1)S(1)}, bf16[2,512,128]{2,1,0:T(8,128)(2,1)S(1)}, u32[]{:S(2)}, u32[]{:S(2)}) collective-permute-start(bf16[2,512,128]{2,1,0:T(8,128)(2,1)S(1)} %collective-permute-done.refs_1_), channel_id=1, source_target_pairs={{0,16},{16,0},{32,48},{48,32},{1,17},{17,1},{33,49},{49,33},{2,18}... | collective-permute-start | bytes 786440 | tf_op jit(solution)/shard_map/ppermute | solution.py:398
  16.5 60.4 %copy-start.12 = (bf16[2,512,128]{2,1,0:T(8,128)(2,1)}, bf16[2,512,128]{2,1,0:T(8,128)(2,1)S(1)}, u32[]{:S(2)}) copy-start(bf16[2,512,128]{2,1,0:T(8,128)(2,1)S(1)} %collective-permute-done.2.refs_2_) | copy-start | bytes 786436
  16.5 60.3 %collective-permute-start.6 = (bf16[2,2,512,128]{3,2,1,0:T(8,128)(2,1)S(1)}, bf16[2,2,512,128]{3,2,1,0:T(8,128)(2,1)S(1)}, u32[]{:S(2)}, u32[]{:S(2)}) collective-permute-start(bf16[2,2,512,128]{3,2,1,0:T(8,128)(2,1)S(1)} %pad_maximum_fusion), channel_id=1, source_target_pairs={{0,32},{16,48},{32,0},{48,16},{1,33},{17,49},{33,1},{49,17},{2,34}... | collective-permute-start | bytes 1572872 | tf_op jit(solution)/shard_map/ppermute | solution.py:398
  19.5 57.4 %copy-start.15 = (bf16[2,2,32,128]{3,2,1,0:T(8,128)(2,1)}, bf16[2,2,32,128]{3,2,1,0:T(8,128)(2,1)S(1)}, u32[]{:S(2)}) copy-start(bf16[2,2,32,128]{3,2,1,0:T(8,128)(2,1)S(1)} %collective-permute-done.8.refs_7_.refs_10_) | copy-start | bytes 98308
  19.5 57.4 %copy-start.9 = (bf16[2,2048,128]{2,1,0:T(8,128)(2,1)}, bf16[2,2048,128]{2,1,0:T(8,128)(2,1)S(1)}, u32[]{:S(2)}) copy-start(bf16[2,2048,128]{2,1,0:T(8,128)(2,1)S(1)} %collective-permute-done.7.refs_5_.refs_8_) | copy-start | bytes 3145732
  75.7 1.0 copy-start.1
  76.8 38.3 %copy-start.13 = (bf16[2,512,128]{2,1,0:T(8,128)(2,1)}, bf16[2,512,128]{2,1,0:T(8,128)(2,1)S(1)}, u32[]{:S(2)}) copy-start(bf16[2,512,128]{2,1,0:T(8,128)(2,1)S(1)} %collective-permute-done.5.refs_5_) | copy-start | bytes 786436
  76.8 38.3 %copy-start.14 = (bf16[2,512,128]{2,1,0:T(8,128)(2,1)}, bf16[2,512,128]{2,1,0:T(8,128)(2,1)S(1)}, u32[]{:S(2)}) copy-start(bf16[2,512,128]{2,1,0:T(8,128)(2,1)S(1)} %collective-permute-done.4.refs_4_) | copy-start | bytes 786436
  76.8 38.3 %copy-start.10 = (bf16[2,2,512,128]{3,2,1,0:T(8,128)(2,1)}, bf16[2,2,512,128]{3,2,1,0:T(8,128)(2,1)S(1)}, u32[]{:S(2)}) copy-start(bf16[2,2,512,128]{3,2,1,0:T(8,128)(2,1)S(1)} %collective-permute-done.6.refs_6_) | copy-start | bytes 1572868
  115.1 62.2 %all-to-all-start.1 = ((bf16[64,72,128]{2,1,0:T(8,128)(2,1)}), bf16[64,72,128]{2,1,0:T(8,128)(2,1)S(1)}, u32[]{:S(2)}, u32[]{:S(2)}) async-start(bf16[64,72,128]{2,1,0:T(8,128)(2,1)} %bitcast.9), calls=%async_computation.1 | async-start | bytes 2359296 | tf_op jit(solution)/shard_map/all_to_all | solution.py:454
  177.4 27.3 %all-to-all-start = ((bf16[64,72,128]{2,1,0:T(8,128)(2,1)}), bf16[64,72,128]{2,1,0:T(8,128)(2,1)S(1)}, u32[]{:S(2)}, u32[]{:S(2)}) async-start(bf16[64,72,128]{2,1,0:T(8,128)(2,1)} %bitcast.14), calls=%async_computation | async-start | bytes 2359296 | tf_op jit(solution)/shard_map/all_to_all | solution.py:454

commit v7 on v6

--- a/solution.py
+++ b/solution.py
@@ -60,14 +60,14 @@
     )(cached_len, v_own, v_par)
 
 
-def attend_kernel(tiles, n_q, n_aliased, len_ref, span_ref, *refs):
+def attend_kernel(tiles, n_q, carried, len_ref, span_ref, *refs):
     inputs = refs[: n_q + 5]
     n_out = 1 + max(tile[0] for tile in tiles) - min(tile[0] for tile in tiles)
-    first_out = n_q + 5 + n_aliased
+    first_out = n_q + 5 + (1 if carried else 0)
     out_refs = refs[first_out : first_out + n_out]
     scratch = refs[first_out + n_out :]
     ko_ref, kp_ref, no_ref, np_ref, vt_ref = scratch[:5]
-    q_buf, acc_ref, top_ref, stage, sem, in_sem, q_sem = scratch[5:]
+    q_buf, acc_ref, top_ref, stage, sem, in_sem, q_sem, carry_sem = scratch[5:]
     requests = sorted({tile[0] for tile in tiles})
     lowest = requests[0]
     rows = ko_ref.shape[1]
@@ -101,6 +101,16 @@
         load_q(t)
     me, core, my_y, my_z, _ = my_place()
     partner = me + 1 - 2 * core
+
+    def carries():
+        for n, (hop_z, hop_y) in enumerate(carried):
+            place = (my_z ^ hop_z ^ (2 * core), my_y ^ hop_y ^ core)
+            yield pltpu.make_async_copy(
+                refs[n_q + 5].at[place], out_refs[0].at[place], carry_sem.at[n]
+            )
+
+    for copy in carries():
+        copy.start()
     n_new = 2 * no_ref.shape[2]
     block = q_buf.shape[2]
     width = 2 * block
@@ -273,10 +283,12 @@
         lax.fori_loop(0, len(tiles), again, 0)
 
     wait_for_sends()
+    for copy in carries():
+        copy.wait()
 
 
 def attend(
-    tiles, vmem, cached_len, span_order, q_arrays, k_own, k_par, n_own, n_par, vt, partials
+    tiles, vmem, cached_len, span_order, q_arrays, k_own, k_par, n_own, n_par, vt, partial, carried
 ):
     rows = k_own.shape[1]
     block = q_arrays[0].shape[-2]
@@ -288,10 +300,9 @@
     keys = (k_own, k_par, n_own, n_par, vt)
     n_in = len(q_arrays) + len(keys)
     return pl.pallas_call(
-        functools.partial(attend_kernel, tiles, len(q_arrays), len(partials)),
+        functools.partial(attend_kernel, tiles, len(q_arrays), carried),
         in_specs=[pl.BlockSpec(memory_space=pltpu.SMEM)] * 2
-        + [pl.BlockSpec(memory_space=pl.ANY)] * n_in
-        + [pl.BlockSpec(memory_space=pltpu.HBM)] * len(partials),
+        + [pl.BlockSpec(memory_space=pl.ANY)] * (n_in + len(partial)),
         out_specs=[pl.BlockSpec(memory_space=pltpu.HBM)] * len(requests),
         scratch_shapes=[pltpu.VMEM((len(requests),) + x.shape[1:], x.dtype) for x in keys]
         + [
@@ -302,16 +313,16 @@
             pltpu.SemaphoreType.DMA((2 * len(tiles),)),
             pltpu.SemaphoreType.DMA((len(requests) * 6,)),
             pltpu.SemaphoreType.DMA((2 * len(tiles),)),
+            pltpu.SemaphoreType.DMA((max(1, len(carried)),)),
         ],
         out_shape=[result] * len(requests),
-        input_output_aliases={2 + n_in + n: n for n in range(len(partials))},
         compiler_params=pltpu.CompilerParams(vmem_limit_bytes=vmem),
         cost_estimate=pl.CostEstimate(
             flops=len(tiles) * width * 2 * rows * 128 * 4,
             bytes_accessed=6 << 20,
             transcendentals=len(tiles) * width * 2 * rows,
         ),
-    )(cached_len, span_order, *q_arrays, *keys, *partials)
+    )(cached_len, span_order, *q_arrays, *keys, *partial)
 
 
 def combine_kernel(request, in_ref, *refs):
@@ -437,7 +448,7 @@
         ((1, by_own), (1, by_other), (1, last)),
     )
     plan = [tuple(tile(r, *pair) for r, pair in call) for call in plan]
-    partials = attend(plan[0], VMEM, *common, arrays[:4], *keys, [])
+    partials = attend(plan[0], VMEM, *common, arrays[:4], *keys, [], ())
     groups = [
         [
             (((y ^ core) * 4 + (z ^ (2 * core))) * 2 + core) * 8 + kv
@@ -449,7 +460,8 @@
     ]
     received = []
     for r in range(requests):
-        (parts,) = attend(plan[1 + r], VMEM if r == 0 else VMEM_ALL, *common, arrays, *keys, [partials[r]])
+        done = tuple(half[:2] for tile in plan[0] if tile[0] == r for half in tile[1:])
+        (parts,) = attend(plan[1 + r], VMEM if r == 0 else VMEM_ALL, *common, arrays, *keys, [partials[r]], done)
         sent = parts.reshape((64,) + parts.shape[3:])
         got = lax.all_to_all(
             sent, ("y", "z", "core", "kv"), 0, 0, axis_index_groups=groups, tiled=True

time: 208 us -> 209 us (level)
  transfers between devices with their start and end apart: 11 -> 11, of which waited for: 2 -> 2; matrix products, arithmetic and copies ran while one was open for 0% -> 0% of each run, Pallas kernels for 56% -> 57%
where the time goes in v7:
time: 209 us; the launch traced here: 207 us
  Pallas kernels  157 us (75%)
  starting transfers between devices  25.3 us (12%)
  waiting for transfers between devices  20.4 us (10%)
    pallas_call x3, Pallas kernels, attend(): pl.pallas_call(functools.partial(attend_kernel, tiles, len(q_arrays), car...  153 us
    all_to_all x2, waiting for transfers between devices, on_device(): lax.all_to_all(sent, ('y', 'z', 'core', 'kv'), 0, 0, axis_index_groups=gr...  19.5 us
    ppermute x9, starting transfers between devices, swapped(): return lax.ppermute(x, axis, [(n, n ^ flip) for n in range(size)])  13.7 us
    all_to_all x2, starting transfers between devices, on_device(): lax.all_to_all(sent, ('y', 'z', 'core', 'kv'), 0, 0, axis_index_groups=gr...  11.7 us
  transfers between devices with their start and end apart: 11, of which 2 were waited for; matrix products, arithmetic and copies ran while one was open for 0% of the time, Pallas kernels for 57%

profile of v7, /device:TPU:0, one launch (start us, length us, event | category | flops | bytes accessed | tf_op | source)
XLA Modules:
  0.0 206.9 jit_solution(705274385406800671)
XLA Ops:
  0.6 0.1 collective-permute-start.1
  0.7 0.5 collective-permute-start.7
  1.2 3.3 %collective-permute-start = (bf16[2,512,128]{2,1,0:T(8,128)(2,1)}, bf16[2,512,128]{2,1,0:T(8,128)(2,1)S(1)}, u32[]{:S(2)}, u32[]{:S(2)}) collective-permute-start(bf16[2,512,128]{2,1,0:T(8,128)(2,1)} %bitcast.16), channel_id=1, source_target_pairs={{0,64},{64,0},{1,65},{65,1},{2,66},{66,2},{3,67},{67,3},{4,68},{68... | collective-permute-start | bytes 786440 | tf_op jit(solution)/shard_map/ppermute | solution.py:409
  4.5 4.0 %collective-permute-start.3 = (bf16[2,512,128]{2,1,0:T(8,128)(2,1)}, bf16[2,512,128]{2,1,0:T(8,128)(2,1)S(1)}, u32[]{:S(2)}, u32[]{:S(2)}) collective-permute-start(bf16[2,512,128]{2,1,0:T(8,128)(2,1)} %bitcast.17), channel_id=1, source_target_pairs={{0,48},{16,32},{32,16},{48,0},{1,49},{17,33},{33,17},{49,1},{2,50}... | collective-permute-start | bytes 786440 | tf_op jit(solution)/shard_map/ppermute | solution.py:409
  8.5 0.0 collective-permute-start.2
  8.5 0.8 pad_maximum_fusion.1.refs_6_.refs_9_
  9.3 0.0 collective-permute-done.1.vp_ref
  9.3 0.1 collective-permute-start.8
  9.4 0.0 copy-start.1
  9.4 1.2 copy-done.1
  10.6 0.7 copy-done.5
  11.3 1.4 shard_map.86.refs_8_.refs_11_
  12.7 0.0 collective-permute-done.refs_1_
  12.7 0.0 copy-start.3
  12.7 2.6 %collective-permute-start.5 = (bf16[2,512,128]{2,1,0:T(8,128)(2,1)S(1)}, bf16[2,512,128]{2,1,0:T(8,128)(2,1)S(1)}, u32[]{:S(2)}, u32[]{:S(2)}) collective-permute-start(bf16[2,512,128]{2,1,0:T(8,128)(2,1)S(1)} %collective-permute-done.refs_1_), channel_id=1, source_target_pairs={{0,48},{16,32},{32,16},{48,0},{1,49},{17,33},{33,17},{49,1},{2,50}... | collective-permute-start | bytes 786440 | tf_op jit(solution)/shard_map/ppermute | solution.py:409
  15.4 0.1 pad_maximum_fusion
  15.4 0.0 collective-permute-done.3.refs_3_
  15.4 0.1 collective-permute-start.4
  15.5 1.0 collective-permute-done.2.refs_2_
  16.5 3.0 %collective-permute-start.6 = (bf16[2,2,512,128]{3,2,1,0:T(8,128)(2,1)S(1)}, bf16[2,2,512,128]{3,2,1,0:T(8,128)(2,1)S(1)}, u32[]{:S(2)}, u32[]{:S(2)}) collective-permute-start(bf16[2,2,512,128]{3,2,1,0:T(8,128)(2,1)S(1)} %pad_maximum_fusion), channel_id=1, source_target_pairs={{0,32},{16,48},{32,0},{48,16},{1,33},{17,49},{33,1},{49,17},{2,34}... | collective-permute-start | bytes 1572872 | tf_op jit(solution)/shard_map/ppermute | solution.py:409
  19.5 0.0 collective-permute-done.8.refs_7_.refs_10_
  19.5 0.0 collective-permute-done.7.refs_5_.refs_8_
  19.5 0.0 copy-done.6
  19.5 0.0 copy-done.15
  19.5 0.0 copy-done.7
  19.5 0.0 copy-start.8
  19.5 57.8 %shard_map.87 = (bf16[4,2,8,72,128]{4,3,2,1,0:T(8,128)(2,1)S(1)}, bf16[4,2,8,72,128]{4,3,2,1,0:T(8,128)(2,1)S(1)}) custom-call(s32[2]{0:T(128)S(1)} %copy-done.6, s32[2,32]{1,0:T(2,128)S(1)} %copy-done.15, bf16[2,512,128]{2,1,0:T(8,128)(2,1)S(1)} %bitcast.21, bf16[2,512,128]{2,1,0:T(8,128)(2,1)S(1)} %collective-permute-done.refs_1_, ...), custom_call_target="tpu_custom_call" | custom-call | flops 6442450944 | bytes 6291456 | tf_op jit(solution)/shard_map/pallas_call | solution.py:302
  77.3 0.0 copy-start.16
  77.3 0.0 collective-permute-done.5.refs_5_
  77.3 0.0 collective-permute-done.4.refs_4_
  77.3 0.0 collective-permute-done.6.refs_6_
  77.4 0.0 copy-start.9
  77.4 0.0 copy-done.4
  77.4 0.0 copy-done
  77.4 0.0 copy-done.3
  77.4 0.0 copy-done.10
  77.4 0.0 copy-done.11
  77.4 0.0 copy-done.14
  77.4 0.0 copy-done.8
  77.4 38.2 %shard_map.89 = bf16[4,2,8,72,128]{4,3,2,1,0:T(8,128)(2,1)} custom-call(s32[2]{0:T(128)S(1)} %copy-done.6, s32[2,32]{1,0:T(2,128)S(1)} %copy-done.15, bf16[2,512,128]{2,1,0:T(8,128)(2,1)S(1)} %bitcast.22, bf16[2,512,128]{2,1,0:T(8,128)(2,1)S(1)} %collective-permute-done.refs_1_, bf16[2,512,128]{2,1,0:T(8,128)(2,1)S(1)} %collective-permute-done.2.refs_2_, ...), custom_call_target="tpu_custom_call" | custom-call | flops 4294967296 | bytes 6291456 | tf_op jit(solution)/shard_map/pallas_call | solution.py:302
  115.7 0.0 copy-done.16
  115.7 5.4 %all-to-all-start.1 = ((bf16[64,72,128]{2,1,0:T(8,128)(2,1)}), bf16[64,72,128]{2,1,0:T(8,128)(2,1)S(1)}, u32[]{:S(2)}, u32[]{:S(2)}) async-start(bf16[64,72,128]{2,1,0:T(8,128)(2,1)} %bitcast.9), calls=%async_computation.1 | async-start | bytes 2359296 | tf_op jit(solution)/shard_map/all_to_all | solution.py:466
  121.2 56.8 %shard_map.88 = bf16[4,2,8,72,128]{4,3,2,1,0:T(8,128)(2,1)} custom-call(s32[2]{0:T(128)} %len_ref.7, s32[2,32]{1,0:T(2,128)} %span_ref.5, bf16[2,512,128]{2,1,0:T(8,128)(2,1)} %bitcast.19, bf16[2,512,128]{2,1,0:T(8,128)(2,1)} %copy-done.3, bf16[2,512,128]{2,1,0:T(8,128)(2,1)} %copy-done.11, bf16[2,512,128]{2,1,0:T(8,128)(2,1)} %copy-done.10, ...), custom_call_target="tpu_custom_call" | custom-call | flops 6442450944 | bytes 6291456 | tf_op jit(solution)/shard_map/pallas_call | solution.py:302
  178.0 0.0 all-to-all-done.1
  178.0 6.2 %all-to-all-start = ((bf16[64,72,128]{2,1,0:T(8,128)(2,1)}), bf16[64,72,128]{2,1,0:T(8,128)(2,1)S(1)}, u32[]{:S(2)}, u32[]{:S(2)}) async-start(bf16[64,72,128]{2,1,0:T(8,128)(2,1)} %bitcast.28), calls=%async_computation | async-start | bytes 2359296 | tf_op jit(solution)/shard_map/all_to_all | solution.py:466
  184.3 1.5 shard_map.90
  185.8 19.5 %all-to-all-done = bf16[64,72,128]{2,1,0:T(8,128)(2,1)S(1)} async-done(((bf16[64,72,128]{2,1,0:T(8,128)(2,1)}), bf16[64,72,128]{2,1,0:T(8,128)(2,1)S(1)}, u32[]{:S(2)}, u32[]{:S(2)}) %all-to-all-start) | async-done | bytes 1179680 | tf_op jit(solution)/shard_map/all_to_all | solution.py:466
  205.2 1.5 shard_map.91
  (16 shorter events, 0.0 us)
Async XLA Ops:
  0.6 8.7 %collective-permute-start.1 = (bf16[2,2048,128]{2,1,0:T(8,128)(2,1)}, bf16[2,2048,128]{2,1,0:T(8,128)(2,1)S(1)}, u32[]{:S(2)}, u32[]{:S(2)}) collective-permute-start(bf16[2,2048,128]{2,1,0:T(8,128)(2,1)} %bitcast.14), channel_id=1, source_target_pairs={{0,8},{8,0},{1,9},{9,1},{2,10},{10,2},{3,11},{11,3},{4,12},{12,4},... | collective-permute-start | bytes 3145736 | tf_op jit(solution)/shard_map/ppermute | solution.py:409
  0.7 18.7 %collective-permute-start.7 = (bf16[2,2048,128]{2,1,0:T(8,128)(2,1)}, bf16[2,2048,128]{2,1,0:T(8,128)(2,1)S(1)}, u32[]{:S(2)}, u32[]{:S(2)}) collective-permute-start(bf16[2,2048,128]{2,1,0:T(8,128)(2,1)} %bitcast.24), channel_id=1, source_target_pairs={{0,8},{8,0},{1,9},{9,1},{2,10},{10,2},{3,11},{11,3},{4,12},{12,4},... | collective-permute-start | bytes 3145736 | tf_op jit(solution)/shard_map/ppermute | solution.py:409
  1.2 11.5 %collective-permute-start = (bf16[2,512,128]{2,1,0:T(8,128)(2,1)}, bf16[2,512,128]{2,1,0:T(8,128)(2,1)S(1)}, u32[]{:S(2)}, u32[]{:S(2)}) collective-permute-start(bf16[2,512,128]{2,1,0:T(8,128)(2,1)} %bitcast.16), channel_id=1, source_target_pairs={{0,64},{64,0},{1,65},{65,1},{2,66},{66,2},{3,67},{67,3},{4,68},{68... | collective-permute-start | bytes 786440 | tf_op jit(solution)/shard_map/ppermute | solution.py:409
  4.5 10.9 %collective-permute-start.3 = (bf16[2,512,128]{2,1,0:T(8,128)(2,1)}, bf16[2,512,128]{2,1,0:T(8,128)(2,1)S(1)}, u32[]{:S(2)}, u32[]{:S(2)}) collective-permute-start(bf16[2,512,128]{2,1,0:T(8,128)(2,1)} %bitcast.17), channel_id=1, source_target_pairs={{0,48},{16,32},{32,16},{48,0},{1,49},{17,33},{33,17},{49,1},{2,50}... | collective-permute-start | bytes 786440 | tf_op jit(solution)/shard_map/ppermute | solution.py:409
  8.5 8.0 %collective-permute-start.2 = (bf16[2,512,128]{2,1,0:T(8,128)(2,1)}, bf16[2,512,128]{2,1,0:T(8,128)(2,1)S(1)}, u32[]{:S(2)}, u32[]{:S(2)}) collective-permute-start(bf16[2,512,128]{2,1,0:T(8,128)(2,1)} %bitcast.18), channel_id=1, source_target_pairs={{0,16},{16,0},{32,48},{48,32},{1,17},{17,1},{33,49},{49,33},{2,18}... | collective-permute-start | bytes 786440 | tf_op jit(solution)/shard_map/ppermute | solution.py:409
  8.5 10.9 %copy-start.6 = (s32[2]{0:T(128)S(1)}, s32[2]{0:T(128)}, u32[]{:S(2)}) copy-start(s32[2]{0:T(128)} %len_ref.7) | copy-start | bytes 28
  8.5 10.9 %copy-start.15 = (s32[2,32]{1,0:T(2,128)S(1)}, s32[2,32]{1,0:T(2,128)}, u32[]{:S(2)}) copy-start(s32[2,32]{1,0:T(2,128)} %span_ref.5) | copy-start | bytes 772
  9.3 68.1 %copy-start.4 = (bf16[2,2,32,128]{3,2,1,0:T(8,128)(2,1)}, bf16[2,2,32,128]{3,2,1,0:T(8,128)(2,1)S(1)}, u32[]{:S(2)}) copy-start(bf16[2,2,32,128]{3,2,1,0:T(8,128)(2,1)S(1)} %pad_maximum_fusion.1.refs_6_.refs_9_) | copy-start | bytes 98308
  9.3 10.1 %collective-permute-start.8 = (bf16[2,2,32,128]{3,2,1,0:T(8,128)(2,1)S(1)}, bf16[2,2,32,128]{3,2,1,0:T(8,128)(2,1)S(1)}, u32[]{:S(2)}, u32[]{:S(2)}) collective-permute-start(bf16[2,2,32,128]{3,2,1,0:T(8,128)(2,1)S(1)} %pad_maximum_fusion.1.refs_6_.refs_9_), channel_id=1, source_target_pairs={{0,8},{8,0},{1,9},{9,1},{2,10},{10,2},{3,11},{11,3},{4,12},{12,4},... | collective-permute-start | bytes 98312 | tf_op jit(solution)/shard_map/ppermute | solution.py:409
  9.4 1.2 copy-start.1
  10.6 0.7 copy-start.5
  11.3 4.1 %copy-start.2 = (bf16[2,32,16,128]{3,2,1,0:T(8,128)(2,1)S(1)}, bf16[2,32,16,128]{3,2,1,0:T(8,128)(2,1)}, u32[]{:S(2)}) copy-start(bf16[2,32,16,128]{3,2,1,0:T(8,128)(2,1)} %param.7) | copy-start | bytes 786436
  11.3 8.2 %copy-start.7 = (bf16[2,2048,1,128]{3,1,2,0:T(8,128)(2,1)S(1)}, bf16[2,2048,1,128]{3,1,2,0:T(8,128)(2,1)}, u32[]{:S(2)}) copy-start(bf16[2,2048,1,128]{3,1,2,0:T(8,128)(2,1)} %param.10) | copy-start | bytes 3145732
  12.7 64.7 %copy-start = (bf16[2,144,4096]{2,1,0:T(8,128)(2,1)}, bf16[2,144,4096]{2,1,0:T(8,128)(2,1)S(1)}, u32[]{:S(2)}) copy-start(bf16[2,144,4096]{2,1,0:T(8,128)(2,1)S(1)} %shard_map.86.refs_8_.refs_11_) | copy-start | bytes 7077892
  12.7 64.7 %copy-start.3 = (bf16[2,512,128]{2,1,0:T(8,128)(2,1)}, bf16[2,512,128]{2,1,0:T(8,128)(2,1)S(1)}, u32[]{:S(2)}) copy-start(bf16[2,512,128]{2,1,0:T(8,128)(2,1)S(1)} %collective-permute-done.refs_1_) | copy-start | bytes 786436
  12.7 64.6 %collective-permute-start.5 = (bf16[2,512,128]{2,1,0:T(8,128)(2,1)S(1)}, bf16[2,512,128]{2,1,0:T(8,128)(2,1)S(1)}, u32[]{:S(2)}, u32[]{:S(2)}) collective-permute-start(bf16[2,512,128]{2,1,0:T(8,128)(2,1)S(1)} %collective-permute-done.refs_1_), channel_id=1, source_target_pairs={{0,48},{16,32},{32,16},{48,0},{1,49},{17,33},{33,17},{49,1},{2,50}... | collective-permute-start | bytes 786440 | tf_op jit(solution)/shard_map/ppermute | solution.py:409
  15.4 62.0 %copy-start.10 = (bf16[2,512,128]{2,1,0:T(8,128)(2,1)}, bf16[2,512,128]{2,1,0:T(8,128)(2,1)S(1)}, u32[]{:S(2)}) copy-start(bf16[2,512,128]{2,1,0:T(8,128)(2,1)S(1)} %collective-permute-done.3.refs_3_) | copy-start | bytes 786436
  15.4 61.9 %collective-permute-start.4 = (bf16[2,512,128]{2,1,0:T(8,128)(2,1)S(1)}, bf16[2,512,128]{2,1,0:T(8,128)(2,1)S(1)}, u32[]{:S(2)}, u32[]{:S(2)}) collective-permute-start(bf16[2,512,128]{2,1,0:T(8,128)(2,1)S(1)} %collective-permute-done.refs_1_), channel_id=1, source_target_pairs={{0,16},{16,0},{32,48},{48,32},{1,17},{17,1},{33,49},{49,33},{2,18}... | collective-permute-start | bytes 786440 | tf_op jit(solution)/shard_map/ppermute | solution.py:409
  16.5 60.9 %copy-start.11 = (bf16[2,512,128]{2,1,0:T(8,128)(2,1)}, bf16[2,512,128]{2,1,0:T(8,128)(2,1)S(1)}, u32[]{:S(2)}) copy-start(bf16[2,512,128]{2,1,0:T(8,128)(2,1)S(1)} %collective-permute-done.2.refs_2_) | copy-start | bytes 786436
  16.5 60.9 %collective-permute-start.6 = (bf16[2,2,512,128]{3,2,1,0:T(8,128)(2,1)S(1)}, bf16[2,2,512,128]{3,2,1,0:T(8,128)(2,1)S(1)}, u32[]{:S(2)}, u32[]{:S(2)}) collective-permute-start(bf16[2,2,512,128]{3,2,1,0:T(8,128)(2,1)S(1)} %pad_maximum_fusion), channel_id=1, source_target_pairs={{0,32},{16,48},{32,0},{48,16},{1,33},{17,49},{33,1},{49,17},{2,34}... | collective-permute-start | bytes 1572872 | tf_op jit(solution)/shard_map/ppermute | solution.py:409
  19.5 58.0 %copy-start.14 = (bf16[2,2,32,128]{3,2,1,0:T(8,128)(2,1)}, bf16[2,2,32,128]{3,2,1,0:T(8,128)(2,1)S(1)}, u32[]{:S(2)}) copy-start(bf16[2,2,32,128]{3,2,1,0:T(8,128)(2,1)S(1)} %collective-permute-done.8.refs_7_.refs_10_) | copy-start | bytes 98308
  19.5 57.9 %copy-start.8 = (bf16[2,2048,128]{2,1,0:T(8,128)(2,1)}, bf16[2,2048,128]{2,1,0:T(8,128)(2,1)S(1)}, u32[]{:S(2)}) copy-start(bf16[2,2048,128]{2,1,0:T(8,128)(2,1)S(1)} %collective-permute-done.7.refs_5_.refs_8_) | copy-start | bytes 3145732
  77.3 38.4 %copy-start.16 = (bf16[4,2,8,72,128]{4,3,2,1,0:T(8,128)(2,1)}, bf16[4,2,8,72,128]{4,3,2,1,0:T(8,128)(2,1)S(1)}, u32[]{:S(2)}) copy-start(bf16[4,2,8,72,128]{4,3,2,1,0:T(8,128)(2,1)S(1)} %get-tuple-element.18.refs_12_) | copy-start | bytes 3538948
  77.3 38.4 %copy-start.12 = (bf16[2,512,128]{2,1,0:T(8,128)(2,1)}, bf16[2,512,128]{2,1,0:T(8,128)(2,1)S(1)}, u32[]{:S(2)}) copy-start(bf16[2,512,128]{2,1,0:T(8,128)(2,1)S(1)} %collective-permute-done.5.refs_5_) | copy-start | bytes 786436
  77.3 38.4 %copy-start.13 = (bf16[2,512,128]{2,1,0:T(8,128)(2,1)}, bf16[2,512,128]{2,1,0:T(8,128)(2,1)S(1)}, u32[]{:S(2)}) copy-start(bf16[2,512,128]{2,1,0:T(8,128)(2,1)S(1)} %collective-permute-done.4.refs_4_) | copy-start | bytes 786436
  77.4 38.4 %copy-start.9 = (bf16[2,2,512,128]{3,2,1,0:T(8,128)(2,1)}, bf16[2,2,512,128]{3,2,1,0:T(8,128)(2,1)S(1)}, u32[]{:S(2)}) copy-start(bf16[2,2,512,128]{3,2,1,0:T(8,128)(2,1)S(1)} %collective-permute-done.6.refs_6_) | copy-start | bytes 1572868
  115.7 62.3 %all-to-all-start.1 = ((bf16[64,72,128]{2,1,0:T(8,128)(2,1)}), bf16[64,72,128]{2,1,0:T(8,128)(2,1)S(1)}, u32[]{:S(2)}, u32[]{:S(2)}) async-start(bf16[64,72,128]{2,1,0:T(8,128)(2,1)} %bitcast.9), calls=%async_computation.1 | async-start | bytes 2359296 | tf_op jit(solution)/shard_map/all_to_all | solution.py:466
  178.0 27.2 %all-to-all-start = ((bf16[64,72,128]{2,1,0:T(8,128)(2,1)}), bf16[64,72,128]{2,1,0:T(8,128)(2,1)S(1)}, u32[]{:S(2)}, u32[]{:S(2)}) async-start(bf16[64,72,128]{2,1,0:T(8,128)(2,1)} %bitcast.28), calls=%async_computation | async-start | bytes 2359296 | tf_op jit(solution)/shard_map/all_to_all | solution.py:466
